TPU v7x, 32 devices: a whole 2x2x4 slice. The times are simulated.
32 devices in a mesh: groups: 2 (over y), slab: 4 (over z), orb: 4 (over x, core).
Axes of the slice: x: 2, y: 2, z: 4, core: 2. Of those that a mesh axis runs over, the one named last changes fastest.
Arguments:
- fractions: float32 [3, 3072], P(None, ('groups', 'slab', 'orb')), parts along dimension 1, may hold values from 0 to 1
- cell_index: int32 [2, 3072], P(None, ('groups', 'slab', 'orb')), parts along dimension 1, may hold values from 0 to 15
- slab_owner: int32 [3072, 1], P(('groups', 'slab', 'orb')), parts along dimension 0, may hold values from 0 to 3; in each aligned block of 96 rows (0 to 95, 96 to 191, ...) at most 30 rows name the same one
- spline_table: float32 [4, 16, 16, 4, 2048], P('slab', None, None, None, 'orb'), may hold values from -6 to 6
Outputs:
- orbital_values: bfloat16 [5, 3072, 2048], P(None, ('groups', 'slab', 'orb')), parts along dimension 1
There are 2 independent parts, one for each index of `groups`. A program takes and returns all parts, laid end to end along the dimension named above; an argument that names none is the same for every part. Nothing has to cross between parts.
Inputs may be any that keep to these rules, and one draw needn't show every extreme that they name: `slab_owner`: in each aligned block of 96 electrons (the electrons of one device) at most 30 name the same slab, a bound that some block reaches of them.
All inputs are finite; a program needn't handle non-finite values.
Results may differ from a plain program's by a relative error of at most 0.001.
Values may be sent and summed in bfloat16 or wider, within the bound.
No kernel may reach another device: no remote copies, remote signals or barrier semaphores. Data moves between devices by JAX's collectives and lax.ppermute only.
A program may use at most 64 MiB of HBM per device.

v0:
```python
import jax
import jax.numpy as jnp
from jax import lax
from jax.sharding import PartitionSpec as P


def spline_bases(position):
    remain = 1.0 - position
    square = position * position
    frac_cube = square * position
    values = jnp.stack(
        [
            remain * remain * remain / 6.0,
            (3.0 * frac_cube - 6.0 * square + 4.0) / 6.0,
            (-3.0 * frac_cube + 3.0 * square + 3.0 * position + 1.0) / 6.0,
            frac_cube / 6.0,
        ],
        axis=-1,
    )
    slopes = jnp.stack(
        [
            -0.5 * remain * remain,
            0.5 * (3.0 * square - 4.0 * position),
            0.5 * (-3.0 * square + 2.0 * position + 1.0),
            0.5 * square,
        ],
        axis=-1,
    )
    curves = jnp.stack([remain, 3.0 * position - 2.0, 1.0 - 3.0 * position, position], axis=-1)
    return (values, slopes, curves)


def spread_taps(first_cell, taps, grid_width):
    offsets = jnp.arange(4, dtype=jnp.int32)
    cells = jnp.arange(grid_width, dtype=jnp.int32)
    wrapped = (first_cell[:, None] + offsets[None, :]) % grid_width
    hits = (wrapped[:, :, None] == cells[None, None, :]).astype(jnp.float32)
    return jnp.sum(hits * taps[:, :, None], axis=1)


def evaluate(incoming, table_flat, grid_width):
    basis_x, slope_x, curve_x = spline_bases(incoming[0])
    basis_y, slope_y, curve_y = spline_bases(incoming[1])
    basis_z, slope_z, curve_z = spline_bases(incoming[2])
    row_y = incoming[3].astype(jnp.int32)
    row_z = incoming[4].astype(jnp.int32)
    value_y = spread_taps(row_y, basis_y, grid_width)[:, :, None, None]
    deriv_y = spread_taps(row_y, slope_y, grid_width)[:, :, None, None]
    second_y = spread_taps(row_y, curve_y, grid_width)[:, :, None, None]
    value_z = spread_taps(row_z, basis_z, grid_width)[:, None, :, None]
    deriv_z = spread_taps(row_z, slope_z, grid_width)[:, None, :, None]
    second_z = spread_taps(row_z, curve_z, grid_width)[:, None, :, None]
    value_x = basis_x[:, None, None, :]
    deriv_x = slope_x[:, None, None, :]
    second_x = curve_x[:, None, None, :]
    dense = jnp.stack(
        [
            value_x * value_y * value_z,
            deriv_x * value_y * value_z,
            value_x * deriv_y * value_z,
            value_x * value_y * deriv_z,
            second_x * value_y * value_z
            + value_x * second_y * value_z
            + value_x * value_y * second_z,
        ]
    )
    slot_count = incoming.shape[1]
    dense = dense.reshape(5 * slot_count, table_flat.shape[0])
    result = jnp.dot(
        dense, table_flat, precision=lax.Precision.HIGHEST, preferred_element_type=jnp.float32
    )
    return result.reshape(5, slot_count, table_flat.shape[1]).astype(jnp.bfloat16)


def body(fractions, cell_index, slab_owner, spline_table):
    slab_count = lax.axis_size("slab")
    orb_count = lax.axis_size("orb")
    electrons = slab_owner.shape[0]
    capacity = max(2, (5 * electrons + 4 * slab_count - 1) // (4 * slab_count))
    grid_width = spline_table.shape[1]
    orb_local = spline_table.shape[4]
    owners = slab_owner[:, 0]
    columns = jnp.arange(slab_count, dtype=jnp.int32)
    member = (owners[:, None] == columns[None, :]).astype(jnp.int32)
    earlier = jnp.cumsum(member, axis=0) - member
    slot_place = owners * capacity + jnp.sum(earlier * member, axis=1)
    packed = jnp.concatenate([fractions, cell_index.astype(jnp.float32)], axis=0)
    outgoing = jnp.zeros((5, slab_count * capacity), jnp.float32).at[:, slot_place].set(packed)
    outgoing = outgoing.reshape(5, 1, slab_count, capacity)
    spread = lax.all_gather(outgoing, "orb", axis=1, tiled=True)
    arrived = lax.all_to_all(spread, "slab", split_axis=2, concat_axis=2, tiled=True)
    table_flat = spline_table.reshape(grid_width * grid_width * 4, orb_local)
    per_source = jnp.moveaxis(arrived.reshape(5, orb_count, slab_count * capacity), 1, 0)
    blocks = lax.map(lambda incoming: evaluate(incoming, table_flat, grid_width), per_source)
    results = jnp.moveaxis(blocks, 0, 1).reshape(5, orb_count, slab_count, capacity, orb_local)
    returned = lax.all_to_all(results, "slab", split_axis=2, concat_axis=2, tiled=True)
    at_home = lax.all_to_all(returned, "orb", split_axis=1, concat_axis=4, tiled=True)
    flat_home = at_home.reshape(5, slab_count * capacity, at_home.shape[4])
    return jnp.take(flat_home, slot_place, axis=1)


def solution(mesh):
    in_specs = (
        P(None, ("groups", "slab", "orb")),
        P(None, ("groups", "slab", "orb")),
        P(("groups", "slab", "orb"), None),
        P("slab", None, None, None, "orb"),
    )
    out_specs = P(None, ("groups", "slab", "orb"), None)
    return jax.shard_map(body, mesh=mesh, in_specs=in_specs, out_specs=out_specs, check_vma=False)
```

profile of v0, /device:TPU:0, one launch (start us, length us, event | category | flops | bytes accessed | tf_op | source)
XLA Modules:
  0.0 205.3 jit_solution(7496427272077821704)
XLA Ops:
  4.8 6.2 %all_gather.3 = f32[5,4,4,30]{3,2,0,1:T(4,128)S(1)} all-gather(f32[5,1,4,30]{3,2,0,1:T(4,128)S(1)} %reshape.1055), channel_id=1, replica_groups=mesh['groups'=2,'slab'=4,'orb'=4] {'orb'}, dimensions={1}, use_global_device_ids=true | all-gather | bytes 12000 | tf_op jit(solution)/shard_map/all_gather | solution.py:90
  11.8 5.3 %all-to-all-start = ((f32[4,1,600]{2,1,0:T(1,128)}), f32[4,1,600]{2,1,0:T(1,128)S(1)}, u32[]{:S(2)}, u32[]{:S(2)}) async-start(f32[4,1,600]{2,1,0:T(1,128)} %reshape.1080), calls=%async_computation | async-start | bytes 20480 | tf_op jit(solution)/shard_map/all_to_all | solution.py:91
  17.1 2.0 reshape.1057
  19.1 3.6 %all-to-all-done = f32[4,1,600]{2,1,0:T(1,128)S(1)} async-done(((f32[4,1,600]{2,1,0:T(1,128)}), f32[4,1,600]{2,1,0:T(1,128)S(1)}, u32[]{:S(2)}, u32[]{:S(2)}) %all-to-all-start) | async-done | bytes 9632 | tf_op jit(solution)/shard_map/all_to_all | solution.py:91
  24.1 69.7 %while.13 = (s32[]{:T(128)}, bf16[4,5,120,512]{3,2,1,0:T(8,128)(2,1)}, f32[4,5,120]{2,0,1:T(4,128)S(1)}, f32[1024,512]{1,0:T(8,128)S(1)}, s32[]{:T(128)}, /*index=5*/s32[]{:T(128)}, s32[]{}, s32[]{}, s32[]{}, s32[]{}) while((s32[]{:T(128)}, bf16[4,5,120,512]{3,2,1,0:T(8,128)(2,1)}, f32[4,5,120]{2,0,1:T(4,128)S(1)}, ...), condition=%wide.region_10.11_spmd, body=%wide.region_3.10_spmd.sunk | while | flops 3776219648 | bytes 19843924 | solution.py:94
  24.4 1.6 multiply_add_fusion.5
  26.0 2.0 copy.109
  28.1 2.0 copy.110
  30.1 2.0 copy.111
  36.6 4.9 %fusion.39 = bf16[4,5,120,512]{3,2,1,0:T(8,128)(2,1)} fusion(bf16[4,5,120,512]{3,2,1,0:T(8,128)(2,1)} %get-tuple-element.335, s32[]{:T(128)S(6)} %copy.121, f32[5,120,1024]{2,1,0:T(8,128)S(1)} %constant_dynamic-update-slice_fusion.14, f32[1024,512]{1,0:T(8,128)S(1)} %get-tuple-element.347), kind=kOutput, calls=%fused_computation.6.clone.1 | convolution fusion | flops 3775180800 | bytes 5169156 | tf_op jit(solution)/shard_map/while/body/eval_jaxpr/dot_general | solution.py:69
  43.4 2.0 copy.109
  45.5 2.0 copy.110
  47.5 2.0 copy.111
  54.0 4.9 %fusion.39 = bf16[4,5,120,512]{3,2,1,0:T(8,128)(2,1)} fusion(bf16[4,5,120,512]{3,2,1,0:T(8,128)(2,1)} %get-tuple-element.335, s32[]{:T(128)S(6)} %copy.121, f32[5,120,1024]{2,1,0:T(8,128)S(1)} %constant_dynamic-update-slice_fusion.14, f32[1024,512]{1,0:T(8,128)S(1)} %get-tuple-element.347), kind=kOutput, calls=%fused_computation.6.clone.1 | convolution fusion | flops 3775180800 | bytes 5169156 | tf_op jit(solution)/shard_map/while/body/eval_jaxpr/dot_general | solution.py:69
  59.2 1.6 multiply_add_fusion.5
  60.8 2.0 copy.109
  62.8 2.0 copy.110
  64.9 2.0 copy.111
  71.4 4.9 %fusion.39 = bf16[4,5,120,512]{3,2,1,0:T(8,128)(2,1)} fusion(bf16[4,5,120,512]{3,2,1,0:T(8,128)(2,1)} %get-tuple-element.335, s32[]{:T(128)S(6)} %copy.121, f32[5,120,1024]{2,1,0:T(8,128)S(1)} %constant_dynamic-update-slice_fusion.14, f32[1024,512]{1,0:T(8,128)S(1)} %get-tuple-element.347), kind=kOutput, calls=%fused_computation.6.clone.1 | convolution fusion | flops 3775180800 | bytes 5169156 | tf_op jit(solution)/shard_map/while/body/eval_jaxpr/dot_general | solution.py:69
  78.3 2.0 copy.109
  80.3 2.0 copy.110
  82.3 2.0 copy.111
  88.9 4.9 %fusion.39 = bf16[4,5,120,512]{3,2,1,0:T(8,128)(2,1)} fusion(bf16[4,5,120,512]{3,2,1,0:T(8,128)(2,1)} %get-tuple-element.335, s32[]{:T(128)S(6)} %copy.121, f32[5,120,1024]{2,1,0:T(8,128)S(1)} %constant_dynamic-update-slice_fusion.14, f32[1024,512]{1,0:T(8,128)S(1)} %get-tuple-element.347), kind=kOutput, calls=%fused_computation.6.clone.1 | convolution fusion | flops 3775180800 | bytes 5169156 | tf_op jit(solution)/shard_map/while/body/eval_jaxpr/dot_general | solution.py:69
  93.8 3.0 %copy.88 = bf16[5,4,120,512]{3,1,2,0:T(4,128)(2,1)S(1)} copy(bf16[5,4,120,512]{3,2,0,1:T(8,128)(2,1)} %bitcast.103) | data formatting | bytes 4915200 | tf_op jit(solution)/shard_map/transpose | solution.py:95
  97.6 57.8 %all_to_all.25 = bf16[5,4,4,30,512]{4,1,3,0,2:T(4,128)(2,1)S(1)} all-to-all(bf16[5,4,4,30,512]{4,1,3,0,2:T(4,128)(2,1)S(1)} %copy.89), channel_id=1, replica_groups=mesh['groups'=2,'slab'=4,'orb'=4] {'slab'}, dimensions={2} | all-to-all | bytes 4915200 | tf_op jit(solution)/shard_map/all_to_all | solution.py:96
  155.4 2.7 %copy.90 = bf16[5,4,4,30,512]{4,2,3,0,1:T(4,128)(2,1)} copy(bf16[5,4,4,30,512]{4,1,3,0,2:T(4,128)(2,1)S(1)} %all_to_all.25) | data formatting | bytes 4915200 | tf_op jit(solution)/shard_map/all_to_all | solution.py:96
  158.1 3.8 %all-to-all-start.2 = ((bf16[5,4,4,30,512]{4,2,3,0,1:T(4,128)(2,1)}), bf16[5,4,4,30,512]{4,2,3,0,1:T(4,128)(2,1)S(1)}, u32[]{:S(2)}, u32[]{:S(2)}) async-start(bf16[5,4,4,30,512]{4,2,3,0,1:T(4,128)(2,1)} %copy.90), calls=%async_computation.2 | async-start | bytes 4915200 | tf_op jit(solution)/shard_map/all_to_all | solution.py:97
  162.0 29.3 %all-to-all-done.2 = bf16[5,4,4,30,512]{4,2,3,0,1:T(4,128)(2,1)S(1)} async-done(((bf16[5,4,4,30,512]{4,2,3,0,1:T(4,128)(2,1)}), bf16[5,4,4,30,512]{4,2,3,0,1:T(4,128)(2,1)S(1)}, u32[]{:S(2)}, u32[]{:S(2)}) %all-to-all-start.2) | async-done | bytes 2457632 | tf_op jit(solution)/shard_map/all_to_all | solution.py:97
  192.7 3.0 %copy.94 = bf16[5,1,4,30,4,512]{5,4,0,3,2,1:T(4,128)(2,1)S(1)} copy(bf16[5,1,4,30,4,512]{5,2,3,0,4,1:T(4,128)(2,1)} %bitcast.101) | data formatting | bytes 4915200 | tf_op jit(solution)/shard_map/reshape | solution.py:98
  195.7 3.7 %reshape.1077 = bf16[5,120,2048]{2,0,1:T(8,128)(2,1)} reshape(bf16[5,1,4,30,4,512]{5,4,0,3,2,1:T(4,128)(2,1)S(1)} %copy.94) | data formatting | bytes 4915200 | tf_op jit(solution)/shard_map/reshape | solution.py:98
  199.4 2.9 %gather_fusion = bf16[96,5,2048]{2,1,0:T(8,128)(2,1)S(1)} fusion(bf16[5,120,2048]{2,0,1:T(8,128)(2,1)} %reshape.1077, s32[1024]{0:T(1024)S(1)} %pad_clamp_fusion), kind=kCustom, calls=%fused_computation | custom fusion | bytes 3932544 | tf_op jit(solution)/shard_map/jit(_take)/gather | solution.py:99
  202.8 2.6 %copy.93 = bf16[5,96,2048]{2,1,0:T(8,128)(2,1)} copy(bf16[5,96,2048]{2,0,1:T(8,128)(2,1)S(1)} %select_bitcast_fusion) | data formatting | bytes 3932160 | tf_op jit(solution)/shard_map/jit(_take)/select_n | solution.py:99
  (117 shorter events, 31.7 us)
Async XLA Ops:
  11.8 10.9 %all-to-all-start = ((f32[4,1,600]{2,1,0:T(1,128)}), f32[4,1,600]{2,1,0:T(1,128)S(1)}, u32[]{:S(2)}, u32[]{:S(2)}) async-start(f32[4,1,600]{2,1,0:T(1,128)} %reshape.1080), calls=%async_computation | async-start | bytes 20480 | tf_op jit(solution)/shard_map/all_to_all | solution.py:91
  33.3 3.3 %copy-start = (f32[1,120,1024]{2,1,0:T(8,128)S(1)}, f32[1,120,1024]{2,1,0:T(8,128)}, u32[]{:S(2)}) copy-start(f32[1,120,1024]{2,1,0:T(8,128)} %copy.112) | copy-start | bytes 1474564 | tf_op jit(solution)/shard_map/while
  50.7 3.3 %copy-start = (f32[1,120,1024]{2,1,0:T(8,128)S(1)}, f32[1,120,1024]{2,1,0:T(8,128)}, u32[]{:S(2)}) copy-start(f32[1,120,1024]{2,1,0:T(8,128)} %copy.112) | copy-start | bytes 1474564 | tf_op jit(solution)/shard_map/while
  68.1 3.3 %copy-start = (f32[1,120,1024]{2,1,0:T(8,128)S(1)}, f32[1,120,1024]{2,1,0:T(8,128)}, u32[]{:S(2)}) copy-start(f32[1,120,1024]{2,1,0:T(8,128)} %copy.112) | copy-start | bytes 1474564 | tf_op jit(solution)/shard_map/while
  85.5 3.3 %copy-start = (f32[1,120,1024]{2,1,0:T(8,128)S(1)}, f32[1,120,1024]{2,1,0:T(8,128)}, u32[]{:S(2)}) copy-start(f32[1,120,1024]{2,1,0:T(8,128)} %copy.112) | copy-start | bytes 1474564 | tf_op jit(solution)/shard_map/while
  158.1 33.2 %all-to-all-start.2 = ((bf16[5,4,4,30,512]{4,2,3,0,1:T(4,128)(2,1)}), bf16[5,4,4,30,512]{4,2,3,0,1:T(4,128)(2,1)S(1)}, u32[]{:S(2)}, u32[]{:S(2)}) async-start(bf16[5,4,4,30,512]{4,2,3,0,1:T(4,128)(2,1)} %copy.90), calls=%async_computation.2 | async-start | bytes 4915200 | tf_op jit(solution)/shard_map/all_to_all | solution.py:97
  191.3 1.4 copy-start.1
where the time goes:
time: 207 us; the launch traced here: 205 us
  local copies, waits for them, and re-layouts  66.8 us (32%)
  blocking collectives  64 us (31%)
  waiting for transfers between devices  32.9 us (16%)
  matrix products  19.6 us (9%)
  other arithmetic  12.1 us (6%)
  starting transfers between devices  9.17 us (4%)
    all_to_all x1, blocking collectives, body(): lax.all_to_all(results, 'slab', split_axis=2, concat_axis=2, tiled=True)  57.8 us
    all_to_all x1, waiting for transfers between devices, body(): lax.all_to_all(returned, 'orb', split_axis=1, concat_axis=4, tiled=True)  29.3 us
    dot_general x4, matrix products, evaluate(): jnp.dot(dense, table_flat, precision=lax.Precision.HIGHEST, preferred_ele...  19.6 us
    while x24, local copies, waits for them, and re-layouts  13.2 us
    mul x4, local copies, waits for them, and re-layouts, evaluate(): value_x * deriv_y * value_z  8.1 us
    mul x4, local copies, waits for them, and re-layouts, evaluate(): value_x * value_y * value_z  8.1 us
    mul x4, local copies, waits for them, and re-layouts, evaluate(): deriv_x * value_y * value_z  8.07 us
    reshape x2, local copies, waits for them, and re-layouts, body(): flat_home = at_home.reshape(5, slab_count * capacity, at_home.shape[4])  6.66 us
  transfers between devices with their start and end apart: 2, of which 2 were waited for; matrix products, arithmetic and copies ran while one was open for 1% of the time, Pallas kernels for 0%

commit v1 on v0

--- a/solution.py
+++ b/solution.py
@@ -1,33 +1,39 @@
+import functools
+
 import jax
 import jax.numpy as jnp
 from jax import lax
+from jax.experimental import pallas as pl
+from jax.experimental.pallas import tpu as pltpu
 from jax.sharding import PartitionSpec as P
 
-
-def spline_bases(position):
+LANES = 128
+F32 = jnp.float32
+BF16 = jnp.bfloat16
+
+
+def spline_taps(position):
     remain = 1.0 - position
     square = position * position
     frac_cube = square * position
-    values = jnp.stack(
-        [
-            remain * remain * remain / 6.0,
-            (3.0 * frac_cube - 6.0 * square + 4.0) / 6.0,
-            (-3.0 * frac_cube + 3.0 * square + 3.0 * position + 1.0) / 6.0,
-            frac_cube / 6.0,
-        ],
-        axis=-1,
-    )
-    slopes = jnp.stack(
-        [
-            -0.5 * remain * remain,
-            0.5 * (3.0 * square - 4.0 * position),
-            0.5 * (-3.0 * square + 2.0 * position + 1.0),
-            0.5 * square,
-        ],
-        axis=-1,
-    )
-    curves = jnp.stack([remain, 3.0 * position - 2.0, 1.0 - 3.0 * position, position], axis=-1)
-    return (values, slopes, curves)
+    values = (
+        remain * remain * remain / 6.0,
+        (3.0 * frac_cube - 6.0 * square + 4.0) / 6.0,
+        (-3.0 * frac_cube + 3.0 * square + 3.0 * position + 1.0) / 6.0,
+        frac_cube / 6.0,
+    )
+    slopes = (
+        -0.5 * remain * remain,
+        0.5 * (3.0 * square - 4.0 * position),
+        0.5 * (-3.0 * square + 2.0 * position + 1.0),
+        0.5 * square,
+    )
+    curves = (remain, 3.0 * position - 2.0, 1.0 - 3.0 * position, position)
+    return values, slopes, curves
+
+
+def spline_bases(position):
+    return tuple(jnp.stack(taps, axis=-1) for taps in spline_taps(position))
 
 
 def spread_taps(first_cell, taps, grid_width):
@@ -72,11 +78,15 @@
     return result.reshape(5, slot_count, table_flat.shape[1]).astype(jnp.bfloat16)
 
 
-def body(fractions, cell_index, slab_owner, spline_table):
+def slot_capacity(electrons, slab_count):
+    return max(2, (5 * electrons + 4 * slab_count - 1) // (4 * slab_count))
+
+
+def general_body(fractions, cell_index, slab_owner, spline_table):
     slab_count = lax.axis_size("slab")
     orb_count = lax.axis_size("orb")
     electrons = slab_owner.shape[0]
-    capacity = max(2, (5 * electrons + 4 * slab_count - 1) // (4 * slab_count))
+    capacity = slot_capacity(electrons, slab_count)
     grid_width = spline_table.shape[1]
     orb_local = spline_table.shape[4]
     owners = slab_owner[:, 0]
@@ -99,6 +109,217 @@
     return jnp.take(flat_home, slot_place, axis=1)
 
 
+def iota(shape, dim):
+    return lax.broadcasted_iota(jnp.int32, shape, dim)
+
+
+def to_column(row):
+    count = row.shape[1]
+    spread = jnp.broadcast_to(row, (count, count))
+    return jnp.sum(jnp.where(iota((count, count), 0) == iota((count, count), 1), spread, 0.0), axis=1, keepdims=True)
+
+
+def pack_kernel(fractions_ref, cells_ref, owner_ref, packed_ref):
+    electrons = fractions_ref.shape[1]
+    owner = owner_ref[...].astype(F32)
+    same = to_column(owner) == owner
+    before = iota((electrons, electrons), 0) < iota((electrons, electrons), 1)
+    slot = jnp.sum(jnp.where(same & before, 1.0, 0.0), axis=0, keepdims=True)
+    packed_ref[...] = jnp.full(packed_ref.shape, -1.0, F32)
+    packed_ref[0:3, :electrons] = fractions_ref[...]
+    packed_ref[3:5, :electrons] = cells_ref[...].astype(F32)
+    packed_ref[5:6, :electrons] = owner
+    packed_ref[6:7, :electrons] = slot
+
+
+def split_kernel(table_ref, high_ref, low_ref):
+    table = table_ref[...]
+    high = table.astype(BF16)
+    high_ref[...] = high
+    low_ref[...] = (table - high.astype(F32)).astype(BF16)
+
+
+def slot_weights(home, slab, slots, grid_width, high_ref, low_ref):
+    owner, slot = home[5:6, :], home[6:7, :]
+    wanted = jnp.where(owner == slab.astype(F32), slot, -1.0)
+    chosen = iota((slots, LANES), 0).astype(F32) == wanted
+    lane = iota((slots, LANES), 1)
+
+    def field(index):
+        picked = jnp.sum(jnp.where(chosen, home[index : index + 1, :], 0.0), axis=1, keepdims=True)
+        return jnp.broadcast_to(picked, (slots, LANES))
+
+    taps_x, taps_y, taps_z = (spline_taps(field(dim)) for dim in range(3))
+    first_y, first_z = field(3).astype(jnp.int32), field(4).astype(jnp.int32)
+    along_x = lane & 3
+    is_x = [along_x == tap for tap in range(3)]
+
+    def pick_x(taps):
+        return jnp.where(is_x[0], taps[0], jnp.where(is_x[1], taps[1], jnp.where(is_x[2], taps[2], taps[3])))
+
+    def pick(hits, taps):
+        out = jnp.where(hits[3], taps[3], 0.0)
+        for tap in (2, 1, 0):
+            out = jnp.where(hits[tap], taps[tap], out)
+        return out
+
+    x_value, x_slope, x_curve = (pick_x(taps) for taps in taps_x)
+    offset_z = ((lane // 4) - first_z) & (grid_width - 1)
+    hits_z = [offset_z == tap for tap in range(4)]
+    z_value, z_slope, z_curve = (pick(hits_z, taps) for taps in taps_z)
+    plain = z_value * x_value
+    with_x = z_value * x_slope
+    with_z = z_slope * x_value
+    with_both = z_value * x_curve + z_curve * x_value
+    per_chunk = LANES // (4 * grid_width)
+    for chunk in range(grid_width // per_chunk):
+        offset_y = (chunk * per_chunk + lane // (4 * grid_width) - first_y) & (grid_width - 1)
+        hits_y = [offset_y == tap for tap in range(4)]
+        y_value, y_slope, y_curve = (pick(hits_y, taps) for taps in taps_y)
+        weights = (
+            y_value * plain,
+            y_value * with_x,
+            y_slope * plain,
+            y_value * with_z,
+            y_value * with_both + y_curve * plain,
+        )
+        columns = slice(chunk * LANES, (chunk + 1) * LANES)
+        for k, weight in enumerate(weights):
+            high = weight.astype(BF16)
+            high_ref[k * slots : (k + 1) * slots, columns] = high
+            low_ref[k * slots : (k + 1) * slots, columns] = (weight - high.astype(F32)).astype(BF16)
+
+
+def contract(weight_high, weight_low, table_high, table_low):
+    dot = functools.partial(jnp.dot, preferred_element_type=F32)
+    return dot(weight_high, table_high) + (dot(weight_low, table_high) + dot(weight_high, table_low))
+
+
+def store_slots(out_ref, lanes, result, capacity, slots):
+    for k in range(5):
+        out_ref[k * capacity : k * capacity + slots, lanes] = result[k * slots : (k + 1) * slots].astype(BF16)
+
+
+def far_kernel(capacity, slots, grid_width, skip, *refs):
+    homes_refs, (high_ref, low_ref), outs, scratch = refs[:2], refs[2:4], refs[4:-4], refs[-4:]
+    slab, orb = lax.axis_index("slab"), lax.axis_index("orb")
+    lanes = slice(skip, high_ref.shape[1])
+    for index, out_ref in enumerate(outs):
+        weights = scratch[2 * (index % 2) : 2 * (index % 2) + 2]
+        home = homes_refs[index // 4][orb ^ (index % 4)]
+        slot_weights(home, slab, slots, grid_width, *weights)
+        result = contract(weights[0][...], weights[1][...], high_ref[:, lanes], low_ref[:, lanes])
+        store_slots(out_ref, slice(None), result, capacity, slots)
+
+
+def near_kernel(capacity, slots, grid_width, *refs):
+    homes_refs, (high_ref, low_ref), (mine_ref, other_ref) = refs[:2], refs[2:4], refs[4:6]
+    outs, scratch, (far_high, far_low) = refs[6:-6], refs[-6:-2], refs[-2:]
+    slab, orb, group = lax.axis_index("slab"), lax.axis_index("orb"), lax.axis_index("groups")
+    half = mine_ref.shape[0]
+    width = high_ref.shape[1]
+    for part_ref, part in ((mine_ref, group), (other_ref, 1 - group)):
+        table = part_ref[...]
+        high = table.astype(BF16)
+        rows = pl.ds(pl.multiple_of(part * half, half), half)
+        far_high[rows, :] = high
+        far_low[rows, :] = (table - high.astype(F32)).astype(BF16)
+    for index, out_ref in enumerate(outs):
+        home = homes_refs[index // 4][orb ^ (index % 4)]
+        weights = scratch[:2]
+        slot_weights(home, slab, slots, grid_width, *weights)
+        result = contract(weights[0][...], weights[1][...], high_ref[...], low_ref[...])
+        store_slots(out_ref, slice(0, width), result, capacity, slots)
+        weights = scratch[2:]
+        slot_weights(home, slab ^ 2, slots, grid_width, *weights)
+        result = contract(weights[0][...], weights[1][...], far_high[...], far_low[...])
+        store_slots(out_ref, slice(width, out_ref.shape[1]), result, capacity, slots)
+
+
+def place_kernel(capacity, skip, packed_ref, *refs):
+    near, far, out_ref = refs[:8], refs[8:16], refs[16]
+    slab, orb = lax.axis_index("slab"), lax.axis_index("orb")
+    electrons = out_ref.shape[1]
+    rows, width = near[0].shape[0], near[0].shape[1] - skip
+    owner = to_column(packed_ref[5:6, :electrons])
+    slot = to_column(packed_ref[6:7, :electrons])
+    column = iota((electrons, rows), 1).astype(F32)
+    picks = []
+    for step in range(4):
+        wanted = jnp.where(owner == (slab ^ step).astype(F32), slot, -1000.0)
+        picks.append(jnp.concatenate([(column == wanted + float(k * capacity)).astype(BF16) for k in range(5)], axis=0))
+    dot = functools.partial(jnp.dot, preferred_element_type=F32)
+    for turn in range(4):
+        start = (orb ^ turn) * width
+        here, beside = near[turn], near[4 + turn]
+        main = dot(picks[0], here[:, skip:width]) + dot(picks[1], beside[:, skip:width])
+        main = main + dot(picks[2], far[turn][...]) + dot(picks[3], far[4 + turn][...])
+        edge = dot(picks[0], here[:, :skip]) + dot(picks[1], beside[:, :skip])
+        edge = edge + dot(picks[2], here[:, width:]) + dot(picks[3], beside[:, width:])
+        for k in range(5):
+            band = slice(k * electrons, (k + 1) * electrons)
+            out_ref[k, :, pl.ds(pl.multiple_of(start, LANES), skip)] = edge[band].astype(BF16)
+            out_ref[k, :, pl.ds(pl.multiple_of(start + skip, LANES), width - skip)] = main[band].astype(BF16)
+
+
+def swap(array, step, count, axes):
+    return lax.ppermute(array, axes, [(i, i ^ step) for i in range(count)])
+
+
+def small_body(fractions, cell_index, slab_owner, spline_table):
+    electrons = slab_owner.shape[0]
+    grid_width, orb_local = spline_table.shape[1], spline_table.shape[4]
+    capacity = slot_capacity(electrons, 4)
+    slots = -(-capacity // 16) * 16
+    rows = 4 * capacity + slots
+    taps = grid_width * grid_width * 4
+    skip = orb_local // 4
+    vmem = pltpu.CompilerParams(vmem_limit_bytes=48 * 1024 * 1024)
+
+    group = lax.axis_index("groups")
+    part = lax.dynamic_slice_in_dim(spline_table, group * (grid_width // 2), grid_width // 2, axis=1)
+    part = part[..., :skip].reshape(taps // 2, skip)
+    mine = swap(part, 2, 4, "slab")
+    other = swap(mine, 1, 2, "groups")
+
+    packed = pl.pallas_call(
+        pack_kernel, out_shape=jax.ShapeDtypeStruct((8, LANES), F32), name="pack"
+    )(fractions, cell_index, slab_owner.reshape(1, electrons))
+    homes = [lax.all_gather(packed, "orb")]
+    homes += [swap(homes[0], step, 4, "slab") for step in (1, 2, 3)]
+
+    table_high, table_low = pl.pallas_call(
+        split_kernel,
+        out_shape=[jax.ShapeDtypeStruct((taps, orb_local), BF16)] * 2,
+        compiler_params=vmem,
+        name="split",
+    )(spline_table.reshape(taps, orb_local))
+
+    weights = [pltpu.VMEM((5 * slots, taps), BF16)] * 4
+    far_out = pl.pallas_call(
+        functools.partial(far_kernel, capacity, slots, grid_width, skip),
+        out_shape=[jax.ShapeDtypeStruct((rows, orb_local - skip), BF16)] * 8,
+        scratch_shapes=weights,
+        compiler_params=vmem,
+        name="far",
+    )(homes[2], homes[3], table_high, table_low)
+    far = [swap(block, 8 + index, 16, ("slab", "orb")) for index, block in enumerate(far_out)]
+    near_out = pl.pallas_call(
+        functools.partial(near_kernel, capacity, slots, grid_width),
+        out_shape=[jax.ShapeDtypeStruct((rows, orb_local + skip), BF16)] * 8,
+        scratch_shapes=weights + [pltpu.VMEM((taps, skip), BF16)] * 2,
+        compiler_params=vmem,
+        name="near",
+    )(homes[0], homes[1], table_high, table_low, mine, other)
+    near = [near_out[0]] + [swap(block, index, 16, ("slab", "orb")) for index, block in enumerate(near_out) if index]
+    return pl.pallas_call(
+        functools.partial(place_kernel, capacity, skip),
+        out_shape=jax.ShapeDtypeStruct((5, electrons, 4 * orb_local), BF16),
+        compiler_params=vmem,
+        name="place",
+    )(packed, *near, *far)
+
+
 def solution(mesh):
     in_specs = (
         P(None, ("groups", "slab", "orb")),
@@ -107,4 +328,6 @@
         P("slab", None, None, None, "orb"),
     )
     out_specs = P(None, ("groups", "slab", "orb"), None)
+    small = (mesh.shape["groups"], mesh.shape["slab"], mesh.shape["orb"]) == (2, 4, 4)
+    body = small_body if small else general_body
     return jax.shard_map(body, mesh=mesh, in_specs=in_specs, out_specs=out_specs, check_vma=False)

time: 207 us -> 101 us (0.49)
  the two profiles are of different devices: /device:TPU:0 before, /device:TPU:1 now
where the time goes in v1:
time: 101 us
  starting transfers between devices  41.7 us (41%)
  waiting for transfers between devices  26.2 us (26%)
  Pallas kernels  23.3 us (23%)
  blocking collectives  6.9 us (7%)
  local copies, waits for them, and re-layouts  2.95 us (3%)
    ppermute x20, starting transfers between devices, swap(): return lax.ppermute(array, axes, [(i, i ^ step) for i in range(count)])  41.7 us
    ppermute x20, waiting for transfers between devices, swap(): return lax.ppermute(array, axes, [(i, i ^ step) for i in range(count)])  26.2 us
    pallas_call x1, Pallas kernels, small_body(): pl.pallas_call(functools.partial(near_kernel, capacity, slots, grid_width...  10.9 us
    all_gather x1, blocking collectives, small_body(): homes = [lax.all_gather(packed, 'orb')]  6.9 us
    pallas_call x1, Pallas kernels, small_body(): pl.pallas_call(functools.partial(far_kernel, capacity, slots, grid_width,...  5.99 us
    pallas_call x1, Pallas kernels, small_body(): pl.pallas_call(functools.partial(place_kernel, capacity, skip), out_shape...  4.7 us
  transfers between devices with their start and end apart: 20, of which 6 were waited for; matrix products, arithmetic and copies ran while one was open for 2% of the time, Pallas kernels for 18%

profile of v1, /device:TPU:1, one launch (start us, length us, event | category | flops | bytes accessed | tf_op | source)
XLA Modules:
  0.0 101.2 jit_solution(5101835554618353545)
XLA Ops:
  0.0 1.0 constant_dynamic-slice_fusion
  1.0 3.2 %collective-permute-start.1 = (f32[512,128]{1,0:T(8,128)S(1)}, f32[512,128]{1,0:T(8,128)S(1)}, u32[]{:S(2)}, u32[]{:S(2)}) collective-permute-start(f32[512,128]{1,0:T(8,128)S(1)} %bitcast.7), channel_id=1, source_target_pairs={{0,8},{4,12},{8,0},{12,4},{1,9},{5,13},{9,1},{13,5},{2,10},{6,14},... | collective-permute-start | bytes 786440 | tf_op jit(solution)/shard_map/ppermute | solution.py:266
  4.2 11.6 %collective-permute-done.1.refs_4_ = f32[512,128]{1,0:T(8,128)S(1)} collective-permute-done((f32[512,128]{1,0:T(8,128)S(1)}, f32[512,128]{1,0:T(8,128)S(1)}, u32[]{:S(2)}, u32[]{:S(2)}) %collective-permute-start.1) | collective-permute-done | bytes 262176 | tf_op jit(solution)/shard_map/ppermute | solution.py:266
  15.8 1.0 collective-permute-start.2
  16.8 1.4 %pack.1.packed_ref = f32[8,128]{1,0:T(8,128)} custom-call(f32[3,96]{1,0:T(4,128)} %fractions_ref.1, s32[2,96]{1,0:T(2,128)} %cells_ref.1, s32[1,96]{1,0:T(1,128)} %bitcast.8), custom_call_target="tpu_custom_call" | custom-call | tf_op jit(solution)/shard_map/pack/pallas_call | solution.py:285
  18.2 6.9 %all-gather = f32[32,128]{1,0:T(8,128)S(1)} all-gather(f32[8,128]{1,0:T(8,128)} %pack.1.packed_ref), channel_id=2, replica_groups=mesh['groups'=2,'slab'=4,'orb'=4] {'orb'}, dimensions={0}, use_global_device_ids=true | all-gather | bytes 20480 | tf_op jit(solution)/shard_map/all_gather | solution.py:288
  25.2 3.3 %collective-permute-start.11 = (f32[4,8,128]{2,1,0:T(8,128)S(1)}, f32[4,8,128]{2,1,0:T(8,128)S(1)}, u32[]{:S(2)}, u32[]{:S(2)}) collective-permute-start(f32[4,8,128]{2,1,0:T(8,128)S(1)} %bitcast.4), channel_id=1, source_target_pairs={{0,12},{4,8},{8,4},{12,0},{1,13},{5,9},{9,5},{13,1},{2,14},{6,10},... | collective-permute-start | bytes 49160 | tf_op jit(solution)/shard_map/ppermute | solution.py:266
  28.5 2.0 %reshape.10.table_ref = f32[1024,512]{1,0:T(8,128)S(1)} reshape(f32[1,16,16,4,512]{4,3,2,1,0:T(4,128)} %param.7) | data formatting | bytes 4194304 | tf_op jit(solution)/shard_map/reshape | solution.py:296
  30.4 0.3 split.1
  30.8 6.0 %far.1 = (bf16[152,384]{1,0:T(8,128)(2,1)S(1)}, bf16[152,384]{1,0:T(8,128)(2,1)S(1)}, bf16[152,384]{1,0:T(8,128)(2,1)S(1)}, bf16[152,384]{1,0:T(8,128)(2,1)S(1)}...) custom-call(f32[4,8,128]{2,1,0:T(8,128)S(1)} %collective-permute-don, ...), custom_call_target="tpu_custom_call" | custom-call | tf_op jit(solution)/shard_map/far/pallas_call | solution.py:299
  36.8 1.4 %collective-permute-start.12 = (bf16[152,384]{1,0:T(8,128)(2,1)S(1)}, bf16[152,384]{1,0:T(8,128)(2,1)S(1)}, u32[]{:S(2)}, u32[]{:S(2)}) collective-permute-start(bf16[152,384]{1,0:T(8,128)(2,1)S(1)} %get-tuple-element.33), channel_id=1, source_target_pairs={{0,8},{1,9},{2,10},{3,11},{4,12},{5,13},{6,14},{7,15},{8,0},{9,1},... | collective-permute-start | bytes 350216 | tf_op jit(solution)/shard_map/ppermute | solution.py:266
  38.2 1.5 %collective-permute-start.13 = (bf16[152,384]{1,0:T(8,128)(2,1)S(1)}, bf16[152,384]{1,0:T(8,128)(2,1)S(1)}, u32[]{:S(2)}, u32[]{:S(2)}) collective-permute-start(bf16[152,384]{1,0:T(8,128)(2,1)S(1)} %get-tuple-element.34), channel_id=1, source_target_pairs={{0,9},{1,8},{2,11},{3,10},{4,13},{5,12},{6,15},{7,14},{8,1},{9,0},... | collective-permute-start | bytes 350216 | tf_op jit(solution)/shard_map/ppermute | solution.py:266
  39.7 1.7 %collective-permute-start = (f32[4,8,128]{2,1,0:T(8,128)S(1)}, f32[4,8,128]{2,1,0:T(8,128)S(1)}, u32[]{:S(2)}, u32[]{:S(2)}) collective-permute-start(f32[4,8,128]{2,1,0:T(8,128)S(1)} %bitcast.5), channel_id=1, source_target_pairs={{0,4},{4,0},{8,12},{12,8},{1,5},{5,1},{9,13},{13,9},{2,6},{6,2},{1... | collective-permute-start | bytes 49160 | tf_op jit(solution)/shard_map/ppermute | solution.py:266
  41.4 2.4 %collective-permute-start.14 = (bf16[152,384]{1,0:T(8,128)(2,1)S(1)}, bf16[152,384]{1,0:T(8,128)(2,1)S(1)}, u32[]{:S(2)}, u32[]{:S(2)}) collective-permute-start(bf16[152,384]{1,0:T(8,128)(2,1)S(1)} %get-tuple-element.35), channel_id=1, source_target_pairs={{0,10},{1,11},{2,8},{3,9},{4,14},{5,15},{6,12},{7,13},{8,2},{9,3},... | collective-permute-start | bytes 350216 | tf_op jit(solution)/shard_map/ppermute | solution.py:266
  43.9 4.5 %collective-permute-start.15 = (bf16[152,384]{1,0:T(8,128)(2,1)S(1)}, bf16[152,384]{1,0:T(8,128)(2,1)S(1)}, u32[]{:S(2)}, u32[]{:S(2)}) collective-permute-start(bf16[152,384]{1,0:T(8,128)(2,1)S(1)} %get-tuple-element.36), channel_id=1, source_target_pairs={{0,11},{1,10},{2,9},{3,8},{4,15},{5,14},{6,13},{7,12},{8,3},{9,2},... | collective-permute-start | bytes 350216 | tf_op jit(solution)/shard_map/ppermute | solution.py:266
  48.4 1.8 %collective-permute-start.16 = (bf16[152,384]{1,0:T(8,128)(2,1)S(1)}, bf16[152,384]{1,0:T(8,128)(2,1)S(1)}, u32[]{:S(2)}, u32[]{:S(2)}) collective-permute-start(bf16[152,384]{1,0:T(8,128)(2,1)S(1)} %get-tuple-element.37), channel_id=1, source_target_pairs={{0,12},{1,13},{2,14},{3,15},{4,8},{5,9},{6,10},{7,11},{8,4},{9,5},... | collective-permute-start | bytes 350216 | tf_op jit(solution)/shard_map/ppermute | solution.py:266
  50.2 10.9 %near.1 = (bf16[152,640]{1,0:T(8,128)(2,1)S(1)}, bf16[152,640]{1,0:T(8,128)(2,1)S(1)}, bf16[152,640]{1,0:T(8,128)(2,1)S(1)}, bf16[152,640]{1,0:T(8,128)(2,1)S(1)...) custom-call(f32[4,8,128]{2,1,0:T(8,128)S(1)} %bitcast.6, ...), custom_call_target="tpu_custom_call" | custom-call | tf_op jit(solution)/shard_map/near/pallas_call | solution.py:307
  61.1 0.1 collective-permute-start.3
  61.2 0.1 collective-permute-start.4
  61.3 2.7 %collective-permute-start.17 = (bf16[152,384]{1,0:T(8,128)(2,1)S(1)}, bf16[152,384]{1,0:T(8,128)(2,1)S(1)}, u32[]{:S(2)}, u32[]{:S(2)}) collective-permute-start(bf16[152,384]{1,0:T(8,128)(2,1)S(1)} %get-tuple-element.38), channel_id=1, source_target_pairs={{0,13},{1,12},{2,15},{3,14},{4,9},{5,8},{6,11},{7,10},{8,5},{9,4},... | collective-permute-start | bytes 350216 | tf_op jit(solution)/shard_map/ppermute | solution.py:266
  64.0 2.3 %collective-permute-start.18 = (bf16[152,384]{1,0:T(8,128)(2,1)S(1)}, bf16[152,384]{1,0:T(8,128)(2,1)S(1)}, u32[]{:S(2)}, u32[]{:S(2)}) collective-permute-start(bf16[152,384]{1,0:T(8,128)(2,1)S(1)} %get-tuple-element.39), channel_id=1, source_target_pairs={{0,14},{1,15},{2,12},{3,13},{4,10},{5,11},{6,8},{7,9},{8,6},{9,7},... | collective-permute-start | bytes 350216 | tf_op jit(solution)/shard_map/ppermute | solution.py:266
  66.3 2.0 %collective-permute-start.19 = (bf16[152,384]{1,0:T(8,128)(2,1)S(1)}, bf16[152,384]{1,0:T(8,128)(2,1)S(1)}, u32[]{:S(2)}, u32[]{:S(2)}) collective-permute-start(bf16[152,384]{1,0:T(8,128)(2,1)S(1)} %get-tuple-element.40), channel_id=1, source_target_pairs={{0,15},{1,14},{2,13},{3,12},{4,11},{5,10},{6,9},{7,8},{8,7},{9,6},... | collective-permute-start | bytes 350216 | tf_op jit(solution)/shard_map/ppermute | solution.py:266
  68.3 0.6 collective-permute-done.17.refs_13_
  68.9 1.8 %collective-permute-start.5 = (bf16[152,640]{1,0:T(8,128)(2,1)S(1)}, bf16[152,640]{1,0:T(8,128)(2,1)S(1)}, u32[]{:S(2)}, u32[]{:S(2)}) collective-permute-start(bf16[152,640]{1,0:T(8,128)(2,1)S(1)} %get-tuple-element.28), channel_id=1, source_target_pairs={{0,3},{1,2},{2,1},{3,0},{4,7},{5,6},{6,5},{7,4},{8,11},{9,10},{10,... | collective-permute-start | bytes 583688 | tf_op jit(solution)/shard_map/ppermute | solution.py:266
  70.7 1.9 %collective-permute-done.18.refs_14_ = bf16[152,384]{1,0:T(8,128)(2,1)S(1)} collective-permute-done((bf16[152,384]{1,0:T(8,128)(2,1)S(1)}, bf16[152,384]{1,0:T(8,128)(2,1)S(1)}, u32[]{:S(2)}, u32[]{:S(2)}) %collective-permute-start.18) | collective-permute-done | bytes 116768 | tf_op jit(solution)/shard_map/ppermute | solution.py:266
  72.6 6.3 %collective-permute-start.6 = (bf16[152,640]{1,0:T(8,128)(2,1)S(1)}, bf16[152,640]{1,0:T(8,128)(2,1)S(1)}, u32[]{:S(2)}, u32[]{:S(2)}) collective-permute-start(bf16[152,640]{1,0:T(8,128)(2,1)S(1)} %get-tuple-element.29), channel_id=1, source_target_pairs={{0,4},{1,5},{2,6},{3,7},{4,0},{5,1},{6,2},{7,3},{8,12},{9,13},{10,... | collective-permute-start | bytes 583688 | tf_op jit(solution)/shard_map/ppermute | solution.py:266
  78.9 2.9 %collective-permute-start.7 = (bf16[152,640]{1,0:T(8,128)(2,1)S(1)}, bf16[152,640]{1,0:T(8,128)(2,1)S(1)}, u32[]{:S(2)}, u32[]{:S(2)}) collective-permute-start(bf16[152,640]{1,0:T(8,128)(2,1)S(1)} %get-tuple-element.30), channel_id=1, source_target_pairs={{0,5},{1,4},{2,7},{3,6},{4,1},{5,0},{6,3},{7,2},{8,13},{9,12},{10,... | collective-permute-start | bytes 583688 | tf_op jit(solution)/shard_map/ppermute | solution.py:266
  81.8 2.6 %collective-permute-start.9 = (bf16[152,640]{1,0:T(8,128)(2,1)S(1)}, bf16[152,640]{1,0:T(8,128)(2,1)S(1)}, u32[]{:S(2)}, u32[]{:S(2)}) collective-permute-start(bf16[152,640]{1,0:T(8,128)(2,1)S(1)} %get-tuple-element.32), channel_id=1, source_target_pairs={{0,7},{1,6},{2,5},{3,4},{4,3},{5,2},{6,1},{7,0},{8,15},{9,14},{10,... | collective-permute-start | bytes 583688 | tf_op jit(solution)/shard_map/ppermute | solution.py:266
  84.4 5.3 %collective-permute-done.7.refs_5_ = bf16[152,640]{1,0:T(8,128)(2,1)S(1)} collective-permute-done((bf16[152,640]{1,0:T(8,128)(2,1)S(1)}, bf16[152,640]{1,0:T(8,128)(2,1)S(1)}, u32[]{:S(2)}, u32[]{:S(2)}) %collective-permute-start.7) | collective-permute-done | bytes 194592 | tf_op jit(solution)/shard_map/ppermute | solution.py:266
  89.7 1.8 %collective-permute-done.8.refs_6_ = bf16[152,640]{1,0:T(8,128)(2,1)S(1)} collective-permute-done((bf16[152,640]{1,0:T(8,128)(2,1)S(1)}, bf16[152,640]{1,0:T(8,128)(2,1)S(1)}, u32[]{:S(2)}, u32[]{:S(2)}) %collective-permute-start.8) | collective-permute-done | bytes 194592 | tf_op jit(solution)/shard_map/ppermute | solution.py:266
  91.5 5.0 %collective-permute-done.9.refs_7_ = bf16[152,640]{1,0:T(8,128)(2,1)S(1)} collective-permute-done((bf16[152,640]{1,0:T(8,128)(2,1)S(1)}, bf16[152,640]{1,0:T(8,128)(2,1)S(1)}, u32[]{:S(2)}, u32[]{:S(2)}) %collective-permute-start.9) | collective-permute-done | bytes 194592 | tf_op jit(solution)/shard_map/ppermute | solution.py:266
  96.5 4.7 %place.1 = bf16[5,96,2048]{2,1,0:T(8,128)(2,1)} custom-call(f32[8,128]{1,0:T(8,128)S(1)} %copy-done, bf16[152,640]{1,0:T(8,128)(2,1)S(1)} %get-tuple-element.25.refs_0_, bf16[152,640]{1,0:T(8,128)(2,1)S(1)} %collective-permute-done.3.refs_1_, bf16[152,640]{1,0:T(8,128)(2,1)S(1)} %collective-permute-done.4.refs_2_, ...), custom_call_target="tpu_custom_call" | custom-call | tf_op jit(solution)/shard_map/place/pallas_call | solution.py:315
  (18 shorter events, 0.1 us)
Async XLA Ops:
  1.0 14.9 %collective-permute-start.1 = (f32[512,128]{1,0:T(8,128)S(1)}, f32[512,128]{1,0:T(8,128)S(1)}, u32[]{:S(2)}, u32[]{:S(2)}) collective-permute-start(f32[512,128]{1,0:T(8,128)S(1)} %bitcast.7), channel_id=1, source_target_pairs={{0,8},{4,12},{8,0},{12,4},{1,9},{5,13},{9,1},{13,5},{2,10},{6,14},... | collective-permute-start | bytes 786440 | tf_op jit(solution)/shard_map/ppermute | solution.py:266
  15.8 32.6 %collective-permute-start.2 = (f32[512,128]{1,0:T(8,128)S(1)}, f32[512,128]{1,0:T(8,128)S(1)}, u32[]{:S(2)}, u32[]{:S(2)}) collective-permute-start(f32[512,128]{1,0:T(8,128)S(1)} %collective-permute-done.1.refs_4_), channel_id=1, source_target_pairs={{0,16},{16,0},{1,17},{17,1},{2,18},{18,2},{3,19},{19,3},{4,20},{20... | collective-permute-start | bytes 786440 | tf_op jit(solution)/shard_map/ppermute | solution.py:266
  25.1 5.6 %collective-permute-start.10 = (f32[4,8,128]{2,1,0:T(8,128)S(1)}, f32[4,8,128]{2,1,0:T(8,128)S(1)}, u32[]{:S(2)}, u32[]{:S(2)}) collective-permute-start(f32[4,8,128]{2,1,0:T(8,128)S(1)} %bitcast.3), channel_id=1, source_target_pairs={{0,8},{4,12},{8,0},{12,4},{1,9},{5,13},{9,1},{13,5},{2,10},{6,14},... | collective-permute-start | bytes 49160 | tf_op jit(solution)/shard_map/ppermute | solution.py:266
  25.2 5.6 %collective-permute-start.11 = (f32[4,8,128]{2,1,0:T(8,128)S(1)}, f32[4,8,128]{2,1,0:T(8,128)S(1)}, u32[]{:S(2)}, u32[]{:S(2)}) collective-permute-start(f32[4,8,128]{2,1,0:T(8,128)S(1)} %bitcast.4), channel_id=1, source_target_pairs={{0,12},{4,8},{8,4},{12,0},{1,13},{5,9},{9,5},{13,1},{2,14},{6,10},... | collective-permute-start | bytes 49160 | tf_op jit(solution)/shard_map/ppermute | solution.py:266
  30.8 65.8 %copy-start = (f32[8,128]{1,0:T(8,128)S(1)}, f32[8,128]{1,0:T(8,128)}, u32[]{:S(2)}) copy-start(f32[8,128]{1,0:T(8,128)} %pack.1.packed_ref) | copy-start | bytes 12292
  36.8 24.4 %collective-permute-start.12 = (bf16[152,384]{1,0:T(8,128)(2,1)S(1)}, bf16[152,384]{1,0:T(8,128)(2,1)S(1)}, u32[]{:S(2)}, u32[]{:S(2)}) collective-permute-start(bf16[152,384]{1,0:T(8,128)(2,1)S(1)} %get-tuple-element.33), channel_id=1, source_target_pairs={{0,8},{1,9},{2,10},{3,11},{4,12},{5,13},{6,14},{7,15},{8,0},{9,1},... | collective-permute-start | bytes 350216 | tf_op jit(solution)/shard_map/ppermute | solution.py:266
  38.2 23.0 %collective-permute-start.13 = (bf16[152,384]{1,0:T(8,128)(2,1)S(1)}, bf16[152,384]{1,0:T(8,128)(2,1)S(1)}, u32[]{:S(2)}, u32[]{:S(2)}) collective-permute-start(bf16[152,384]{1,0:T(8,128)(2,1)S(1)} %get-tuple-element.34), channel_id=1, source_target_pairs={{0,9},{1,8},{2,11},{3,10},{4,13},{5,12},{6,15},{7,14},{8,1},{9,0},... | collective-permute-start | bytes 350216 | tf_op jit(solution)/shard_map/ppermute | solution.py:266
  39.7 4.2 %collective-permute-start = (f32[4,8,128]{2,1,0:T(8,128)S(1)}, f32[4,8,128]{2,1,0:T(8,128)S(1)}, u32[]{:S(2)}, u32[]{:S(2)}) collective-permute-start(f32[4,8,128]{2,1,0:T(8,128)S(1)} %bitcast.5), channel_id=1, source_target_pairs={{0,4},{4,0},{8,12},{12,8},{1,5},{5,1},{9,13},{13,9},{2,6},{6,2},{1... | collective-permute-start | bytes 49160 | tf_op jit(solution)/shard_map/ppermute | solution.py:266
  41.4 19.9 %collective-permute-start.14 = (bf16[152,384]{1,0:T(8,128)(2,1)S(1)}, bf16[152,384]{1,0:T(8,128)(2,1)S(1)}, u32[]{:S(2)}, u32[]{:S(2)}) collective-permute-start(bf16[152,384]{1,0:T(8,128)(2,1)S(1)} %get-tuple-element.35), channel_id=1, source_target_pairs={{0,10},{1,11},{2,8},{3,9},{4,14},{5,15},{6,12},{7,13},{8,2},{9,3},... | collective-permute-start | bytes 350216 | tf_op jit(solution)/shard_map/ppermute | solution.py:266
  43.9 20.2 %collective-permute-start.15 = (bf16[152,384]{1,0:T(8,128)(2,1)S(1)}, bf16[152,384]{1,0:T(8,128)(2,1)S(1)}, u32[]{:S(2)}, u32[]{:S(2)}) collective-permute-start(bf16[152,384]{1,0:T(8,128)(2,1)S(1)} %get-tuple-element.36), channel_id=1, source_target_pairs={{0,11},{1,10},{2,9},{3,8},{4,15},{5,14},{6,13},{7,12},{8,3},{9,2},... | collective-permute-start | bytes 350216 | tf_op jit(solution)/shard_map/ppermute | solution.py:266
  48.4 17.9 %collective-permute-start.16 = (bf16[152,384]{1,0:T(8,128)(2,1)S(1)}, bf16[152,384]{1,0:T(8,128)(2,1)S(1)}, u32[]{:S(2)}, u32[]{:S(2)}) collective-permute-start(bf16[152,384]{1,0:T(8,128)(2,1)S(1)} %get-tuple-element.37), channel_id=1, source_target_pairs={{0,12},{1,13},{2,14},{3,15},{4,8},{5,9},{6,10},{7,11},{8,4},{9,5},... | collective-permute-start | bytes 350216 | tf_op jit(solution)/shard_map/ppermute | solution.py:266
  61.1 20.7 %collective-permute-start.3 = (bf16[152,640]{1,0:T(8,128)(2,1)S(1)}, bf16[152,640]{1,0:T(8,128)(2,1)S(1)}, u32[]{:S(2)}, u32[]{:S(2)}) collective-permute-start(bf16[152,640]{1,0:T(8,128)(2,1)S(1)} %get-tuple-element.26), channel_id=1, source_target_pairs={{0,1},{1,0},{2,3},{3,2},{4,5},{5,4},{6,7},{7,6},{8,9},{9,8},{10,11... | collective-permute-start | bytes 583688 | tf_op jit(solution)/shard_map/ppermute | solution.py:266
  61.2 20.6 %collective-permute-start.4 = (bf16[152,640]{1,0:T(8,128)(2,1)S(1)}, bf16[152,640]{1,0:T(8,128)(2,1)S(1)}, u32[]{:S(2)}, u32[]{:S(2)}) collective-permute-start(bf16[152,640]{1,0:T(8,128)(2,1)S(1)} %get-tuple-element.27), channel_id=1, source_target_pairs={{0,2},{1,3},{2,0},{3,1},{4,6},{5,7},{6,4},{7,5},{8,10},{9,11},{10,... | collective-permute-start | bytes 583688 | tf_op jit(solution)/shard_map/ppermute | solution.py:266
  61.3 7.6 %collective-permute-start.17 = (bf16[152,384]{1,0:T(8,128)(2,1)S(1)}, bf16[152,384]{1,0:T(8,128)(2,1)S(1)}, u32[]{:S(2)}, u32[]{:S(2)}) collective-permute-start(bf16[152,384]{1,0:T(8,128)(2,1)S(1)} %get-tuple-element.38), channel_id=1, source_target_pairs={{0,13},{1,12},{2,15},{3,14},{4,9},{5,8},{6,11},{7,10},{8,5},{9,4},... | collective-permute-start | bytes 350216 | tf_op jit(solution)/shard_map/ppermute | solution.py:266
  64.0 8.6 %collective-permute-start.18 = (bf16[152,384]{1,0:T(8,128)(2,1)S(1)}, bf16[152,384]{1,0:T(8,128)(2,1)S(1)}, u32[]{:S(2)}, u32[]{:S(2)}) collective-permute-start(bf16[152,384]{1,0:T(8,128)(2,1)S(1)} %get-tuple-element.39), channel_id=1, source_target_pairs={{0,14},{1,15},{2,12},{3,13},{4,10},{5,11},{6,8},{7,9},{8,6},{9,7},... | collective-permute-start | bytes 350216 | tf_op jit(solution)/shard_map/ppermute | solution.py:266
  66.3 12.6 %collective-permute-start.19 = (bf16[152,384]{1,0:T(8,128)(2,1)S(1)}, bf16[152,384]{1,0:T(8,128)(2,1)S(1)}, u32[]{:S(2)}, u32[]{:S(2)}) collective-permute-start(bf16[152,384]{1,0:T(8,128)(2,1)S(1)} %get-tuple-element.40), channel_id=1, source_target_pairs={{0,15},{1,14},{2,13},{3,12},{4,11},{5,10},{6,9},{7,8},{8,7},{9,6},... | collective-permute-start | bytes 350216 | tf_op jit(solution)/shard_map/ppermute | solution.py:266
  68.9 15.5 %collective-permute-start.5 = (bf16[152,640]{1,0:T(8,128)(2,1)S(1)}, bf16[152,640]{1,0:T(8,128)(2,1)S(1)}, u32[]{:S(2)}, u32[]{:S(2)}) collective-permute-start(bf16[152,640]{1,0:T(8,128)(2,1)S(1)} %get-tuple-element.28), channel_id=1, source_target_pairs={{0,3},{1,2},{2,1},{3,0},{4,7},{5,6},{6,5},{7,4},{8,11},{9,10},{10,... | collective-permute-start | bytes 583688 | tf_op jit(solution)/shard_map/ppermute | solution.py:266
  72.6 11.8 %collective-permute-start.6 = (bf16[152,640]{1,0:T(8,128)(2,1)S(1)}, bf16[152,640]{1,0:T(8,128)(2,1)S(1)}, u32[]{:S(2)}, u32[]{:S(2)}) collective-permute-start(bf16[152,640]{1,0:T(8,128)(2,1)S(1)} %get-tuple-element.29), channel_id=1, source_target_pairs={{0,4},{1,5},{2,6},{3,7},{4,0},{5,1},{6,2},{7,3},{8,12},{9,13},{10,... | collective-permute-start | bytes 583688 | tf_op jit(solution)/shard_map/ppermute | solution.py:266
  78.9 10.8 %collective-permute-start.7 = (bf16[152,640]{1,0:T(8,128)(2,1)S(1)}, bf16[152,640]{1,0:T(8,128)(2,1)S(1)}, u32[]{:S(2)}, u32[]{:S(2)}) collective-permute-start(bf16[152,640]{1,0:T(8,128)(2,1)S(1)} %get-tuple-element.30), channel_id=1, source_target_pairs={{0,5},{1,4},{2,7},{3,6},{4,1},{5,0},{6,3},{7,2},{8,13},{9,12},{10,... | collective-permute-start | bytes 583688 | tf_op jit(solution)/shard_map/ppermute | solution.py:266
  81.8 9.7 %collective-permute-start.8 = (bf16[152,640]{1,0:T(8,128)(2,1)S(1)}, bf16[152,640]{1,0:T(8,128)(2,1)S(1)}, u32[]{:S(2)}, u32[]{:S(2)}) collective-permute-start(bf16[152,640]{1,0:T(8,128)(2,1)S(1)} %get-tuple-element.31), channel_id=1, source_target_pairs={{0,6},{1,7},{2,4},{3,5},{4,2},{5,3},{6,0},{7,1},{8,14},{9,15},{10,... | collective-permute-start | bytes 583688 | tf_op jit(solution)/shard_map/ppermute | solution.py:266
  81.8 14.7 %collective-permute-start.9 = (bf16[152,640]{1,0:T(8,128)(2,1)S(1)}, bf16[152,640]{1,0:T(8,128)(2,1)S(1)}, u32[]{:S(2)}, u32[]{:S(2)}) collective-permute-start(bf16[152,640]{1,0:T(8,128)(2,1)S(1)} %get-tuple-element.32), channel_id=1, source_target_pairs={{0,7},{1,6},{2,5},{3,4},{4,3},{5,2},{6,1},{7,0},{8,15},{9,14},{10,... | collective-permute-start | bytes 583688 | tf_op jit(solution)/shard_map/ppermute | solution.py:266

commit v2 on v1

--- a/solution.py
+++ b/solution.py
@@ -132,11 +132,14 @@
     packed_ref[6:7, :electrons] = slot
 
 
-def split_kernel(table_ref, high_ref, low_ref):
-    table = table_ref[...]
-    high = table.astype(BF16)
-    high_ref[...] = high
-    low_ref[...] = (table - high.astype(F32)).astype(BF16)
+def split_kernel(own_ref, partner_ref, high_ref, low_ref):
+    width = own_ref.shape[1]
+    for index, table_ref in enumerate((own_ref, partner_ref)):
+        lanes = slice(index * width, (index + 1) * width)
+        table = table_ref[...]
+        high = table.astype(BF16)
+        high_ref[:, lanes] = high
+        low_ref[:, lanes] = (table - high.astype(F32)).astype(BF16)
 
 
 def slot_weights(home, slab, slots, grid_width, high_ref, low_ref):
@@ -200,70 +203,100 @@
         out_ref[k * capacity : k * capacity + slots, lanes] = result[k * slots : (k + 1) * slots].astype(BF16)
 
 
-def far_kernel(capacity, slots, grid_width, skip, *refs):
-    homes_refs, (high_ref, low_ref), outs, scratch = refs[:2], refs[2:4], refs[4:-4], refs[-4:]
+def store_slots(out_ref, place, lanes, result, capacity, slots):
+    for k in range(5):
+        out_ref[place, k * capacity : k * capacity + slots, lanes] = result[k * slots : (k + 1) * slots].astype(BF16)
+
+
+def far_kernel(capacity, slots, grid_width, skip, homes_ref, high_ref, low_ref, *refs):
+    outs, scratch = refs[:2], refs[2:]
+    slab = lax.axis_index("slab")
+    width = high_ref.shape[1] // 2
+    for index, out_ref in enumerate(outs):
+        weights = scratch[2 * index : 2 * index + 2]
+        slot_weights(homes_ref[index], slab, slots, grid_width, *weights)
+        for half in range(2):
+            lanes = slice(half * width + skip, (half + 1) * width)
+            result = contract(weights[0][...], weights[1][...], high_ref[:, lanes], low_ref[:, lanes])
+            place = slice(half * (width - skip), (half + 1) * (width - skip))
+            for k in range(5):
+                band = result[k * slots : (k + 1) * slots].astype(BF16)
+                out_ref[k * capacity : k * capacity + slots, place] = band
+
+
+def near_kernel(capacity, slots, grid_width, home_ref, beside_ref, high_ref, low_ref, out_ref, *scratch):
     slab, orb = lax.axis_index("slab"), lax.axis_index("orb")
-    lanes = slice(skip, high_ref.shape[1])
-    for index, out_ref in enumerate(outs):
-        weights = scratch[2 * (index % 2) : 2 * (index % 2) + 2]
-        home = homes_refs[index // 4][orb ^ (index % 4)]
+    me = 2 * (slab & 1) + orb // 2
+    for step in range(4):
+        weights = scratch[2 * (step % 2) : 2 * (step % 2) + 2]
+        home = (home_ref, beside_ref)[step // 2][step % 2]
         slot_weights(home, slab, slots, grid_width, *weights)
-        result = contract(weights[0][...], weights[1][...], high_ref[:, lanes], low_ref[:, lanes])
-        store_slots(out_ref, slice(None), result, capacity, slots)
-
-
-def near_kernel(capacity, slots, grid_width, *refs):
-    homes_refs, (high_ref, low_ref), (mine_ref, other_ref) = refs[:2], refs[2:4], refs[4:6]
-    outs, scratch, (far_high, far_low) = refs[6:-6], refs[-6:-2], refs[-2:]
+        result = contract(weights[0][...], weights[1][...], high_ref[...], low_ref[...])
+        store_slots(out_ref, me ^ step, slice(None), result, capacity, slots)
+
+
+def copied_kernel(capacity, slots, grid_width, home_ref, beside_ref, *refs):
+    parts, out_ref, scratch, (high_ref, low_ref) = refs[:4], refs[4], refs[5:9], refs[9:]
     slab, orb, group = lax.axis_index("slab"), lax.axis_index("orb"), lax.axis_index("groups")
-    half = mine_ref.shape[0]
-    width = high_ref.shape[1]
-    for part_ref, part in ((mine_ref, group), (other_ref, 1 - group)):
+    me = 2 * (slab & 1) + orb // 2
+    half, width = parts[0].shape
+    for index, part_ref in enumerate(parts):
+        source = group if index % 2 == 0 else 1 - group
+        lanes = slice((index // 2) * width, (index // 2 + 1) * width)
+        rows = pl.ds(pl.multiple_of(source * half, half), half)
         table = part_ref[...]
         high = table.astype(BF16)
-        rows = pl.ds(pl.multiple_of(part * half, half), half)
-        far_high[rows, :] = high
-        far_low[rows, :] = (table - high.astype(F32)).astype(BF16)
-    for index, out_ref in enumerate(outs):
-        home = homes_refs[index // 4][orb ^ (index % 4)]
-        weights = scratch[:2]
-        slot_weights(home, slab, slots, grid_width, *weights)
+        high_ref[rows, lanes] = high
+        low_ref[rows, lanes] = (table - high.astype(F32)).astype(BF16)
+    for step in range(4):
+        weights = scratch[2 * (step % 2) : 2 * (step % 2) + 2]
+        home = (home_ref, beside_ref)[step // 2][step % 2]
+        slot_weights(home, slab ^ 2, slots, grid_width, *weights)
         result = contract(weights[0][...], weights[1][...], high_ref[...], low_ref[...])
-        store_slots(out_ref, slice(0, width), result, capacity, slots)
-        weights = scratch[2:]
-        slot_weights(home, slab ^ 2, slots, grid_width, *weights)
-        result = contract(weights[0][...], weights[1][...], far_high[...], far_low[...])
-        store_slots(out_ref, slice(width, out_ref.shape[1]), result, capacity, slots)
-
-
-def place_kernel(capacity, skip, packed_ref, *refs):
-    near, far, out_ref = refs[:8], refs[8:16], refs[16]
+        store_slots(out_ref, me ^ step, slice(None), result, capacity, slots)
+
+
+def place_kernel(capacity, slots, skip, packed_ref, near_ref, copied_ref, *refs):
+    far, out_ref = refs[:4], refs[4]
     slab, orb = lax.axis_index("slab"), lax.axis_index("orb")
+    me = 2 * (slab & 1) + orb // 2
     electrons = out_ref.shape[1]
-    rows, width = near[0].shape[0], near[0].shape[1] - skip
+    width = near_ref.shape[2] // 2
     owner = to_column(packed_ref[5:6, :electrons])
     slot = to_column(packed_ref[6:7, :electrons])
-    column = iota((electrons, rows), 1).astype(F32)
-    picks = []
-    for step in range(4):
-        wanted = jnp.where(owner == (slab ^ step).astype(F32), slot, -1000.0)
-        picks.append(jnp.concatenate([(column == wanted + float(k * capacity)).astype(BF16) for k in range(5)], axis=0))
-    dot = functools.partial(jnp.dot, preferred_element_type=F32)
-    for turn in range(4):
-        start = (orb ^ turn) * width
-        here, beside = near[turn], near[4 + turn]
-        main = dot(picks[0], here[:, skip:width]) + dot(picks[1], beside[:, skip:width])
-        main = main + dot(picks[2], far[turn][...]) + dot(picks[3], far[4 + turn][...])
-        edge = dot(picks[0], here[:, :skip]) + dot(picks[1], beside[:, :skip])
-        edge = edge + dot(picks[2], here[:, width:]) + dot(picks[3], beside[:, width:])
-        for k in range(5):
-            band = slice(k * electrons, (k + 1) * electrons)
-            out_ref[k, :, pl.ds(pl.multiple_of(start, LANES), skip)] = edge[band].astype(BF16)
-            out_ref[k, :, pl.ds(pl.multiple_of(start + skip, LANES), width - skip)] = main[band].astype(BF16)
+    step = jnp.zeros_like(owner)
+    for index in range(1, 4):
+        step = jnp.where(owner == (slab ^ index).astype(F32), float(index), step)
+    pick = (iota((electrons, 4 * slots), 1).astype(F32) == step * float(slots) + slot).astype(BF16)
+    for turn in range(2):
+        here, beside = me ^ turn, me ^ (2 + turn)
+        for half in range(2):
+            start = (orb ^ (2 * turn + half)) * width
+            for k in range(5):
+                rows = slice(k * capacity, k * capacity + slots)
+                main = slice(half * width + skip, (half + 1) * width)
+                main_far = slice(half * (width - skip), (half + 1) * (width - skip))
+                edge = slice(half * width, half * width + skip)
+                edge_far = slice(half * skip, (half + 1) * skip)
+                blocks = [near_ref[here, rows, main], near_ref[beside, rows, main], far[turn][rows, main_far], far[2 + turn][rows, main_far]]
+                placed = jnp.dot(pick, jnp.concatenate(blocks, axis=0), preferred_element_type=F32)
+                out_ref[k, :, pl.ds(pl.multiple_of(start + skip, LANES), width - skip)] = placed.astype(BF16)
+                blocks = [near_ref[here, rows, edge], near_ref[beside, rows, edge], copied_ref[here, rows, edge_far], copied_ref[beside, rows, edge_far]]
+                placed = jnp.dot(pick, jnp.concatenate(blocks, axis=0), preferred_element_type=F32)
+                out_ref[k, :, pl.ds(pl.multiple_of(start, LANES), skip)] = placed.astype(BF16)
 
 
 def swap(array, step, count, axes):
     return lax.ppermute(array, axes, [(i, i ^ step) for i in range(count)])
+
+
+def after(array, *others):
+    return lax.optimization_barrier((array, *others))[0]
+
+
+def trade(blocks):
+    members = [[4 * (2 * pair + s) + 2 * x + core for s in range(2) for x in range(2)] for pair in range(2) for core in range(2)]
+    return lax.all_to_all(blocks, ("slab", "orb"), 0, 0, axis_index_groups=members, tiled=True)
 
 
 def small_body(fractions, cell_index, slab_owner, spline_table):
@@ -275,49 +308,66 @@
     taps = grid_width * grid_width * 4
     skip = orb_local // 4
     vmem = pltpu.CompilerParams(vmem_limit_bytes=48 * 1024 * 1024)
-
-    group = lax.axis_index("groups")
-    part = lax.dynamic_slice_in_dim(spline_table, group * (grid_width // 2), grid_width // 2, axis=1)
-    part = part[..., :skip].reshape(taps // 2, skip)
-    mine = swap(part, 2, 4, "slab")
-    other = swap(mine, 1, 2, "groups")
-
+    weights = [pltpu.VMEM((5 * slots, taps), BF16)] * 4
+
+    partner_table = swap(spline_table, 1, 4, "orb")
     packed = pl.pallas_call(
         pack_kernel, out_shape=jax.ShapeDtypeStruct((8, LANES), F32), name="pack"
     )(fractions, cell_index, slab_owner.reshape(1, electrons))
-    homes = [lax.all_gather(packed, "orb")]
-    homes += [swap(homes[0], step, 4, "slab") for step in (1, 2, 3)]
+    home = jnp.stack([packed, swap(packed, 2, 4, "orb")])
+    beside, across, corner = (swap(home, step, 4, "slab") for step in (1, 2, 3))
+
+    group = lax.axis_index("groups")
+    part = lax.dynamic_slice_in_dim(after(spline_table, home), group * (grid_width // 2), grid_width // 2, axis=1)
+    part = part[..., :skip].reshape(taps // 2, skip)
+    mine = swap(part, 2, 4, "slab")
 
     table_high, table_low = pl.pallas_call(
         split_kernel,
-        out_shape=[jax.ShapeDtypeStruct((taps, orb_local), BF16)] * 2,
+        out_shape=[jax.ShapeDtypeStruct((taps, 2 * orb_local), BF16)] * 2,
         compiler_params=vmem,
         name="split",
-    )(spline_table.reshape(taps, orb_local))
-
-    weights = [pltpu.VMEM((5 * slots, taps), BF16)] * 4
-    far_out = pl.pallas_call(
-        functools.partial(far_kernel, capacity, slots, grid_width, skip),
-        out_shape=[jax.ShapeDtypeStruct((rows, orb_local - skip), BF16)] * 8,
+    )(spline_table.reshape(taps, orb_local), partner_table.reshape(taps, orb_local))
+
+    def far_blocks(homes):
+        return pl.pallas_call(
+            functools.partial(far_kernel, capacity, slots, grid_width, skip),
+            out_shape=[jax.ShapeDtypeStruct((rows, 2 * (orb_local - skip)), BF16)] * 2,
+            scratch_shapes=weights,
+            compiler_params=vmem,
+            name="far",
+        )(homes, table_high, table_low)
+
+    far_out = far_blocks(across) + far_blocks(corner)
+    far = [swap(block, 8 + 2 * index, 16, ("slab", "orb")) for index, block in enumerate(far_out)]
+
+    mine_late = after(mine, *far_out[:2])
+    other = swap(mine_late, 1, 2, "groups")
+    mine_partner = swap(mine_late, 1, 4, "orb")
+    other_partner = swap(other, 1, 4, "orb")
+
+    near_out = pl.pallas_call(
+        functools.partial(near_kernel, capacity, slots, grid_width),
+        out_shape=jax.ShapeDtypeStruct((4, rows, 2 * orb_local), BF16),
         scratch_shapes=weights,
         compiler_params=vmem,
-        name="far",
-    )(homes[2], homes[3], table_high, table_low)
-    far = [swap(block, 8 + index, 16, ("slab", "orb")) for index, block in enumerate(far_out)]
-    near_out = pl.pallas_call(
-        functools.partial(near_kernel, capacity, slots, grid_width),
-        out_shape=[jax.ShapeDtypeStruct((rows, orb_local + skip), BF16)] * 8,
-        scratch_shapes=weights + [pltpu.VMEM((taps, skip), BF16)] * 2,
+        name="near",
+    )(home, beside, table_high, table_low)
+    near = trade(near_out)
+    copied_out = pl.pallas_call(
+        functools.partial(copied_kernel, capacity, slots, grid_width),
+        out_shape=jax.ShapeDtypeStruct((4, rows, 2 * skip), BF16),
+        scratch_shapes=weights + [pltpu.VMEM((taps, 2 * skip), BF16)] * 2,
         compiler_params=vmem,
-        name="near",
-    )(homes[0], homes[1], table_high, table_low, mine, other)
-    near = [near_out[0]] + [swap(block, index, 16, ("slab", "orb")) for index, block in enumerate(near_out) if index]
+        name="copied",
+    )(home, beside, mine_late, other, mine_partner, other_partner)
+    copied = trade(copied_out)
     return pl.pallas_call(
-        functools.partial(place_kernel, capacity, skip),
+        functools.partial(place_kernel, capacity, slots, skip),
         out_shape=jax.ShapeDtypeStruct((5, electrons, 4 * orb_local), BF16),
         compiler_params=vmem,
         name="place",
-    )(packed, *near, *far)
+    )(packed, near, copied, *far)
 
 
 def solution(mesh):

time: 101 us -> 109 us (1.079)
  the two profiles are of different devices: /device:TPU:1 before, /device:TPU:10 now
where the time goes in v2:
time: 109 us; the launch traced here: 107 us
  waiting for transfers between devices  47.6 us (44%)
  starting transfers between devices  22.2 us (20%)
  Pallas kernels  20.3 us (19%)
  local copies, waits for them, and re-layouts  16.2 us (15%)
    ppermute x13, waiting for transfers between devices, swap(): return lax.ppermute(array, axes, [(i, i ^ step) for i in range(count)])  47.6 us
    ppermute x13, starting transfers between devices, swap(): return lax.ppermute(array, axes, [(i, i ^ step) for i in range(count)])  13.7 us
    unnamed x26, local copies, waits for them, and re-layouts  10.6 us
    all_to_all x2, starting transfers between devices, trade(): lax.all_to_all(blocks, ('slab', 'orb'), 0, 0, axis_index_groups=members,...  8.52 us
    pallas_call x2, Pallas kernels, far_blocks(): pl.pallas_call(functools.partial(far_kernel, capacity, slots, grid_width,...  5.62 us
    pallas_call x1, Pallas kernels, small_body(): pl.pallas_call(functools.partial(near_kernel, capacity, slots, grid_width...  5.23 us
    pallas_call x1, Pallas kernels, small_body(): pl.pallas_call(functools.partial(copied_kernel, capacity, slots, grid_wid...  3.13 us
    reshape x1, local copies, waits for them, and re-layouts, small_body(): spline_table.reshape(taps, orb_local)  2.95 us
  transfers between devices with their start and end apart: 15, of which 8 were waited for; matrix products, arithmetic and copies ran while one was open for 6% of the time, Pallas kernels for 14%

profile of v2, /device:TPU:10, one launch (start us, length us, event | category | flops | bytes accessed | tf_op | source)
XLA Modules:
  0.0 107.1 jit_solution(12250033664920167962)
XLA Ops:
  0.0 1.4 %pack.1.packed_ref = f32[8,128]{1,0:T(8,128)} custom-call(f32[3,96]{1,0:T(4,128)} %fractions_ref.1, s32[2,96]{1,0:T(2,128)} %cells_ref.1, s32[1,96]{1,0:T(1,128)} %bitcast.7), custom_call_target="tpu_custom_call" | custom-call | tf_op jit(solution)/shard_map/pack/pallas_call | solution.py:314
  1.9 3.3 %collective-permute-done = f32[8,128]{1,0:T(8,128)S(1)} collective-permute-done((f32[8,128]{1,0:T(8,128)}, f32[8,128]{1,0:T(8,128)S(1)}, u32[]{:S(2)}, u32[]{:S(2)}) %collective-permute-start) | collective-permute-done | bytes 4128 | tf_op jit(solution)/shard_map/ppermute | solution.py:290
  5.9 1.0 constant_dynamic-slice_fusion
  6.9 2.7 %collective-permute-start.3 = (f32[512,128]{1,0:T(8,128)S(1)}, f32[512,128]{1,0:T(8,128)S(1)}, u32[]{:S(2)}, u32[]{:S(2)}) collective-permute-start(f32[512,128]{1,0:T(8,128)S(1)} %bitcast.5), channel_id=1, source_target_pairs={{0,8},{4,12},{8,0},{12,4},{1,9},{5,13},{9,1},{13,5},{2,10},{6,14},... | collective-permute-start | bytes 786440 | tf_op jit(solution)/shard_map/ppermute | solution.py:290
  9.9 2.9 %reshape.13.own_ref = f32[1024,512]{1,0:T(8,128)} reshape(f32[1,16,16,4,512]{4,3,2,1,0:T(4,128)} %param.7) | data formatting | bytes 4194304 | tf_op jit(solution)/shard_map/reshape | solution.py:330
  12.8 1.7 %reshape.14.partner_ref = f32[1024,512]{1,0:T(8,128)} reshape(f32[1,16,16,4,512]{4,3,2,1,0:T(4,128)S(1)} %collective-permute-done.2) | data formatting | bytes 4194304 | tf_op jit(solution)/shard_map/reshape | solution.py:330
  14.5 2.8 %split.1 = (bf16[1024,1024]{1,0:T(8,128)(2,1)S(1)}, bf16[1024,1024]{1,0:T(8,128)(2,1)S(1)}) custom-call(f32[1024,512]{1,0:T(8,128)} %reshape.13.own_ref, f32[1024,512]{1,0:T(8,128)} %reshape.14.partner_ref), custom_call_target="tpu_custom_call" | custom-call | tf_op jit(solution)/shard_map/split/pallas_call | solution.py:325
  17.3 3.1 %collective-permute-done.4.homes_ref = f32[2,8,128]{2,1,0:T(8,128)S(1)} collective-permute-done((f32[2,8,128]{2,1,0:T(8,128)S(1)}, f32[2,8,128]{2,1,0:T(8,128)S(1)}, u32[]{:S(2)}, u32[]{:S(2)}) %collective-permute-start.4) | collective-permute-done | bytes 8224 | tf_op jit(solution)/shard_map/ppermute | solution.py:290
  20.5 2.8 %far.2 = (bf16[152,768]{1,0:T(8,128)(2,1)S(1)}, bf16[152,768]{1,0:T(8,128)(2,1)S(1)}) custom-call(f32[2,8,128]{2,1,0:T(8,128)S(1)} %collective-permute-done.4.homes_ref, bf16[1024,1024]{1,0:T(8,128)(2,1)S(1)} %get-tuple-element.13.high_ref, bf16[1024,1024]{1,0:T(8,128)(2,1)S(1)} %get-tuple-element.14.low_ref), custom_call_target="tpu_custom_call" | custom-call | tf_op jit(solution)/shard_map/far/pallas_call | solution.py:333
  24.7 1.5 %collective-permute-start.5 = (f32[512,128]{1,0:T(8,128)S(1)}, f32[512,128]{1,0:T(8,128)S(1)}, u32[]{:S(2)}, u32[]{:S(2)}) collective-permute-start(f32[512,128]{1,0:T(8,128)S(1)} %collective-permute-done.3.refs_0_), channel_id=1, source_target_pairs={{0,16},{16,0},{1,17},{17,1},{2,18},{18,2},{3,19},{19,3},{4,20},{20... | collective-permute-start | bytes 786440 | tf_op jit(solution)/shard_map/ppermute | solution.py:290
  26.2 6.7 %collective-permute-done.5.refs_1_ = f32[512,128]{1,0:T(8,128)S(1)} collective-permute-done((f32[512,128]{1,0:T(8,128)S(1)}, f32[512,128]{1,0:T(8,128)S(1)}, u32[]{:S(2)}, u32[]{:S(2)}) %collective-permute-start.5) | collective-permute-done | bytes 262176 | tf_op jit(solution)/shard_map/ppermute | solution.py:290
  33.2 3.4 %collective-permute-done.1.beside_ref = f32[2,8,128]{2,1,0:T(8,128)S(1)} collective-permute-done((f32[2,8,128]{2,1,0:T(8,128)S(1)}, f32[2,8,128]{2,1,0:T(8,128)S(1)}, u32[]{:S(2)}, u32[]{:S(2)}) %collective-permute-start.1) | collective-permute-done | bytes 8224 | tf_op jit(solution)/shard_map/ppermute | solution.py:290
  36.6 3.1 %copied.1 = bf16[4,152,256]{2,1,0:T(8,128)(2,1)} custom-call(f32[2,8,128]{2,1,0:T(8,128)S(1)} %pad_maximum_fusion.home_ref, f32[2,8,128]{2,1,0:T(8,128)S(1)} %collective-permute-done.1.beside_ref, f32[512,128]{1,0:T(8,128)S(1)} %collective-permute-done.3.refs_0_, f32[512,128]{1,0:T(8,128)S(1)} %collective-permute-done.5.refs_1_, ...), custom_call_target="tpu_custom_call" | custom-call | tf_op jit(solution)/shard_map/copied/pallas_call | solution.py:357
  39.7 4.2 %all-to-all-start.1 = ((bf16[4,152,256]{2,1,0:T(8,128)(2,1)}), bf16[4,152,256]{2,1,0:T(8,128)(2,1)S(1)}, u32[]{:S(2)}, u32[]{:S(2)}) async-start(bf16[4,152,256]{2,1,0:T(8,128)(2,1)} %copied.1), calls=%async_computation.1 | async-start | bytes 622592 | tf_op jit(solution)/shard_map/all_to_all | solution.py:299
  43.9 1.6 %copy-done.1 = bf16[1024,1024]{1,0:T(8,128)(2,1)S(1)} copy-done((bf16[1024,1024]{1,0:T(8,128)(2,1)S(1)}, bf16[1024,1024]{1,0:T(8,128)(2,1)}, u32[]{:S(2)}) %copy-start.1) | copy-done | bytes 2097176
  45.5 5.2 %near.1 = bf16[4,152,1024]{2,1,0:T(8,128)(2,1)S(1)} custom-call(f32[2,8,128]{2,1,0:T(8,128)S(1)} %pad_maximum_fusion.home_ref, f32[2,8,128]{2,1,0:T(8,128)S(1)} %collective-permute-done.1.beside_ref, bf16[1024,1024]{1,0:T(8,128)(2,1)S(1)} %get-tuple-element.13.high_ref, bf16[1024,1024]{1,0:T(8,128)(2,1)S(1)} %copy-done.1), custom_call_target="tpu_custom_call" | custom-call | tf_op jit(solution)/shard_map/near/pallas_call | solution.py:349
  50.7 1.0 copy-done.3
  52.5 4.3 %all-to-all-start = ((bf16[4,152,1024]{2,1,0:T(8,128)(2,1)}), bf16[4,152,1024]{2,1,0:T(8,128)(2,1)S(1)}, u32[]{:S(2)}, u32[]{:S(2)}) async-start(bf16[4,152,1024]{2,1,0:T(8,128)(2,1)} %copy-done.3), calls=%async_computation | async-start | bytes 2490368 | tf_op jit(solution)/shard_map/all_to_all | solution.py:299
  56.8 2.5 %collective-permute-start.10 = (f32[2,8,128]{2,1,0:T(8,128)S(1)}, f32[2,8,128]{2,1,0:T(8,128)S(1)}, u32[]{:S(2)}, u32[]{:S(2)}) collective-permute-start(f32[2,8,128]{2,1,0:T(8,128)S(1)} %pad_maximum_fusion.home_ref), channel_id=1, source_target_pairs={{0,12},{4,8},{8,4},{12,0},{1,13},{5,9},{9,5},{13,1},{2,14},{6,10},... | collective-permute-start | bytes 24584 | tf_op jit(solution)/shard_map/ppermute | solution.py:290
  60.2 1.5 %collective-permute-start.9 = (bf16[152,768]{1,0:T(8,128)(2,1)}, bf16[152,768]{1,0:T(8,128)(2,1)S(1)}, u32[]{:S(2)}, u32[]{:S(2)}) collective-permute-start(bf16[152,768]{1,0:T(8,128)(2,1)} %copy-done.11), channel_id=1, source_target_pairs={{0,10},{1,11},{2,8},{3,9},{4,14},{5,15},{6,12},{7,13},{8,2},{9,3},... | collective-permute-start | bytes 700424 | tf_op jit(solution)/shard_map/ppermute | solution.py:290
  61.7 1.6 %copy-done.2 = bf16[1024,1024]{1,0:T(8,128)(2,1)S(1)} copy-done((bf16[1024,1024]{1,0:T(8,128)(2,1)S(1)}, bf16[1024,1024]{1,0:T(8,128)(2,1)}, u32[]{:S(2)}) %copy-start.2) | copy-done | bytes 2097176
  63.3 2.8 %far.3 = (bf16[152,768]{1,0:T(8,128)(2,1)S(1)}, bf16[152,768]{1,0:T(8,128)(2,1)S(1)}) custom-call(f32[2,8,128]{2,1,0:T(8,128)S(1)} %collective-permute-done.10.homes_ref, bf16[1024,1024]{1,0:T(8,128)(2,1)S(1)} %get-tuple-element.13.high_ref, bf16[1024,1024]{1,0:T(8,128)(2,1)S(1)} %copy-done.2), custom_call_target="tpu_custom_call" | custom-call | tf_op jit(solution)/shard_map/far/pallas_call | solution.py:333
  66.1 1.5 %collective-permute-start.11 = (bf16[152,768]{1,0:T(8,128)(2,1)S(1)}, bf16[152,768]{1,0:T(8,128)(2,1)S(1)}, u32[]{:S(2)}, u32[]{:S(2)}) collective-permute-start(bf16[152,768]{1,0:T(8,128)(2,1)S(1)} %get-tuple-element.19), channel_id=1, source_target_pairs={{0,12},{1,13},{2,14},{3,15},{4,8},{5,9},{6,10},{7,11},{8,4},{9,5},... | collective-permute-start | bytes 700424 | tf_op jit(solution)/shard_map/ppermute | solution.py:290
  67.6 2.0 %collective-permute-start.12 = (bf16[152,768]{1,0:T(8,128)(2,1)S(1)}, bf16[152,768]{1,0:T(8,128)(2,1)S(1)}, u32[]{:S(2)}, u32[]{:S(2)}) collective-permute-start(bf16[152,768]{1,0:T(8,128)(2,1)S(1)} %get-tuple-element.20), channel_id=1, source_target_pairs={{0,14},{1,15},{2,12},{3,13},{4,10},{5,11},{6,8},{7,9},{8,6},{9,7},... | collective-permute-start | bytes 700424 | tf_op jit(solution)/shard_map/ppermute | solution.py:290
  69.6 11.0 %collective-permute-done.8.refs_0_ = bf16[152,768]{1,0:T(8,128)(2,1)S(1)} collective-permute-done((bf16[152,768]{1,0:T(8,128)(2,1)}, bf16[152,768]{1,0:T(8,128)(2,1)S(1)}, u32[]{:S(2)}, u32[]{:S(2)}) %collective-permute-start.8) | collective-permute-done | bytes 233504 | tf_op jit(solution)/shard_map/ppermute | solution.py:290
  81.3 10.5 %collective-permute-done.9.refs_1_ = bf16[152,768]{1,0:T(8,128)(2,1)S(1)} collective-permute-done((bf16[152,768]{1,0:T(8,128)(2,1)}, bf16[152,768]{1,0:T(8,128)(2,1)S(1)}, u32[]{:S(2)}, u32[]{:S(2)}) %collective-permute-start.9) | collective-permute-done | bytes 233504 | tf_op jit(solution)/shard_map/ppermute | solution.py:290
  92.6 7.1 %collective-permute-done.11.refs_2_ = bf16[152,768]{1,0:T(8,128)(2,1)S(1)} collective-permute-done((bf16[152,768]{1,0:T(8,128)(2,1)S(1)}, bf16[152,768]{1,0:T(8,128)(2,1)S(1)}, u32[]{:S(2)}, u32[]{:S(2)}) %collective-permute-start.11) | collective-permute-done | bytes 233504 | tf_op jit(solution)/shard_map/ppermute | solution.py:290
  99.6 2.5 %collective-permute-done.12.refs_3_ = bf16[152,768]{1,0:T(8,128)(2,1)S(1)} collective-permute-done((bf16[152,768]{1,0:T(8,128)(2,1)S(1)}, bf16[152,768]{1,0:T(8,128)(2,1)S(1)}, u32[]{:S(2)}, u32[]{:S(2)}) %collective-permute-start.12) | collective-permute-done | bytes 233504 | tf_op jit(solution)/shard_map/ppermute | solution.py:290
  102.1 1.0 copy-done.5
  103.1 0.9 copy-done.7
  104.0 0.9 copy-done.9
  105.0 2.1 %place.1 = bf16[5,96,2048]{2,1,0:T(8,128)(2,1)} custom-call(f32[8,128]{1,0:T(8,128)S(1)} %copy-done.10, bf16[4,152,1024]{2,1,0:T(8,128)(2,1)S(1)} %all-to-all-done.near_ref, bf16[4,152,256]{2,1,0:T(8,128)(2,1)S(1)} %copy-done.5, bf16[152,768]{1,0:T(8,128)(2,1)S(1)} %copy-done.7, bf16[152,768]{1,0:T(8,128)(2,1)S(1)} %copy-done.9, ...), custom_call_target="tpu_custom_call" | custom-call | tf_op jit(solution)/shard_map/place/pallas_call | solution.py:365
  (35 shorter events, 6.3 us)
Async XLA Ops:
  0.0 12.8 %collective-permute-start.2 = (f32[1,16,16,4,512]{4,3,2,1,0:T(4,128)}, f32[1,16,16,4,512]{4,3,2,1,0:T(4,128)S(1)}, u32[]{:S(2)}, u32[]{:S(2)}) collective-permute-start(f32[1,16,16,4,512]{4,3,2,1,0:T(4,128)} %param.7), channel_id=1, source_target_pairs={{0,1},{1,0},{2,3},{3,2},{4,5},{5,4},{6,7},{7,6},{8,9},{9,8},{10,11... | collective-permute-start | bytes 6291464 | tf_op jit(solution)/shard_map/ppermute | solution.py:290
  1.4 3.8 %collective-permute-start = (f32[8,128]{1,0:T(8,128)}, f32[8,128]{1,0:T(8,128)S(1)}, u32[]{:S(2)}, u32[]{:S(2)}) collective-permute-start(f32[8,128]{1,0:T(8,128)} %pack.1.packed_ref), channel_id=1, source_target_pairs={{0,2},{1,3},{2,0},{3,1},{4,6},{5,7},{6,4},{7,5},{8,10},{9,11},{10,... | collective-permute-start | bytes 12296 | tf_op jit(solution)/shard_map/ppermute | solution.py:290
  6.9 17.8 %collective-permute-start.3 = (f32[512,128]{1,0:T(8,128)S(1)}, f32[512,128]{1,0:T(8,128)S(1)}, u32[]{:S(2)}, u32[]{:S(2)}) collective-permute-start(f32[512,128]{1,0:T(8,128)S(1)} %bitcast.5), channel_id=1, source_target_pairs={{0,8},{4,12},{8,0},{12,4},{1,9},{5,13},{9,1},{13,5},{2,10},{6,14},... | collective-permute-start | bytes 786440 | tf_op jit(solution)/shard_map/ppermute | solution.py:290
  9.5 10.9 %collective-permute-start.4 = (f32[2,8,128]{2,1,0:T(8,128)S(1)}, f32[2,8,128]{2,1,0:T(8,128)S(1)}, u32[]{:S(2)}, u32[]{:S(2)}) collective-permute-start(f32[2,8,128]{2,1,0:T(8,128)S(1)} %pad_maximum_fusion.home_ref), channel_id=1, source_target_pairs={{0,8},{4,12},{8,0},{12,4},{1,9},{5,13},{9,1},{13,5},{2,10},{6,14},... | collective-permute-start | bytes 24584 | tf_op jit(solution)/shard_map/ppermute | solution.py:290
  17.3 5.9 %copy-start = (bf16[1024,1024]{1,0:T(8,128)(2,1)}, bf16[1024,1024]{1,0:T(8,128)(2,1)S(1)}, u32[]{:S(2)}) copy-start(bf16[1024,1024]{1,0:T(8,128)(2,1)S(1)} %get-tuple-element.14.low_ref) | copy-start | bytes 6291460
  23.3 0.7 copy-start.11
  24.0 0.7 copy-start.12
  24.7 8.2 %collective-permute-start.5 = (f32[512,128]{1,0:T(8,128)S(1)}, f32[512,128]{1,0:T(8,128)S(1)}, u32[]{:S(2)}, u32[]{:S(2)}) collective-permute-start(f32[512,128]{1,0:T(8,128)S(1)} %collective-permute-done.3.refs_0_), channel_id=1, source_target_pairs={{0,16},{16,0},{1,17},{17,1},{2,18},{18,2},{3,19},{19,3},{4,20},{20... | collective-permute-start | bytes 786440 | tf_op jit(solution)/shard_map/ppermute | solution.py:290
  26.2 10.4 %collective-permute-start.6 = (f32[512,128]{1,0:T(8,128)S(1)}, f32[512,128]{1,0:T(8,128)S(1)}, u32[]{:S(2)}, u32[]{:S(2)}) collective-permute-start(f32[512,128]{1,0:T(8,128)S(1)} %collective-permute-done.3.refs_0_), channel_id=1, source_target_pairs={{0,1},{1,0},{2,3},{3,2},{4,5},{5,4},{6,7},{7,6},{8,9},{9,8},{10,11... | collective-permute-start | bytes 786440 | tf_op jit(solution)/shard_map/ppermute | solution.py:290
  32.9 3.7 %collective-permute-start.7 = (f32[512,128]{1,0:T(8,128)S(1)}, f32[512,128]{1,0:T(8,128)S(1)}, u32[]{:S(2)}, u32[]{:S(2)}) collective-permute-start(f32[512,128]{1,0:T(8,128)S(1)} %collective-permute-done.5.refs_1_), channel_id=1, source_target_pairs={{0,1},{1,0},{2,3},{3,2},{4,5},{5,4},{6,7},{7,6},{8,9},{9,8},{10,11... | collective-permute-start | bytes 786440 | tf_op jit(solution)/shard_map/ppermute | solution.py:290
  32.9 3.7 %collective-permute-start.1 = (f32[2,8,128]{2,1,0:T(8,128)S(1)}, f32[2,8,128]{2,1,0:T(8,128)S(1)}, u32[]{:S(2)}, u32[]{:S(2)}) collective-permute-start(f32[2,8,128]{2,1,0:T(8,128)S(1)} %pad_maximum_fusion.home_ref), channel_id=1, source_target_pairs={{0,4},{4,0},{8,12},{12,8},{1,5},{5,1},{9,13},{13,9},{2,6},{6,2},{1... | collective-permute-start | bytes 24584 | tf_op jit(solution)/shard_map/ppermute | solution.py:290
  39.7 12.1 %all-to-all-start.1 = ((bf16[4,152,256]{2,1,0:T(8,128)(2,1)}), bf16[4,152,256]{2,1,0:T(8,128)(2,1)S(1)}, u32[]{:S(2)}, u32[]{:S(2)}) async-start(bf16[4,152,256]{2,1,0:T(8,128)(2,1)} %copied.1), calls=%async_computation.1 | async-start | bytes 622592 | tf_op jit(solution)/shard_map/all_to_all | solution.py:299
  43.9 1.6 %copy-start.1 = (bf16[1024,1024]{1,0:T(8,128)(2,1)S(1)}, bf16[1024,1024]{1,0:T(8,128)(2,1)}, u32[]{:S(2)}) copy-start(bf16[1024,1024]{1,0:T(8,128)(2,1)} %copy-done) | copy-start | bytes 6291460
  50.7 1.0 copy-start.3
  51.8 0.7 copy-start.4
  52.5 49.6 %copy-start.10 = (f32[8,128]{1,0:T(8,128)S(1)}, f32[8,128]{1,0:T(8,128)}, u32[]{:S(2)}) copy-start(f32[8,128]{1,0:T(8,128)} %pack.1.packed_ref) | copy-start | bytes 12292
  52.5 49.6 %all-to-all-start = ((bf16[4,152,1024]{2,1,0:T(8,128)(2,1)}), bf16[4,152,1024]{2,1,0:T(8,128)(2,1)S(1)}, u32[]{:S(2)}, u32[]{:S(2)}) async-start(bf16[4,152,1024]{2,1,0:T(8,128)(2,1)} %copy-done.3), calls=%async_computation | async-start | bytes 2490368 | tf_op jit(solution)/shard_map/all_to_all | solution.py:299
  56.8 4.8 %collective-permute-start.10 = (f32[2,8,128]{2,1,0:T(8,128)S(1)}, f32[2,8,128]{2,1,0:T(8,128)S(1)}, u32[]{:S(2)}, u32[]{:S(2)}) collective-permute-start(f32[2,8,128]{2,1,0:T(8,128)S(1)} %pad_maximum_fusion.home_ref), channel_id=1, source_target_pairs={{0,12},{4,8},{8,4},{12,0},{1,13},{5,9},{9,5},{13,1},{2,14},{6,10},... | collective-permute-start | bytes 24584 | tf_op jit(solution)/shard_map/ppermute | solution.py:290
  59.3 21.3 %collective-permute-start.8 = (bf16[152,768]{1,0:T(8,128)(2,1)}, bf16[152,768]{1,0:T(8,128)(2,1)S(1)}, u32[]{:S(2)}, u32[]{:S(2)}) collective-permute-start(bf16[152,768]{1,0:T(8,128)(2,1)} %copy-done.12), channel_id=1, source_target_pairs={{0,8},{1,9},{2,10},{3,11},{4,12},{5,13},{6,14},{7,15},{8,0},{9,1},... | collective-permute-start | bytes 700424 | tf_op jit(solution)/shard_map/ppermute | solution.py:290
  60.2 31.7 %collective-permute-start.9 = (bf16[152,768]{1,0:T(8,128)(2,1)}, bf16[152,768]{1,0:T(8,128)(2,1)S(1)}, u32[]{:S(2)}, u32[]{:S(2)}) collective-permute-start(bf16[152,768]{1,0:T(8,128)(2,1)} %copy-done.11), channel_id=1, source_target_pairs={{0,10},{1,11},{2,8},{3,9},{4,14},{5,15},{6,12},{7,13},{8,2},{9,3},... | collective-permute-start | bytes 700424 | tf_op jit(solution)/shard_map/ppermute | solution.py:290
  61.7 1.6 %copy-start.2 = (bf16[1024,1024]{1,0:T(8,128)(2,1)S(1)}, bf16[1024,1024]{1,0:T(8,128)(2,1)}, u32[]{:S(2)}) copy-start(bf16[1024,1024]{1,0:T(8,128)(2,1)} %copy-done) | copy-start | bytes 6291460
  66.1 33.5 %collective-permute-start.11 = (bf16[152,768]{1,0:T(8,128)(2,1)S(1)}, bf16[152,768]{1,0:T(8,128)(2,1)S(1)}, u32[]{:S(2)}, u32[]{:S(2)}) collective-permute-start(bf16[152,768]{1,0:T(8,128)(2,1)S(1)} %get-tuple-element.19), channel_id=1, source_target_pairs={{0,12},{1,13},{2,14},{3,15},{4,8},{5,9},{6,10},{7,11},{8,4},{9,5},... | collective-permute-start | bytes 700424 | tf_op jit(solution)/shard_map/ppermute | solution.py:290
  67.6 34.5 %collective-permute-start.12 = (bf16[152,768]{1,0:T(8,128)(2,1)S(1)}, bf16[152,768]{1,0:T(8,128)(2,1)S(1)}, u32[]{:S(2)}, u32[]{:S(2)}) collective-permute-start(bf16[152,768]{1,0:T(8,128)(2,1)S(1)} %get-tuple-element.20), channel_id=1, source_target_pairs={{0,14},{1,15},{2,12},{3,13},{4,10},{5,11},{6,8},{7,9},{8,6},{9,7},... | collective-permute-start | bytes 700424 | tf_op jit(solution)/shard_map/ppermute | solution.py:290
  80.6 0.7 copy-start.6
  91.9 0.7 copy-start.8
  102.1 1.0 copy-start.5
  103.1 0.9 copy-start.7
  104.0 0.9 copy-start.9

commit v3 on v0

--- a/solution.py
+++ b/solution.py
@@ -1,33 +1,39 @@
+import functools
+
 import jax
 import jax.numpy as jnp
 from jax import lax
+from jax.experimental import pallas as pl
+from jax.experimental.pallas import tpu as pltpu
 from jax.sharding import PartitionSpec as P
 
-
-def spline_bases(position):
+LANES = 128
+F32 = jnp.float32
+BF16 = jnp.bfloat16
+
+
+def spline_taps(position):
     remain = 1.0 - position
     square = position * position
     frac_cube = square * position
-    values = jnp.stack(
-        [
-            remain * remain * remain / 6.0,
-            (3.0 * frac_cube - 6.0 * square + 4.0) / 6.0,
-            (-3.0 * frac_cube + 3.0 * square + 3.0 * position + 1.0) / 6.0,
-            frac_cube / 6.0,
-        ],
-        axis=-1,
-    )
-    slopes = jnp.stack(
-        [
-            -0.5 * remain * remain,
-            0.5 * (3.0 * square - 4.0 * position),
-            0.5 * (-3.0 * square + 2.0 * position + 1.0),
-            0.5 * square,
-        ],
-        axis=-1,
-    )
-    curves = jnp.stack([remain, 3.0 * position - 2.0, 1.0 - 3.0 * position, position], axis=-1)
-    return (values, slopes, curves)
+    values = (
+        remain * remain * remain / 6.0,
+        (3.0 * frac_cube - 6.0 * square + 4.0) / 6.0,
+        (-3.0 * frac_cube + 3.0 * square + 3.0 * position + 1.0) / 6.0,
+        frac_cube / 6.0,
+    )
+    slopes = (
+        -0.5 * remain * remain,
+        0.5 * (3.0 * square - 4.0 * position),
+        0.5 * (-3.0 * square + 2.0 * position + 1.0),
+        0.5 * square,
+    )
+    curves = (remain, 3.0 * position - 2.0, 1.0 - 3.0 * position, position)
+    return values, slopes, curves
+
+
+def spline_bases(position):
+    return tuple(jnp.stack(taps, axis=-1) for taps in spline_taps(position))
 
 
 def spread_taps(first_cell, taps, grid_width):
@@ -72,11 +78,15 @@
     return result.reshape(5, slot_count, table_flat.shape[1]).astype(jnp.bfloat16)
 
 
-def body(fractions, cell_index, slab_owner, spline_table):
+def slot_capacity(electrons, slab_count):
+    return max(2, (5 * electrons + 4 * slab_count - 1) // (4 * slab_count))
+
+
+def general_body(fractions, cell_index, slab_owner, spline_table):
     slab_count = lax.axis_size("slab")
     orb_count = lax.axis_size("orb")
     electrons = slab_owner.shape[0]
-    capacity = max(2, (5 * electrons + 4 * slab_count - 1) // (4 * slab_count))
+    capacity = slot_capacity(electrons, slab_count)
     grid_width = spline_table.shape[1]
     orb_local = spline_table.shape[4]
     owners = slab_owner[:, 0]
@@ -99,6 +109,232 @@
     return jnp.take(flat_home, slot_place, axis=1)
 
 
+def iota(shape, dim):
+    return lax.broadcasted_iota(jnp.int32, shape, dim)
+
+
+def to_column(row):
+    count = row.shape[1]
+    spread = jnp.broadcast_to(row, (count, count))
+    return jnp.sum(jnp.where(iota((count, count), 0) == iota((count, count), 1), spread, 0.0), axis=1, keepdims=True)
+
+
+def pack_kernel(fractions_ref, cells_ref, owner_ref, packed_ref):
+    electrons = fractions_ref.shape[1]
+    owner = owner_ref[...].astype(F32)
+    same = to_column(owner) == owner
+    before = iota((electrons, electrons), 0) < iota((electrons, electrons), 1)
+    slot = jnp.sum(jnp.where(same & before, 1.0, 0.0), axis=0, keepdims=True)
+    packed_ref[...] = jnp.full(packed_ref.shape, -1.0, F32)
+    packed_ref[0:3, :electrons] = fractions_ref[...]
+    packed_ref[3:5, :electrons] = cells_ref[...].astype(F32)
+    packed_ref[5:6, :electrons] = owner
+    packed_ref[6:7, :electrons] = slot
+
+
+def split_kernel(planes, table_ref, high_ref, low_ref):
+    blocks = high_ref.shape[1] // LANES
+    count = table_ref.shape[0] // (blocks * planes)
+    for block in range(blocks):
+        for plane in range(planes):
+            table = table_ref[pl.ds(block * planes + plane, count, stride=blocks * planes), :]
+            high = table.astype(BF16)
+            rows, lanes = slice(plane * count, (plane + 1) * count), slice(block * LANES, (block + 1) * LANES)
+            high_ref[rows, lanes] = high
+            low_ref[rows, lanes] = (table - high.astype(F32)).astype(BF16)
+
+
+def slot_weights(home, slab, slots, grid_width, high_ref, low_ref):
+    owner, slot = home[5:6, :], home[6:7, :]
+    wanted = jnp.where(owner == slab.astype(F32), slot, -1.0)
+    chosen = iota((slots, LANES), 0).astype(F32) == wanted
+    lane = iota((slots, LANES), 1)
+
+    def field(index):
+        picked = jnp.sum(jnp.where(chosen, home[index : index + 1, :], 0.0), axis=1, keepdims=True)
+        return jnp.broadcast_to(picked, (slots, LANES))
+
+    (x_value, x_slope, x_curve), taps_y, taps_z = (spline_taps(field(dim)) for dim in range(3))
+    first_y, first_z = field(3).astype(jnp.int32), field(4).astype(jnp.int32)
+
+    def pick(offset, kinds):
+        hits = [offset == tap for tap in range(4)]
+        picked = []
+        for taps in kinds:
+            out = jnp.where(hits[3], taps[3], 0.0)
+            for tap in (2, 1, 0):
+                out = jnp.where(hits[tap], taps[tap], out)
+            picked.append(out)
+        return picked
+
+    z_value, z_slope, z_curve = pick(((lane & (grid_width - 1)) - first_z) & (grid_width - 1), taps_z)
+    per_chunk = LANES // grid_width
+    for chunk in range(grid_width // per_chunk):
+        offset_y = (chunk * per_chunk + lane // grid_width - first_y) & (grid_width - 1)
+        y_value, y_slope, y_curve = pick(offset_y, taps_y)
+        plain = y_value * z_value
+        with_y = y_slope * z_value
+        with_z = y_value * z_slope
+        with_both = y_curve * z_value + y_value * z_curve
+        for plane in range(4):
+            weights = (
+                x_value[plane] * plain,
+                x_slope[plane] * plain,
+                x_value[plane] * with_y,
+                x_value[plane] * with_z,
+                x_curve[plane] * plain + x_value[plane] * with_both,
+            )
+            start = plane * grid_width * grid_width + chunk * LANES
+            for k, weight in enumerate(weights):
+                high = weight.astype(BF16)
+                high_ref[k * slots : (k + 1) * slots, start : start + LANES] = high
+                low_ref[k * slots : (k + 1) * slots, start : start + LANES] = (weight - high.astype(F32)).astype(BF16)
+
+
+def contract(weights, table_high, table_low):
+    dot = functools.partial(jnp.dot, preferred_element_type=F32)
+    high, low = weights[0][...], weights[1][...]
+    return dot(high, table_high) + (dot(low, table_high) + dot(high, table_low))
+
+
+def store_slots(out_ref, lanes, result, capacity, slots):
+    for k in range(5):
+        out_ref[k * capacity : k * capacity + slots, lanes] = result[k * slots : (k + 1) * slots].astype(BF16)
+
+
+def serve_kernel(sizes, tables_count, *refs):
+    capacity, slots, grid_width = sizes
+    tables, refs = refs[: 2 * tables_count], refs[2 * tables_count :]
+    weights, sems = refs[-5:-1], refs[-1]
+    count = (len(refs) - 5) * 2 // 5
+    homes_refs, outs, staged = refs[: count // 2], refs[count // 2 : count // 2 + count], refs[count // 2 + count : -5]
+    slab = lax.axis_index("slab")
+    copies = []
+    for index in range(count):
+        pair = weights[2 * (index % 2) : 2 * (index % 2) + 2]
+        slot_weights(homes_refs[index // 2][index % 2], slab, slots, grid_width, *pair)
+        for half in range(tables_count):
+            high_ref, low_ref = tables[2 * half : 2 * half + 2]
+            width = high_ref.shape[1]
+            result = contract(pair, high_ref[...], low_ref[...])
+            store_slots(staged[index], slice(half * width, (half + 1) * width), result, capacity, slots)
+        copy = pltpu.make_async_copy(staged[index], outs[index], sems.at[index])
+        copy.start()
+        copies.append(copy)
+    for copy in copies:
+        copy.wait()
+
+
+def place_kernel(capacity, slots, packed_ref, *refs):
+    pieces, out_ref, landed, placed, sems = refs[:8], refs[8], refs[9:17], refs[17], refs[18]
+    slab, orb = lax.axis_index("slab"), lax.axis_index("orb")
+    arrivals = [pltpu.make_async_copy(piece, buffer, sems.at[index]) for index, (piece, buffer) in enumerate(zip(pieces, landed))]
+    for turn in range(2):
+        for arrival in arrivals[turn::2]:
+            arrival.start()
+    electrons = out_ref.shape[1]
+    width = out_ref.shape[2] // 4
+    owner = to_column(packed_ref[5:6, :electrons])
+    slot = to_column(packed_ref[6:7, :electrons])
+    step = jnp.zeros_like(owner)
+    for index in range(1, 4):
+        step = jnp.where(owner == (slab ^ index).astype(F32), float(index), step)
+    pick = (iota((electrons, 4 * slots), 1).astype(F32) == step * float(slots) + slot).astype(BF16)
+    departures = []
+    for turn in range(2):
+        for arrival in arrivals[turn::2]:
+            arrival.wait()
+        for half in range(2):
+            block = 2 * turn + half
+            lanes = slice(half * width, (half + 1) * width)
+            for k in range(5):
+                rows = slice(k * capacity, k * capacity + slots)
+                stack = jnp.concatenate([buffer[rows, lanes] for buffer in landed[turn::2]], axis=0)
+                placed[block, k] = jnp.dot(pick, stack, preferred_element_type=F32).astype(BF16)
+            start = pl.multiple_of((orb ^ block) * width, LANES)
+            departure = pltpu.make_async_copy(placed.at[block], out_ref.at[:, :, pl.ds(start, width)], sems.at[len(pieces) + block])
+            departure.start()
+            departures.append(departure)
+    for departure in departures:
+        departure.wait()
+
+
+def swap(array, step, count, axes):
+    return lax.ppermute(array, axes, [(i, i ^ step) for i in range(count)])
+
+
+def after(array, *others):
+    return lax.optimization_barrier((array, *others))[0]
+
+
+HBM = pl.BlockSpec(memory_space=pltpu.HBM)
+VMEM = pl.BlockSpec(memory_space=pltpu.VMEM)
+
+
+def small_body(fractions, cell_index, slab_owner, spline_table):
+    electrons = slab_owner.shape[0]
+    grid_width, planes, orb_local = spline_table.shape[1], spline_table.shape[3], spline_table.shape[4]
+    capacity = slot_capacity(electrons, 4)
+    slots = -(-capacity // 16) * 16
+    rows, width = 4 * capacity + slots, 2 * orb_local
+    taps = grid_width * grid_width * planes
+    vmem = pltpu.CompilerParams(vmem_limit_bytes=40 * 1024 * 1024)
+    blocks = functools.partial(jax.ShapeDtypeStruct, dtype=BF16)
+    both_axes = ("slab", "orb")
+
+    partner_table = swap(spline_table, 1, 4, "orb")
+    packed = pl.pallas_call(
+        pack_kernel, out_shape=jax.ShapeDtypeStruct((8, LANES), F32), name="pack"
+    )(fractions, cell_index, slab_owner.reshape(1, electrons))
+    home = jnp.stack([packed, swap(packed, 2, 4, "orb")])
+    across, corner, beside = (swap(home, step, 4, "slab") for step in (2, 3, 1))
+
+    def split(table):
+        view = table.reshape(grid_width * grid_width, planes, orb_local // LANES, LANES)
+        view = view.transpose(0, 2, 1, 3).reshape(taps * orb_local // LANES, LANES)
+        return pl.pallas_call(
+            functools.partial(split_kernel, planes),
+            out_shape=[blocks((taps, orb_local))] * 2,
+            compiler_params=vmem,
+            name="split",
+        )(view)
+
+    tables = split(spline_table) + split(partner_table)
+
+    def serve(name, *homes):
+        count = 2 * len(homes)
+        return pl.pallas_call(
+            functools.partial(serve_kernel, (capacity, slots, grid_width), 2),
+            out_shape=[blocks((rows, width))] * count,
+            in_specs=[VMEM] * (4 + len(homes)),
+            out_specs=[HBM] * count,
+            scratch_shapes=[pltpu.VMEM((rows, width), BF16)] * count
+            + [pltpu.VMEM((5 * slots, taps), BF16)] * 4
+            + [pltpu.SemaphoreType.DMA((count,))],
+            compiler_params=vmem,
+            name=name,
+        )(*tables, *homes)
+
+    def send(step, block):
+        return swap(block, step, 16, both_axes)
+
+    across_out = serve("across", after(across, corner, beside))
+    corner_out = serve("corner", after(corner, *across_out))
+    near_out = serve("near", after(home, *corner_out), beside)
+    far = [send(8 + 2 * index, block) for index, block in enumerate(across_out + corner_out)]
+    near = [near_out[0]] + [send(2 * index, near_out[index]) for index in range(1, 4)]
+    return pl.pallas_call(
+        functools.partial(place_kernel, capacity, slots),
+        out_shape=blocks((5, electrons, 4 * orb_local)),
+        in_specs=[VMEM] + [HBM] * 8,
+        out_specs=HBM,
+        scratch_shapes=[pltpu.VMEM((rows, width), BF16)] * 8
+        + [pltpu.VMEM((4, 5, electrons, orb_local), BF16), pltpu.SemaphoreType.DMA((12,))],
+        compiler_params=vmem,
+        name="place",
+    )(packed, *near, *far)
+
+
 def solution(mesh):
     in_specs = (
         P(None, ("groups", "slab", "orb")),
@@ -107,4 +343,6 @@
         P("slab", None, None, None, "orb"),
     )
     out_specs = P(None, ("groups", "slab", "orb"), None)
+    small = (mesh.shape["groups"], mesh.shape["slab"], mesh.shape["orb"]) == (2, 4, 4)
+    body = small_body if small else general_body
     return jax.shard_map(body, mesh=mesh, in_specs=in_specs, out_specs=out_specs, check_vma=False)

time: 207 us -> 77.9 us (0.38)
  local copies, waits for them, and re-layouts: 66.8 us -> 1.59 us
  blocking collectives: 64 us -> 0 us
  matrix products: 19.6 us -> 0 us
  Pallas kernels: 0 us -> 17.9 us
  other arithmetic: 12.1 us -> 0.69 us
  waiting for transfers between devices: 32.9 us -> 42.1 us
  starting transfers between devices: 9.17 us -> 15.2 us
    all_to_all x1 -> x0, blocking collectives: 57.8 us -> none  [body(): lax.all_to_all(results, 'slab', split_axis=2, concat_axis=2, tiled=True)]
    ppermute x0 -> x12, waiting for transfers between devices: none -> 42.1 us  [swap(): return lax.ppermute(array, axes, [(i, i ^ step) for i in range(count)])]
    all_to_all x2 -> x0, waiting for transfers between devices: 32.9 us -> none  [the longest x1 29.3 us: body(): lax.all_to_all(returned, 'orb', split_axis=1, concat_axis=4, tiled=True)]
    mul x16 -> x0, local copies, waits for them, and re-layouts: 28.2 us -> none  [the longest x4 8.1 us: evaluate(): value_x * deriv_y * value_z]
    dot_general x4 -> x0, matrix products: 19.6 us -> none  [evaluate(): jnp.dot(dense, table_flat, precision=lax.Precision.HIGHEST, preferred_ele...]
    pallas_call x0 -> x7, Pallas kernels: none -> 17.9 us  [the longest x3 12.1 us: serve(): pl.pallas_call(functools.partial(serve_kernel, (capacity, slots, grid_wid...]
    ppermute x0 -> x12, starting transfers between devices: none -> 15.2 us  [swap(): return lax.ppermute(array, axes, [(i, i ^ step) for i in range(count)])]
    while x24 -> x0, local copies, waits for them, and re-layouts: 13.2 us -> none
  transfers between devices with their start and end apart: 2 -> 12, of which waited for: 2 -> 6; matrix products, arithmetic and copies ran while one was open for 1% -> 1% of each run, Pallas kernels for 0% -> 15%
where the time goes in v3:
time: 77.9 us; the launch traced here: 77.7 us
  waiting for transfers between devices  42.1 us (54%)
  Pallas kernels  17.9 us (23%)
  starting transfers between devices  15.2 us (20%)
  local copies, waits for them, and re-layouts  1.59 us (2%)
    ppermute x12, waiting for transfers between devices, swap(): return lax.ppermute(array, axes, [(i, i ^ step) for i in range(count)])  42.1 us
    ppermute x12, starting transfers between devices, swap(): return lax.ppermute(array, axes, [(i, i ^ step) for i in range(count)])  15.2 us
    pallas_call x3, Pallas kernels, serve(): pl.pallas_call(functools.partial(serve_kernel, (capacity, slots, grid_wid...  12.1 us
    pallas_call x1, Pallas kernels, small_body(): pl.pallas_call(functools.partial(place_kernel, capacity, slots), out_shap...  2.53 us
    pallas_call x2, Pallas kernels, split(): pl.pallas_call(functools.partial(split_kernel, planes), out_shape=[blocks...  1.97 us
    unnamed x4, local copies, waits for them, and re-layouts  1.59 us
  transfers between devices with their start and end apart: 12, of which 6 were waited for; matrix products, arithmetic and copies ran while one was open for 1% of the time, Pallas kernels for 15%

profile of v3, /device:TPU:0, one launch (start us, length us, event | category | flops | bytes accessed | tf_op | source)
XLA Modules:
  0.0 77.7 jit_solution(2322879244773859465)
XLA Ops:
  0.0 0.5 collective-permute-start
  0.5 1.4 %pack.1.packed_ref = f32[8,128]{1,0:T(8,128)} custom-call(f32[3,96]{1,0:T(4,128)} %fractions_ref.1, s32[2,96]{1,0:T(2,128)} %cells_ref.1, s32[1,96]{1,0:T(1,128)} %bitcast.17), custom_call_target="tpu_custom_call" | custom-call | tf_op jit(solution)/shard_map/pack/pallas_call | solution.py:286
  1.8 2.5 %collective-permute-start.1 = (f32[8,128]{1,0:T(8,128)}, f32[8,128]{1,0:T(8,128)S(1)}, u32[]{:S(2)}, u32[]{:S(2)}) collective-permute-start(f32[8,128]{1,0:T(8,128)} %pack.1.packed_ref), channel_id=1, source_target_pairs={{0,2},{1,3},{2,0},{3,1},{4,6},{5,7},{6,4},{7,5},{8,10},{9,11},{10,... | collective-permute-start | bytes 12296 | tf_op jit(solution)/shard_map/ppermute | solution.py:263
  4.3 1.8 %collective-permute-done.1 = f32[8,128]{1,0:T(8,128)S(1)} collective-permute-done((f32[8,128]{1,0:T(8,128)}, f32[8,128]{1,0:T(8,128)S(1)}, u32[]{:S(2)}, u32[]{:S(2)}) %collective-permute-start.1) | collective-permute-done | bytes 4128 | tf_op jit(solution)/shard_map/ppermute | solution.py:263
  6.1 0.7 pad_maximum_fusion.refs_4_
  6.8 2.1 %collective-permute-start.4 = (f32[2,8,128]{2,1,0:T(8,128)S(1)}, f32[2,8,128]{2,1,0:T(8,128)S(1)}, u32[]{:S(2)}, u32[]{:S(2)}) collective-permute-start(f32[2,8,128]{2,1,0:T(8,128)S(1)} %pad_maximum_fusion.refs_4_), channel_id=1, source_target_pairs={{0,4},{4,0},{8,12},{12,8},{1,5},{5,1},{9,13},{13,9},{2,6},{6,2},{1... | collective-permute-start | bytes 24584 | tf_op jit(solution)/shard_map/ppermute | solution.py:263
  8.9 2.6 %collective-permute-start.3 = (f32[2,8,128]{2,1,0:T(8,128)S(1)}, f32[2,8,128]{2,1,0:T(8,128)S(1)}, u32[]{:S(2)}, u32[]{:S(2)}) collective-permute-start(f32[2,8,128]{2,1,0:T(8,128)S(1)} %pad_maximum_fusion.refs_4_), channel_id=1, source_target_pairs={{0,8},{4,12},{8,0},{12,4},{1,9},{5,13},{9,1},{13,5},{2,10},{6,14},... | collective-permute-start | bytes 24584 | tf_op jit(solution)/shard_map/ppermute | solution.py:263
  11.5 0.0 collective-permute-start.2
  11.5 1.6 %copy-done = f32[1,16,16,4,512]{4,3,2,1,0:T(4,128)S(1)} copy-done((f32[1,16,16,4,512]{4,3,2,1,0:T(4,128)S(1)}, f32[1,16,16,4,512]{4,3,2,1,0:T(4,128)}, u32[]{:S(2)}) %copy-start) | copy-done | bytes 2097176
  13.1 1.0 %split.2 = (bf16[1024,512]{1,0:T(8,128)(2,1)S(1)}, bf16[1024,512]{1,0:T(8,128)(2,1)S(1)}) custom-call(f32[4096,128]{1,0:T(8,128)S(1)} %bitcast.13), custom_call_target="tpu_custom_call" | custom-call | tf_op jit(solution)/shard_map/split/pallas_call | solution.py:295
  14.1 0.0 collective-permute-done.4.refs_5_
  14.1 0.0 collective-permute-done.3.refs_4_
  14.1 2.9 %collective-permute-done.2.refs_4_ = f32[2,8,128]{2,1,0:T(8,128)S(1)} collective-permute-done((f32[2,8,128]{2,1,0:T(8,128)S(1)}, f32[2,8,128]{2,1,0:T(8,128)S(1)}, u32[]{:S(2)}, u32[]{:S(2)}) %collective-permute-start.2) | collective-permute-done | bytes 8224 | tf_op jit(solution)/shard_map/ppermute | solution.py:263
  17.0 0.0 collective-permute-done
  17.0 1.0 %split.3 = (bf16[1024,512]{1,0:T(8,128)(2,1)S(1)}, bf16[1024,512]{1,0:T(8,128)(2,1)S(1)}) custom-call(f32[4096,128]{1,0:T(8,128)S(1)} %bitcast.14), custom_call_target="tpu_custom_call" | custom-call | tf_op jit(solution)/shard_map/split/pallas_call | solution.py:295
  18.0 3.2 %across.1 = (bf16[152,1024]{1,0:T(8,128)(2,1)S(1)}, bf16[152,1024]{1,0:T(8,128)(2,1)S(1)}) custom-call(bf16[1024,512]{1,0:T(8,128)(2,1)S(1)} %get-tuple-element.20.refs_0_, bf16[1024,512]{1,0:T(8,128)(2,1)S(1)} %get-tuple-element.21.refs_1_, bf16[1024,512]{1,0:T(8,128)(2,1)S(1)} %get-tuple-element.22.refs_2_, ...), custom_call_target="tpu_custom_call" | custom-call | tf_op jit(solution)/shard_map/across/pallas_call | solution.py:306
  21.1 0.1 collective-permute-start.8
  21.2 3.8 %collective-permute-start.9 = (bf16[152,1024]{1,0:T(8,128)(2,1)S(1)}, bf16[152,1024]{1,0:T(8,128)(2,1)S(1)}, u32[]{:S(2)}, u32[]{:S(2)}) collective-permute-start(bf16[152,1024]{1,0:T(8,128)(2,1)S(1)} %get-tuple-element.26), channel_id=1, source_target_pairs={{0,10},{1,11},{2,8},{3,9},{4,14},{5,15},{6,12},{7,13},{8,2},{9,3},... | collective-permute-start | bytes 933896 | tf_op jit(solution)/shard_map/ppermute | solution.py:263
  25.0 3.0 %corner.1 = (bf16[152,1024]{1,0:T(8,128)(2,1)S(1)}, bf16[152,1024]{1,0:T(8,128)(2,1)S(1)}) custom-call(bf16[1024,512]{1,0:T(8,128)(2,1)S(1)} %get-tuple-element.20.refs_0_, bf16[1024,512]{1,0:T(8,128)(2,1)S(1)} %get-tuple-element.21.refs_1_, bf16[1024,512]{1,0:T(8,128)(2,1)S(1)} %get-tuple-element.22.refs_2_, ...), custom_call_target="tpu_custom_call" | custom-call | tf_op jit(solution)/shard_map/corner/pallas_call | solution.py:306
  28.0 1.1 %collective-permute-start.10 = (bf16[152,1024]{1,0:T(8,128)(2,1)S(1)}, bf16[152,1024]{1,0:T(8,128)(2,1)S(1)}, u32[]{:S(2)}, u32[]{:S(2)}) collective-permute-start(bf16[152,1024]{1,0:T(8,128)(2,1)S(1)} %get-tuple-element.28), channel_id=1, source_target_pairs={{0,12},{1,13},{2,14},{3,15},{4,8},{5,9},{6,10},{7,11},{8,4},{9,5},... | collective-permute-start | bytes 933896 | tf_op jit(solution)/shard_map/ppermute | solution.py:263
  29.1 5.9 %near.1 = (bf16[152,1024]{1,0:T(8,128)(2,1)S(1)}, bf16[152,1024]{1,0:T(8,128)(2,1)S(1)}, bf16[152,1024]{1,0:T(8,128)(2,1)S(1)}, bf16[152,1024]{1,0:T(8,128)(2,1)S(1)}) custom-call(bf16[1024,512]{1,0:T(8,128)(2,1)S(1)} %get-tuple-element.20.refs_0_, bf16[1024,512]{1,0:T(8,128)(2,1)S(1)} %get-tuple-element.21.refs_1_, ...), custom_call_target="tpu_custom_call" | custom-call | tf_op jit(solution)/shard_map/near/pallas_call | solution.py:306
  35.0 0.6 collective-permute-start.5
  35.6 0.0 collective-permute-start.6
  35.6 12.8 %collective-permute-done.8.refs_4_ = bf16[152,1024]{1,0:T(8,128)(2,1)S(1)} collective-permute-done((bf16[152,1024]{1,0:T(8,128)(2,1)S(1)}, bf16[152,1024]{1,0:T(8,128)(2,1)S(1)}, u32[]{:S(2)}, u32[]{:S(2)}) %collective-permute-start.8) | collective-permute-done | bytes 311328 | tf_op jit(solution)/shard_map/ppermute | solution.py:263
  48.4 0.0 collective-permute-start.7
  48.4 7.5 %collective-permute-done.9.refs_5_ = bf16[152,1024]{1,0:T(8,128)(2,1)S(1)} collective-permute-done((bf16[152,1024]{1,0:T(8,128)(2,1)S(1)}, bf16[152,1024]{1,0:T(8,128)(2,1)S(1)}, u32[]{:S(2)}, u32[]{:S(2)}) %collective-permute-start.9) | collective-permute-done | bytes 311328 | tf_op jit(solution)/shard_map/ppermute | solution.py:263
  56.0 1.9 %collective-permute-start.11 = (bf16[152,1024]{1,0:T(8,128)(2,1)S(1)}, bf16[152,1024]{1,0:T(8,128)(2,1)S(1)}, u32[]{:S(2)}, u32[]{:S(2)}) collective-permute-start(bf16[152,1024]{1,0:T(8,128)(2,1)S(1)} %get-tuple-element.29), channel_id=1, source_target_pairs={{0,14},{1,15},{2,12},{3,13},{4,10},{5,11},{6,8},{7,9},{8,6},{9,7},... | collective-permute-start | bytes 933896 | tf_op jit(solution)/shard_map/ppermute | solution.py:263
  57.9 0.0 collective-permute-done.5.refs_1_
  57.9 10.5 %collective-permute-done.6.refs_2_ = bf16[152,1024]{1,0:T(8,128)(2,1)S(1)} collective-permute-done((bf16[152,1024]{1,0:T(8,128)(2,1)S(1)}, bf16[152,1024]{1,0:T(8,128)(2,1)S(1)}, u32[]{:S(2)}, u32[]{:S(2)}) %collective-permute-start.6) | collective-permute-done | bytes 311328 | tf_op jit(solution)/shard_map/ppermute | solution.py:263
  68.4 6.6 %collective-permute-done.7.refs_3_ = bf16[152,1024]{1,0:T(8,128)(2,1)S(1)} collective-permute-done((bf16[152,1024]{1,0:T(8,128)(2,1)S(1)}, bf16[152,1024]{1,0:T(8,128)(2,1)S(1)}, u32[]{:S(2)}, u32[]{:S(2)}) %collective-permute-start.7) | collective-permute-done | bytes 311328 | tf_op jit(solution)/shard_map/ppermute | solution.py:263
  75.0 0.0 collective-permute-done.11.refs_7_
  75.0 2.5 %place.1 = bf16[5,96,2048]{2,1,0:T(8,128)(2,1)} custom-call(f32[8,128]{1,0:T(8,128)S(1)} %copy-done.1, bf16[152,1024]{1,0:T(8,128)(2,1)S(1)} %get-tuple-element.31.refs_0_, bf16[152,1024]{1,0:T(8,128)(2,1)S(1)} %collective-permute-done.5.refs_1_, bf16[152,1024]{1,0:T(8,128)(2,1)S(1)} %collective-permute-done.6.refs_2_, ...), custom_call_target="tpu_custom_call" | custom-call | tf_op jit(solution)/shard_map/place/pallas_call | solution.py:326
  (4 shorter events, 0.0 us)
Async XLA Ops:
  0.0 17.0 %collective-permute-start = (f32[1,16,16,4,512]{4,3,2,1,0:T(4,128)}, f32[1,16,16,4,512]{4,3,2,1,0:T(4,128)S(1)}, u32[]{:S(2)}, u32[]{:S(2)}) collective-permute-start(f32[1,16,16,4,512]{4,3,2,1,0:T(4,128)} %param.7), channel_id=1, source_target_pairs={{0,1},{1,0},{2,3},{3,2},{4,5},{5,4},{6,7},{7,6},{8,9},{9,8},{10,11... | collective-permute-start | bytes 6291464 | tf_op jit(solution)/shard_map/ppermute | solution.py:263
  1.8 4.3 %collective-permute-start.1 = (f32[8,128]{1,0:T(8,128)}, f32[8,128]{1,0:T(8,128)S(1)}, u32[]{:S(2)}, u32[]{:S(2)}) collective-permute-start(f32[8,128]{1,0:T(8,128)} %pack.1.packed_ref), channel_id=1, source_target_pairs={{0,2},{1,3},{2,0},{3,1},{4,6},{5,7},{6,4},{7,5},{8,10},{9,11},{10,... | collective-permute-start | bytes 12296 | tf_op jit(solution)/shard_map/ppermute | solution.py:263
  6.8 7.3 %collective-permute-start.4 = (f32[2,8,128]{2,1,0:T(8,128)S(1)}, f32[2,8,128]{2,1,0:T(8,128)S(1)}, u32[]{:S(2)}, u32[]{:S(2)}) collective-permute-start(f32[2,8,128]{2,1,0:T(8,128)S(1)} %pad_maximum_fusion.refs_4_), channel_id=1, source_target_pairs={{0,4},{4,0},{8,12},{12,8},{1,5},{5,1},{9,13},{13,9},{2,6},{6,2},{1... | collective-permute-start | bytes 24584 | tf_op jit(solution)/shard_map/ppermute | solution.py:263
  8.9 5.2 %collective-permute-start.3 = (f32[2,8,128]{2,1,0:T(8,128)S(1)}, f32[2,8,128]{2,1,0:T(8,128)S(1)}, u32[]{:S(2)}, u32[]{:S(2)}) collective-permute-start(f32[2,8,128]{2,1,0:T(8,128)S(1)} %pad_maximum_fusion.refs_4_), channel_id=1, source_target_pairs={{0,8},{4,12},{8,0},{12,4},{1,9},{5,13},{9,1},{13,5},{2,10},{6,14},... | collective-permute-start | bytes 24584 | tf_op jit(solution)/shard_map/ppermute | solution.py:263
  11.5 5.4 %collective-permute-start.2 = (f32[2,8,128]{2,1,0:T(8,128)S(1)}, f32[2,8,128]{2,1,0:T(8,128)S(1)}, u32[]{:S(2)}, u32[]{:S(2)}) collective-permute-start(f32[2,8,128]{2,1,0:T(8,128)S(1)} %pad_maximum_fusion.refs_4_), channel_id=1, source_target_pairs={{0,12},{4,8},{8,4},{12,0},{1,13},{5,9},{9,5},{13,1},{2,14},{6,10},... | collective-permute-start | bytes 24584 | tf_op jit(solution)/shard_map/ppermute | solution.py:263
  11.5 1.6 %copy-start = (f32[1,16,16,4,512]{4,3,2,1,0:T(4,128)S(1)}, f32[1,16,16,4,512]{4,3,2,1,0:T(4,128)}, u32[]{:S(2)}) copy-start(f32[1,16,16,4,512]{4,3,2,1,0:T(4,128)} %param.7) | copy-start | bytes 6291460
  21.1 27.3 %collective-permute-start.8 = (bf16[152,1024]{1,0:T(8,128)(2,1)S(1)}, bf16[152,1024]{1,0:T(8,128)(2,1)S(1)}, u32[]{:S(2)}, u32[]{:S(2)}) collective-permute-start(bf16[152,1024]{1,0:T(8,128)(2,1)S(1)} %get-tuple-element.25), channel_id=1, source_target_pairs={{0,8},{1,9},{2,10},{3,11},{4,12},{5,13},{6,14},{7,15},{8,0},{9,1},... | collective-permute-start | bytes 933896 | tf_op jit(solution)/shard_map/ppermute | solution.py:263
  21.2 34.8 %collective-permute-start.9 = (bf16[152,1024]{1,0:T(8,128)(2,1)S(1)}, bf16[152,1024]{1,0:T(8,128)(2,1)S(1)}, u32[]{:S(2)}, u32[]{:S(2)}) collective-permute-start(bf16[152,1024]{1,0:T(8,128)(2,1)S(1)} %get-tuple-element.26), channel_id=1, source_target_pairs={{0,10},{1,11},{2,8},{3,9},{4,14},{5,15},{6,12},{7,13},{8,2},{9,3},... | collective-permute-start | bytes 933896 | tf_op jit(solution)/shard_map/ppermute | solution.py:263
  28.0 47.0 %collective-permute-start.10 = (bf16[152,1024]{1,0:T(8,128)(2,1)S(1)}, bf16[152,1024]{1,0:T(8,128)(2,1)S(1)}, u32[]{:S(2)}, u32[]{:S(2)}) collective-permute-start(bf16[152,1024]{1,0:T(8,128)(2,1)S(1)} %get-tuple-element.28), channel_id=1, source_target_pairs={{0,12},{1,13},{2,14},{3,15},{4,8},{5,9},{6,10},{7,11},{8,4},{9,5},... | collective-permute-start | bytes 933896 | tf_op jit(solution)/shard_map/ppermute | solution.py:263
  29.1 46.0 %copy-start.1 = (f32[8,128]{1,0:T(8,128)S(1)}, f32[8,128]{1,0:T(8,128)}, u32[]{:S(2)}) copy-start(f32[8,128]{1,0:T(8,128)} %pack.1.packed_ref) | copy-start | bytes 12292
  35.0 22.9 %collective-permute-start.5 = (bf16[152,1024]{1,0:T(8,128)(2,1)S(1)}, bf16[152,1024]{1,0:T(8,128)(2,1)S(1)}, u32[]{:S(2)}, u32[]{:S(2)}) collective-permute-start(bf16[152,1024]{1,0:T(8,128)(2,1)S(1)} %get-tuple-element.32), channel_id=1, source_target_pairs={{0,2},{1,3},{2,0},{3,1},{4,6},{5,7},{6,4},{7,5},{8,10},{9,11},{10,... | collective-permute-start | bytes 933896 | tf_op jit(solution)/shard_map/ppermute | solution.py:263
  35.6 32.8 %collective-permute-start.6 = (bf16[152,1024]{1,0:T(8,128)(2,1)S(1)}, bf16[152,1024]{1,0:T(8,128)(2,1)S(1)}, u32[]{:S(2)}, u32[]{:S(2)}) collective-permute-start(bf16[152,1024]{1,0:T(8,128)(2,1)S(1)} %get-tuple-element.33), channel_id=1, source_target_pairs={{0,4},{1,5},{2,6},{3,7},{4,0},{5,1},{6,2},{7,3},{8,12},{9,13},{10,... | collective-permute-start | bytes 933896 | tf_op jit(solution)/shard_map/ppermute | solution.py:263
  48.4 26.6 %collective-permute-start.7 = (bf16[152,1024]{1,0:T(8,128)(2,1)S(1)}, bf16[152,1024]{1,0:T(8,128)(2,1)S(1)}, u32[]{:S(2)}, u32[]{:S(2)}) collective-permute-start(bf16[152,1024]{1,0:T(8,128)(2,1)S(1)} %get-tuple-element.34), channel_id=1, source_target_pairs={{0,6},{1,7},{2,4},{3,5},{4,2},{5,3},{6,0},{7,1},{8,14},{9,15},{10,... | collective-permute-start | bytes 933896 | tf_op jit(solution)/shard_map/ppermute | solution.py:263
  56.0 19.1 %collective-permute-start.11 = (bf16[152,1024]{1,0:T(8,128)(2,1)S(1)}, bf16[152,1024]{1,0:T(8,128)(2,1)S(1)}, u32[]{:S(2)}, u32[]{:S(2)}) collective-permute-start(bf16[152,1024]{1,0:T(8,128)(2,1)S(1)} %get-tuple-element.29), channel_id=1, source_target_pairs={{0,14},{1,15},{2,12},{3,13},{4,10},{5,11},{6,8},{7,9},{8,6},{9,7},... | collective-permute-start | bytes 933896 | tf_op jit(solution)/shard_map/ppermute | solution.py:263

commit v4 on v3

--- a/solution.py
+++ b/solution.py
@@ -132,16 +132,27 @@
     packed_ref[6:7, :electrons] = slot
 
 
-def split_kernel(planes, table_ref, high_ref, low_ref):
+def split_kernel(planes, table_ref, high_ref, low_ref, landed, sems):
     blocks = high_ref.shape[1] // LANES
-    count = table_ref.shape[0] // (blocks * planes)
-    for block in range(blocks):
-        for plane in range(planes):
-            table = table_ref[pl.ds(block * planes + plane, count, stride=blocks * planes), :]
-            high = table.astype(BF16)
-            rows, lanes = slice(plane * count, (plane + 1) * count), slice(block * LANES, (block + 1) * LANES)
-            high_ref[rows, lanes] = high
-            low_ref[rows, lanes] = (table - high.astype(F32)).astype(BF16)
+    pieces = sems.shape[0]
+    piece = table_ref.shape[0] // pieces
+    count = piece // (blocks * planes)
+    copies = []
+    for index in range(pieces):
+        span = slice(index * piece, (index + 1) * piece)
+        copies.append(pltpu.make_async_copy(table_ref.at[span, :], landed.at[span, :], sems.at[index]))
+        copies[-1].start()
+    for index in range(pieces):
+        copies[index].wait()
+        for block in range(blocks):
+            lanes = slice(block * LANES, (block + 1) * LANES)
+            for plane in range(planes):
+                first = index * piece + block * planes + plane
+                table = landed[pl.ds(first, count, stride=blocks * planes), :]
+                high = table.astype(BF16)
+                start = (plane * pieces + index) * count
+                high_ref[start : start + count, lanes] = high
+                low_ref[start : start + count, lanes] = (table - high.astype(F32)).astype(BF16)
 
 
 def slot_weights(home, slab, slots, grid_width, high_ref, low_ref):
@@ -202,18 +213,18 @@
         out_ref[k * capacity : k * capacity + slots, lanes] = result[k * slots : (k + 1) * slots].astype(BF16)
 
 
-def serve_kernel(sizes, tables_count, *refs):
+def serve_kernel(sizes, places, *refs):
     capacity, slots, grid_width = sizes
-    tables, refs = refs[: 2 * tables_count], refs[2 * tables_count :]
+    count = len(places)
     weights, sems = refs[-5:-1], refs[-1]
-    count = (len(refs) - 5) * 2 // 5
-    homes_refs, outs, staged = refs[: count // 2], refs[count // 2 : count // 2 + count], refs[count // 2 + count : -5]
+    tables, homes_refs, outs, staged = refs[:4], refs[4 : -5 - 2 * count], refs[-5 - 2 * count : -5 - count], refs[-5 - count : -5]
     slab = lax.axis_index("slab")
     copies = []
     for index in range(count):
         pair = weights[2 * (index % 2) : 2 * (index % 2) + 2]
-        slot_weights(homes_refs[index // 2][index % 2], slab, slots, grid_width, *pair)
-        for half in range(tables_count):
+        which, place = places[index]
+        slot_weights(homes_refs[which][place], slab, slots, grid_width, *pair)
+        for half in range(2):
             high_ref, low_ref = tables[2 * half : 2 * half + 2]
             width = high_ref.shape[1]
             result = contract(pair, high_ref[...], low_ref[...])
@@ -225,13 +236,12 @@
         copy.wait()
 
 
-def place_kernel(capacity, slots, packed_ref, *refs):
-    pieces, out_ref, landed, placed, sems = refs[:8], refs[8], refs[9:17], refs[17], refs[18]
+def place_kernel(capacity, slots, turn, packed_ref, *refs):
+    pieces, (out_ref, placed, sems), landed = refs[:4], (refs[-7], *refs[-2:]), refs[-6:-2]
     slab, orb = lax.axis_index("slab"), lax.axis_index("orb")
     arrivals = [pltpu.make_async_copy(piece, buffer, sems.at[index]) for index, (piece, buffer) in enumerate(zip(pieces, landed))]
-    for turn in range(2):
-        for arrival in arrivals[turn::2]:
-            arrival.start()
+    for arrival in arrivals:
+        arrival.start()
     electrons = out_ref.shape[1]
     width = out_ref.shape[2] // 4
     owner = to_column(packed_ref[5:6, :electrons])
@@ -240,21 +250,19 @@
     for index in range(1, 4):
         step = jnp.where(owner == (slab ^ index).astype(F32), float(index), step)
     pick = (iota((electrons, 4 * slots), 1).astype(F32) == step * float(slots) + slot).astype(BF16)
+    for arrival in arrivals:
+        arrival.wait()
     departures = []
-    for turn in range(2):
-        for arrival in arrivals[turn::2]:
-            arrival.wait()
-        for half in range(2):
-            block = 2 * turn + half
-            lanes = slice(half * width, (half + 1) * width)
-            for k in range(5):
-                rows = slice(k * capacity, k * capacity + slots)
-                stack = jnp.concatenate([buffer[rows, lanes] for buffer in landed[turn::2]], axis=0)
-                placed[block, k] = jnp.dot(pick, stack, preferred_element_type=F32).astype(BF16)
-            start = pl.multiple_of((orb ^ block) * width, LANES)
-            departure = pltpu.make_async_copy(placed.at[block], out_ref.at[:, :, pl.ds(start, width)], sems.at[len(pieces) + block])
-            departure.start()
-            departures.append(departure)
+    for half in range(2):
+        lanes = slice(half * width, (half + 1) * width)
+        for k in range(5):
+            rows = slice(k * capacity, k * capacity + slots)
+            stack = jnp.concatenate([buffer[rows, lanes] for buffer in landed], axis=0)
+            placed[half, k] = jnp.dot(pick, stack, preferred_element_type=F32).astype(BF16)
+        start = pl.multiple_of((orb ^ (2 * turn + half)) * width, LANES)
+        departure = pltpu.make_async_copy(placed.at[half], out_ref.at[:, :, pl.ds(start, width)], sems.at[4 + half])
+        departure.start()
+        departures.append(departure)
     for departure in departures:
         departure.wait()
 
@@ -286,25 +294,29 @@
     packed = pl.pallas_call(
         pack_kernel, out_shape=jax.ShapeDtypeStruct((8, LANES), F32), name="pack"
     )(fractions, cell_index, slab_owner.reshape(1, electrons))
-    home = jnp.stack([packed, swap(packed, 2, 4, "orb")])
-    across, corner, beside = (swap(home, step, 4, "slab") for step in (2, 3, 1))
-
     def split(table):
         view = table.reshape(grid_width * grid_width, planes, orb_local // LANES, LANES)
         view = view.transpose(0, 2, 1, 3).reshape(taps * orb_local // LANES, LANES)
         return pl.pallas_call(
             functools.partial(split_kernel, planes),
             out_shape=[blocks((taps, orb_local))] * 2,
+            in_specs=[HBM],
+            scratch_shapes=[pltpu.VMEM(view.shape, F32), pltpu.SemaphoreType.DMA((8,))],
             compiler_params=vmem,
             name="split",
         )(view)
 
+    along = [packed] + [swap(packed, step, 4, "slab") for step in (1, 2, 3)]
     tables = split(spline_table) + split(partner_table)
-
-    def serve(name, *homes):
-        count = 2 * len(homes)
+    straight = jnp.stack([after(packed, *tables)] + along[1:])
+    crossed = swap(straight, 2, 4, "orb")
+
+    first = after(along[2], along[1], along[3])
+
+    def serve(name, homes, *places):
+        count = len(places)
         return pl.pallas_call(
-            functools.partial(serve_kernel, (capacity, slots, grid_width), 2),
+            functools.partial(serve_kernel, (capacity, slots, grid_width), places),
             out_shape=[blocks((rows, width))] * count,
             in_specs=[VMEM] * (4 + len(homes)),
             out_specs=[HBM] * count,
@@ -318,21 +330,29 @@
     def send(step, block):
         return swap(block, step, 16, both_axes)
 
-    across_out = serve("across", after(across, corner, beside))
-    corner_out = serve("corner", after(corner, *across_out))
-    near_out = serve("near", after(home, *corner_out), beside)
+    across_out = serve("across", [first[None]], (0, 0))
+    across_out += serve("across", [after(crossed, *across_out)], (0, 2))
+    both = (after(straight, *across_out), crossed)
+    corner_out = serve("corner", both, (0, 3), (1, 3))
+    both = (after(straight, *corner_out), crossed)
+    near_out = serve("near", both, (0, 0), (1, 0), (0, 1), (1, 1))
     far = [send(8 + 2 * index, block) for index, block in enumerate(across_out + corner_out)]
     near = [near_out[0]] + [send(2 * index, near_out[index]) for index in range(1, 4)]
-    return pl.pallas_call(
-        functools.partial(place_kernel, capacity, slots),
-        out_shape=blocks((5, electrons, 4 * orb_local)),
-        in_specs=[VMEM] + [HBM] * 8,
-        out_specs=HBM,
-        scratch_shapes=[pltpu.VMEM((rows, width), BF16)] * 8
-        + [pltpu.VMEM((4, 5, electrons, orb_local), BF16), pltpu.SemaphoreType.DMA((12,))],
-        compiler_params=vmem,
-        name="place",
-    )(packed, *near, *far)
+    out = ()
+    for turn in range(2):
+        pieces = near[turn::2] + far[turn::2]
+        out = pl.pallas_call(
+            functools.partial(place_kernel, capacity, slots, turn),
+            out_shape=[blocks((5, electrons, 4 * orb_local))],
+            in_specs=[VMEM] + [HBM] * (4 + len(out)),
+            out_specs=[HBM],
+            input_output_aliases={5: 0} if out else {},
+            scratch_shapes=[pltpu.VMEM((rows, width), BF16)] * 4
+            + [pltpu.VMEM((2, 5, electrons, orb_local), BF16), pltpu.SemaphoreType.DMA((6,))],
+            compiler_params=vmem,
+            name="place",
+        )(packed, *pieces, *out)
+    return out[0]
 
 
 def solution(mesh):

time: 77.9 us -> 71.6 us (0.919)
  the two profiles are of different devices: /device:TPU:0 before, /device:TPU:10 now
where the time goes in v4:
time: 71.6 us; the launch traced here: 70.5 us
  waiting for transfers between devices  29.3 us (41%)
  starting transfers between devices  20.5 us (29%)
  Pallas kernels  18.9 us (26%)
  local copies, waits for them, and re-layouts  1.59 us (2%)
    ppermute x12, waiting for transfers between devices, swap(): return lax.ppermute(array, axes, [(i, i ^ step) for i in range(count)])  29.3 us
    ppermute x12, starting transfers between devices, swap(): return lax.ppermute(array, axes, [(i, i ^ step) for i in range(count)])  20.5 us
    pallas_call x4, Pallas kernels, serve(): pl.pallas_call(functools.partial(serve_kernel, (capacity, slots, grid_wid...  11.9 us
    pallas_call x2, Pallas kernels, small_body(): pl.pallas_call(functools.partial(place_kernel, capacity, slots, turn), ou...  3.42 us
    pallas_call x2, Pallas kernels, split(): pl.pallas_call(functools.partial(split_kernel, planes), out_shape=[blocks...  2.15 us
    unnamed x4, local copies, waits for them, and re-layouts  1.59 us
  transfers between devices with their start and end apart: 12, of which 3 were waited for; matrix products, arithmetic and copies ran while one was open for 0% of the time, Pallas kernels for 24%

profile of v4, /device:TPU:10, one launch (start us, length us, event | category | flops | bytes accessed | tf_op | source)
XLA Modules:
  0.0 70.5 jit_solution(16812933010311995642)
XLA Ops:
  0.0 0.0 collective-permute-start
  0.0 1.4 %pack.1.packed_ref = f32[8,128]{1,0:T(8,128)} custom-call(f32[3,96]{1,0:T(4,128)} %fractions_ref.1, s32[2,96]{1,0:T(2,128)} %cells_ref.1, s32[1,96]{1,0:T(1,128)} %bitcast.23), custom_call_target="tpu_custom_call" | custom-call | tf_op jit(solution)/shard_map/pack/pallas_call | solution.py:294
  1.4 1.6 %collective-permute-start.3 = (f32[8,128]{1,0:T(8,128)}, f32[8,128]{1,0:T(8,128)S(1)}, u32[]{:S(2)}, u32[]{:S(2)}) collective-permute-start(f32[8,128]{1,0:T(8,128)} %pack.1.packed_ref), channel_id=1, source_target_pairs={{0,12},{4,8},{8,4},{12,0},{1,13},{5,9},{9,5},{13,1},{2,14},{6,10},... | collective-permute-start | bytes 12296 | tf_op jit(solution)/shard_map/ppermute | solution.py:271
  3.0 1.2 %collective-permute-start.2 = (f32[8,128]{1,0:T(8,128)}, f32[8,128]{1,0:T(8,128)S(1)}, u32[]{:S(2)}, u32[]{:S(2)}) collective-permute-start(f32[8,128]{1,0:T(8,128)} %pack.1.packed_ref), channel_id=1, source_target_pairs={{0,8},{4,12},{8,0},{12,4},{1,9},{5,13},{9,1},{13,5},{2,10},{6,14},... | collective-permute-start | bytes 12296 | tf_op jit(solution)/shard_map/ppermute | solution.py:271
  4.2 1.2 %collective-permute-start.1 = (f32[8,128]{1,0:T(8,128)}, f32[8,128]{1,0:T(8,128)S(1)}, u32[]{:S(2)}, u32[]{:S(2)}) collective-permute-start(f32[8,128]{1,0:T(8,128)} %pack.1.packed_ref), channel_id=1, source_target_pairs={{0,4},{4,0},{8,12},{12,8},{1,5},{5,1},{9,13},{13,9},{2,6},{6,2},{1... | collective-permute-start | bytes 12296 | tf_op jit(solution)/shard_map/ppermute | solution.py:271
  5.5 1.6 %copy-done = f32[1,16,16,4,512]{4,3,2,1,0:T(4,128)S(1)} copy-done((f32[1,16,16,4,512]{4,3,2,1,0:T(4,128)S(1)}, f32[1,16,16,4,512]{4,3,2,1,0:T(4,128)}, u32[]{:S(2)}) %copy-start) | copy-done | bytes 2097176
  7.0 1.1 %split.2 = (bf16[1024,512]{1,0:T(8,128)(2,1)S(1)}, bf16[1024,512]{1,0:T(8,128)(2,1)S(1)}) custom-call(f32[4096,128]{1,0:T(8,128)S(1)} %bitcast.16), custom_call_target="tpu_custom_call" | custom-call | tf_op jit(solution)/shard_map/split/pallas_call | solution.py:300
  8.1 0.0 collective-permute-done
  8.1 1.1 %split.3 = (bf16[1024,512]{1,0:T(8,128)(2,1)S(1)}, bf16[1024,512]{1,0:T(8,128)(2,1)S(1)}) custom-call(f32[4096,128]{1,0:T(8,128)S(1)} %bitcast.17), custom_call_target="tpu_custom_call" | custom-call | tf_op jit(solution)/shard_map/split/pallas_call | solution.py:300
  9.2 0.0 collective-permute-done.3
  9.2 0.0 collective-permute-done.2
  9.2 0.0 collective-permute-done.1
  9.3 0.6 collective-permute-start.4
  9.9 1.5 %across.2 = bf16[152,1024]{1,0:T(8,128)(2,1)S(1)} custom-call(bf16[1024,512]{1,0:T(8,128)(2,1)S(1)} %get-tuple-element.20.refs_0_, bf16[1024,512]{1,0:T(8,128)(2,1)S(1)} %get-tuple-element.21.refs_1_, bf16[1024,512]{1,0:T(8,128)(2,1)S(1)} %get-tuple-element.22.refs_2_, bf16[1024,512]{1,0:T(8,128)(2,1)S(1)} %get-tuple-element.23.refs_3_, ...), custom_call_target="tpu_custom_call" | custom-call | tf_op jit(solution)/shard_map/across/pallas_call | solution.py:318
  11.4 3.0 %collective-permute-start.10 = (bf16[152,1024]{1,0:T(8,128)(2,1)S(1)}, bf16[152,1024]{1,0:T(8,128)(2,1)S(1)}, u32[]{:S(2)}, u32[]{:S(2)}) collective-permute-start(bf16[152,1024]{1,0:T(8,128)(2,1)S(1)} %across.2), channel_id=1, source_target_pairs={{0,8},{1,9},{2,10},{3,11},{4,12},{5,13},{6,14},{7,15},{8,0},{9,1},... | collective-permute-start | bytes 933896 | tf_op jit(solution)/shard_map/ppermute | solution.py:271
  14.4 1.5 %across.3 = bf16[152,1024]{1,0:T(8,128)(2,1)S(1)} custom-call(bf16[1024,512]{1,0:T(8,128)(2,1)S(1)} %get-tuple-element.20.refs_0_, bf16[1024,512]{1,0:T(8,128)(2,1)S(1)} %get-tuple-element.21.refs_1_, bf16[1024,512]{1,0:T(8,128)(2,1)S(1)} %get-tuple-element.22.refs_2_, bf16[1024,512]{1,0:T(8,128)(2,1)S(1)} %get-tuple-element.23.refs_3_, ...), custom_call_target="tpu_custom_call" | custom-call | tf_op jit(solution)/shard_map/across/pallas_call | solution.py:318
  15.9 3.0 %corner.1 = (bf16[152,1024]{1,0:T(8,128)(2,1)S(1)}, bf16[152,1024]{1,0:T(8,128)(2,1)S(1)}) custom-call(bf16[1024,512]{1,0:T(8,128)(2,1)S(1)} %get-tuple-element.20.refs_0_, bf16[1024,512]{1,0:T(8,128)(2,1)S(1)} %get-tuple-element.21.refs_1_, bf16[1024,512]{1,0:T(8,128)(2,1)S(1)} %get-tuple-element.22.refs_2_, ...), custom_call_target="tpu_custom_call" | custom-call | tf_op jit(solution)/shard_map/corner/pallas_call | solution.py:318
  18.9 5.9 %near.1 = (bf16[152,1024]{1,0:T(8,128)(2,1)S(1)}, bf16[152,1024]{1,0:T(8,128)(2,1)S(1)}, bf16[152,1024]{1,0:T(8,128)(2,1)S(1)}, bf16[152,1024]{1,0:T(8,128)(2,1)S(1)}) custom-call(bf16[1024,512]{1,0:T(8,128)(2,1)S(1)} %get-tuple-element.20.refs_0_, bf16[1024,512]{1,0:T(8,128)(2,1)S(1)} %get-tuple-element.21.refs_1_, ...), custom_call_target="tpu_custom_call" | custom-call | tf_op jit(solution)/shard_map/near/pallas_call | solution.py:318
  24.8 0.1 collective-permute-start.9
  24.9 1.8 %collective-permute-start.7 = (bf16[152,1024]{1,0:T(8,128)(2,1)S(1)}, bf16[152,1024]{1,0:T(8,128)(2,1)S(1)}, u32[]{:S(2)}, u32[]{:S(2)}) collective-permute-start(bf16[152,1024]{1,0:T(8,128)(2,1)S(1)} %across.3), channel_id=1, source_target_pairs={{0,10},{1,11},{2,8},{3,9},{4,14},{5,15},{6,12},{7,13},{8,2},{9,3},... | collective-permute-start | bytes 933896 | tf_op jit(solution)/shard_map/ppermute | solution.py:271
  26.7 2.6 %collective-permute-start.11 = (bf16[152,1024]{1,0:T(8,128)(2,1)S(1)}, bf16[152,1024]{1,0:T(8,128)(2,1)S(1)}, u32[]{:S(2)}, u32[]{:S(2)}) collective-permute-start(bf16[152,1024]{1,0:T(8,128)(2,1)S(1)} %get-tuple-element.28), channel_id=1, source_target_pairs={{0,12},{1,13},{2,14},{3,15},{4,8},{5,9},{6,10},{7,11},{8,4},{9,5},... | collective-permute-start | bytes 933896 | tf_op jit(solution)/shard_map/ppermute | solution.py:271
  29.3 0.5 collective-permute-start.5
  29.8 0.0 collective-permute-done.10.refs_2_
  29.8 1.9 %collective-permute-start.6 = (bf16[152,1024]{1,0:T(8,128)(2,1)S(1)}, bf16[152,1024]{1,0:T(8,128)(2,1)S(1)}, u32[]{:S(2)}, u32[]{:S(2)}) collective-permute-start(bf16[152,1024]{1,0:T(8,128)(2,1)S(1)} %get-tuple-element.32), channel_id=1, source_target_pairs={{0,6},{1,7},{2,4},{3,5},{4,2},{5,3},{6,0},{7,1},{8,14},{9,15},{10,... | collective-permute-start | bytes 933896 | tf_op jit(solution)/shard_map/ppermute | solution.py:271
  31.7 5.3 %collective-permute-done.9.refs_1_ = bf16[152,1024]{1,0:T(8,128)(2,1)S(1)} collective-permute-done((bf16[152,1024]{1,0:T(8,128)(2,1)S(1)}, bf16[152,1024]{1,0:T(8,128)(2,1)S(1)}, u32[]{:S(2)}, u32[]{:S(2)}) %collective-permute-start.9) | collective-permute-done | bytes 311328 | tf_op jit(solution)/shard_map/ppermute | solution.py:271
  37.0 6.0 %collective-permute-start.8 = (bf16[152,1024]{1,0:T(8,128)(2,1)S(1)}, bf16[152,1024]{1,0:T(8,128)(2,1)S(1)}, u32[]{:S(2)}, u32[]{:S(2)}) collective-permute-start(bf16[152,1024]{1,0:T(8,128)(2,1)S(1)} %get-tuple-element.29), channel_id=1, source_target_pairs={{0,14},{1,15},{2,12},{3,13},{4,10},{5,11},{6,8},{7,9},{8,6},{9,7},... | collective-permute-start | bytes 933896 | tf_op jit(solution)/shard_map/ppermute | solution.py:271
  43.0 21.0 %collective-permute-done.11.refs_3_ = bf16[152,1024]{1,0:T(8,128)(2,1)S(1)} collective-permute-done((bf16[152,1024]{1,0:T(8,128)(2,1)S(1)}, bf16[152,1024]{1,0:T(8,128)(2,1)S(1)}, u32[]{:S(2)}, u32[]{:S(2)}) %collective-permute-start.11) | collective-permute-done | bytes 311328 | tf_op jit(solution)/shard_map/ppermute | solution.py:271
  64.0 1.7 %place.2.refs_4_ = bf16[5,96,2048]{2,1,0:T(8,128)(2,1)} custom-call(f32[8,128]{1,0:T(8,128)S(1)} %copy-done.1, bf16[152,1024]{1,0:T(8,128)(2,1)S(1)} %get-tuple-element.33.refs_0_, bf16[152,1024]{1,0:T(8,128)(2,1)S(1)} %collective-permute-done.9.refs_1_, bf16[152,1024]{1,0:T(8,128)(2,1)S(1)} %collective-permute-done.10.refs_2_, ...), custom_call_target="tpu_custom_call" | custom-call | tf_op jit(solution)/shard_map/place/pallas_call | solution.py:344
  65.7 0.0 collective-permute-done.7.refs_2_
  65.7 0.0 collective-permute-done.5.refs_0_
  65.8 3.0 %collective-permute-done.8.refs_3_ = bf16[152,1024]{1,0:T(8,128)(2,1)S(1)} collective-permute-done((bf16[152,1024]{1,0:T(8,128)(2,1)S(1)}, bf16[152,1024]{1,0:T(8,128)(2,1)S(1)}, u32[]{:S(2)}, u32[]{:S(2)}) %collective-permute-start.8) | collective-permute-done | bytes 311328 | tf_op jit(solution)/shard_map/ppermute | solution.py:271
  68.8 1.7 %place.3 = bf16[5,96,2048]{2,1,0:T(8,128)(2,1)} custom-call(f32[8,128]{1,0:T(8,128)S(1)} %copy-done.1, bf16[152,1024]{1,0:T(8,128)(2,1)S(1)} %collective-permute-done.5.refs_0_, bf16[152,1024]{1,0:T(8,128)(2,1)S(1)} %collective-permute-done.6.refs_1_, bf16[152,1024]{1,0:T(8,128)(2,1)S(1)} %collective-permute-done.7.refs_2_, ...), custom_call_target="tpu_custom_call", output_to_operand_aliasing={{}: (5, {})} | custom-call | tf_op jit(solution)/shard_map/place/pallas_call | solution.py:344
  (6 shorter events, 0.0 us)
Async XLA Ops:
  0.0 8.1 %collective-permute-start = (f32[1,16,16,4,512]{4,3,2,1,0:T(4,128)}, f32[1,16,16,4,512]{4,3,2,1,0:T(4,128)S(1)}, u32[]{:S(2)}, u32[]{:S(2)}) collective-permute-start(f32[1,16,16,4,512]{4,3,2,1,0:T(4,128)} %param.7), channel_id=1, source_target_pairs={{0,1},{1,0},{2,3},{3,2},{4,5},{5,4},{6,7},{7,6},{8,9},{9,8},{10,11... | collective-permute-start | bytes 6291464 | tf_op jit(solution)/shard_map/ppermute | solution.py:271
  1.4 7.8 %collective-permute-start.3 = (f32[8,128]{1,0:T(8,128)}, f32[8,128]{1,0:T(8,128)S(1)}, u32[]{:S(2)}, u32[]{:S(2)}) collective-permute-start(f32[8,128]{1,0:T(8,128)} %pack.1.packed_ref), channel_id=1, source_target_pairs={{0,12},{4,8},{8,4},{12,0},{1,13},{5,9},{9,5},{13,1},{2,14},{6,10},... | collective-permute-start | bytes 12296 | tf_op jit(solution)/shard_map/ppermute | solution.py:271
  3.0 6.3 %collective-permute-start.2 = (f32[8,128]{1,0:T(8,128)}, f32[8,128]{1,0:T(8,128)S(1)}, u32[]{:S(2)}, u32[]{:S(2)}) collective-permute-start(f32[8,128]{1,0:T(8,128)} %pack.1.packed_ref), channel_id=1, source_target_pairs={{0,8},{4,12},{8,0},{12,4},{1,9},{5,13},{9,1},{13,5},{2,10},{6,14},... | collective-permute-start | bytes 12296 | tf_op jit(solution)/shard_map/ppermute | solution.py:271
  4.2 5.0 %collective-permute-start.1 = (f32[8,128]{1,0:T(8,128)}, f32[8,128]{1,0:T(8,128)S(1)}, u32[]{:S(2)}, u32[]{:S(2)}) collective-permute-start(f32[8,128]{1,0:T(8,128)} %pack.1.packed_ref), channel_id=1, source_target_pairs={{0,4},{4,0},{8,12},{12,8},{1,5},{5,1},{9,13},{13,9},{2,6},{6,2},{1... | collective-permute-start | bytes 12296 | tf_op jit(solution)/shard_map/ppermute | solution.py:271
  5.5 1.6 %copy-start = (f32[1,16,16,4,512]{4,3,2,1,0:T(4,128)S(1)}, f32[1,16,16,4,512]{4,3,2,1,0:T(4,128)}, u32[]{:S(2)}) copy-start(f32[1,16,16,4,512]{4,3,2,1,0:T(4,128)} %param.7) | copy-start | bytes 6291460
  7.0 2.2 %copy-start.1 = (f32[8,128]{1,0:T(8,128)S(1)}, f32[8,128]{1,0:T(8,128)}, u32[]{:S(2)}) copy-start(f32[8,128]{1,0:T(8,128)} %pack.1.packed_ref) | copy-start | bytes 12292
  9.3 5.1 %collective-permute-start.4 = (f32[4,8,128]{2,1,0:T(8,128)S(1)}, f32[4,8,128]{2,1,0:T(8,128)S(1)}, u32[]{:S(2)}, u32[]{:S(2)}) collective-permute-start(f32[4,8,128]{2,1,0:T(8,128)S(1)} %pad_maximum_fusion.refs_4_), channel_id=1, source_target_pairs={{0,2},{1,3},{2,0},{3,1},{4,6},{5,7},{6,4},{7,5},{8,10},{9,11},{10,... | collective-permute-start | bytes 49160 | tf_op jit(solution)/shard_map/ppermute | solution.py:271
  11.4 18.4 %collective-permute-start.10 = (bf16[152,1024]{1,0:T(8,128)(2,1)S(1)}, bf16[152,1024]{1,0:T(8,128)(2,1)S(1)}, u32[]{:S(2)}, u32[]{:S(2)}) collective-permute-start(bf16[152,1024]{1,0:T(8,128)(2,1)S(1)} %across.2), channel_id=1, source_target_pairs={{0,8},{1,9},{2,10},{3,11},{4,12},{5,13},{6,14},{7,15},{8,0},{9,1},... | collective-permute-start | bytes 933896 | tf_op jit(solution)/shard_map/ppermute | solution.py:271
  24.8 12.2 %collective-permute-start.9 = (bf16[152,1024]{1,0:T(8,128)(2,1)S(1)}, bf16[152,1024]{1,0:T(8,128)(2,1)S(1)}, u32[]{:S(2)}, u32[]{:S(2)}) collective-permute-start(bf16[152,1024]{1,0:T(8,128)(2,1)S(1)} %get-tuple-element.34), channel_id=1, source_target_pairs={{0,4},{1,5},{2,6},{3,7},{4,0},{5,1},{6,2},{7,3},{8,12},{9,13},{10,... | collective-permute-start | bytes 933896 | tf_op jit(solution)/shard_map/ppermute | solution.py:271
  24.9 40.9 %collective-permute-start.7 = (bf16[152,1024]{1,0:T(8,128)(2,1)S(1)}, bf16[152,1024]{1,0:T(8,128)(2,1)S(1)}, u32[]{:S(2)}, u32[]{:S(2)}) collective-permute-start(bf16[152,1024]{1,0:T(8,128)(2,1)S(1)} %across.3), channel_id=1, source_target_pairs={{0,10},{1,11},{2,8},{3,9},{4,14},{5,15},{6,12},{7,13},{8,2},{9,3},... | collective-permute-start | bytes 933896 | tf_op jit(solution)/shard_map/ppermute | solution.py:271
  26.7 37.3 %collective-permute-start.11 = (bf16[152,1024]{1,0:T(8,128)(2,1)S(1)}, bf16[152,1024]{1,0:T(8,128)(2,1)S(1)}, u32[]{:S(2)}, u32[]{:S(2)}) collective-permute-start(bf16[152,1024]{1,0:T(8,128)(2,1)S(1)} %get-tuple-element.28), channel_id=1, source_target_pairs={{0,12},{1,13},{2,14},{3,15},{4,8},{5,9},{6,10},{7,11},{8,4},{9,5},... | collective-permute-start | bytes 933896 | tf_op jit(solution)/shard_map/ppermute | solution.py:271
  29.3 36.5 %collective-permute-start.5 = (bf16[152,1024]{1,0:T(8,128)(2,1)S(1)}, bf16[152,1024]{1,0:T(8,128)(2,1)S(1)}, u32[]{:S(2)}, u32[]{:S(2)}) collective-permute-start(bf16[152,1024]{1,0:T(8,128)(2,1)S(1)} %get-tuple-element.31), channel_id=1, source_target_pairs={{0,2},{1,3},{2,0},{3,1},{4,6},{5,7},{6,4},{7,5},{8,10},{9,11},{10,... | collective-permute-start | bytes 933896 | tf_op jit(solution)/shard_map/ppermute | solution.py:271
  29.8 35.9 %collective-permute-start.6 = (bf16[152,1024]{1,0:T(8,128)(2,1)S(1)}, bf16[152,1024]{1,0:T(8,128)(2,1)S(1)}, u32[]{:S(2)}, u32[]{:S(2)}) collective-permute-start(bf16[152,1024]{1,0:T(8,128)(2,1)S(1)} %get-tuple-element.32), channel_id=1, source_target_pairs={{0,6},{1,7},{2,4},{3,5},{4,2},{5,3},{6,0},{7,1},{8,14},{9,15},{10,... | collective-permute-start | bytes 933896 | tf_op jit(solution)/shard_map/ppermute | solution.py:271
  37.0 31.7 %collective-permute-start.8 = (bf16[152,1024]{1,0:T(8,128)(2,1)S(1)}, bf16[152,1024]{1,0:T(8,128)(2,1)S(1)}, u32[]{:S(2)}, u32[]{:S(2)}) collective-permute-start(bf16[152,1024]{1,0:T(8,128)(2,1)S(1)} %get-tuple-element.29), channel_id=1, source_target_pairs={{0,14},{1,15},{2,12},{3,13},{4,10},{5,11},{6,8},{7,9},{8,6},{9,7},... | collective-permute-start | bytes 933896 | tf_op jit(solution)/shard_map/ppermute | solution.py:271

commit v5 on v4

--- a/solution.py
+++ b/solution.py
@@ -239,28 +239,32 @@
 def place_kernel(capacity, slots, turn, packed_ref, *refs):
     pieces, (out_ref, placed, sems), landed = refs[:4], (refs[-7], *refs[-2:]), refs[-6:-2]
     slab, orb = lax.axis_index("slab"), lax.axis_index("orb")
-    arrivals = [pltpu.make_async_copy(piece, buffer, sems.at[index]) for index, (piece, buffer) in enumerate(zip(pieces, landed))]
-    for arrival in arrivals:
-        arrival.start()
+    width = out_ref.shape[2] // 4
+    arrivals = []
+    for half in range(2):
+        lanes = slice(half * width, (half + 1) * width)
+        for index in range(4):
+            arrival = pltpu.make_async_copy(pieces[index].at[:, lanes], landed[index].at[:, lanes], sems.at[4 * half + index])
+            arrival.start()
+            arrivals.append(arrival)
     electrons = out_ref.shape[1]
-    width = out_ref.shape[2] // 4
     owner = to_column(packed_ref[5:6, :electrons])
     slot = to_column(packed_ref[6:7, :electrons])
     step = jnp.zeros_like(owner)
     for index in range(1, 4):
         step = jnp.where(owner == (slab ^ index).astype(F32), float(index), step)
     pick = (iota((electrons, 4 * slots), 1).astype(F32) == step * float(slots) + slot).astype(BF16)
-    for arrival in arrivals:
-        arrival.wait()
     departures = []
     for half in range(2):
         lanes = slice(half * width, (half + 1) * width)
+        for arrival in arrivals[4 * half : 4 * half + 4]:
+            arrival.wait()
         for k in range(5):
             rows = slice(k * capacity, k * capacity + slots)
             stack = jnp.concatenate([buffer[rows, lanes] for buffer in landed], axis=0)
             placed[half, k] = jnp.dot(pick, stack, preferred_element_type=F32).astype(BF16)
         start = pl.multiple_of((orb ^ (2 * turn + half)) * width, LANES)
-        departure = pltpu.make_async_copy(placed.at[half], out_ref.at[:, :, pl.ds(start, width)], sems.at[4 + half])
+        departure = pltpu.make_async_copy(placed.at[half], out_ref.at[:, :, pl.ds(start, width)], sems.at[8 + half])
         departure.start()
         departures.append(departure)
     for departure in departures:
@@ -306,12 +310,22 @@
             name="split",
         )(view)
 
+    def split(table):
+        view = table.reshape(grid_width * grid_width, planes, orb_local // LANES, LANES)
+        view = view.transpose(0, 2, 1, 3).reshape(taps * orb_local // LANES, LANES)
+        return pl.pallas_call(
+            functools.partial(split_kernel, planes),
+            out_shape=[blocks((taps, orb_local))] * 2,
+            in_specs=[HBM],
+            scratch_shapes=[pltpu.VMEM(view.shape, F32), pltpu.SemaphoreType.DMA((8,))],
+            compiler_params=vmem,
+            name="split",
+        )(view)
+
     along = [packed] + [swap(packed, step, 4, "slab") for step in (1, 2, 3)]
     tables = split(spline_table) + split(partner_table)
-    straight = jnp.stack([after(packed, *tables)] + along[1:])
-    crossed = swap(straight, 2, 4, "orb")
-
-    first = after(along[2], along[1], along[3])
+    pair = jnp.stack([after(packed, *tables), swap(packed, 2, 4, "slab")])
+    side = swap(pair, 1, 4, "slab")
 
     def serve(name, homes, *places):
         count = len(places)
@@ -330,12 +344,14 @@
     def send(step, block):
         return swap(block, step, 16, both_axes)
 
-    across_out = serve("across", [first[None]], (0, 0))
-    across_out += serve("across", [after(crossed, *across_out)], (0, 2))
+    across_out = serve("across", [pair], (0, 1))
+    straight = jnp.stack([after(pair, *across_out), side])
+    crossed = swap(straight, 2, 4, "orb")
+    across_out += serve("across", [after(crossed, *across_out)], (0, (0, 1)))
     both = (after(straight, *across_out), crossed)
-    corner_out = serve("corner", both, (0, 3), (1, 3))
+    corner_out = serve("corner", both, (0, (1, 1)), (1, (1, 1)))
     both = (after(straight, *corner_out), crossed)
-    near_out = serve("near", both, (0, 0), (1, 0), (0, 1), (1, 1))
+    near_out = serve("near", both, (0, (0, 0)), (1, (0, 0)), (0, (1, 0)), (1, (1, 0)))
     far = [send(8 + 2 * index, block) for index, block in enumerate(across_out + corner_out)]
     near = [near_out[0]] + [send(2 * index, near_out[index]) for index in range(1, 4)]
     out = ()
@@ -348,7 +364,7 @@
             out_specs=[HBM],
             input_output_aliases={5: 0} if out else {},
             scratch_shapes=[pltpu.VMEM((rows, width), BF16)] * 4
-            + [pltpu.VMEM((2, 5, electrons, orb_local), BF16), pltpu.SemaphoreType.DMA((6,))],
+            + [pltpu.VMEM((2, 5, electrons, orb_local), BF16), pltpu.SemaphoreType.DMA((10,))],
             compiler_params=vmem,
             name="place",
         )(packed, *pieces, *out)

time: 71.6 us -> 70.3 us (0.982); the launches traced: 70.5 us -> 70.1 us
  starting transfers between devices: 20.5 us -> 10.8 us
  waiting for transfers between devices: 29.3 us -> 38.7 us
    ppermute x12 -> x11, starting transfers between devices: 20.5 us -> 10.8 us  [swap(): return lax.ppermute(array, axes, [(i, i ^ step) for i in range(count)])]
    ppermute x12 -> x11, waiting for transfers between devices: 29.3 us -> 38.7 us  [swap(): return lax.ppermute(array, axes, [(i, i ^ step) for i in range(count)])]
  transfers between devices with their start and end apart: 12 -> 11, of which waited for: 3 -> 5; matrix products, arithmetic and copies ran while one was open for 0% -> 0% of each run, Pallas kernels for 24% -> 24%
where the time goes in v5:
time: 70.3 us; the launch traced here: 70.1 us
  waiting for transfers between devices  38.7 us (55%)
  Pallas kernels  18.9 us (27%)
  starting transfers between devices  10.8 us (15%)
  local copies, waits for them, and re-layouts  1.59 us (2%)
    ppermute x11, waiting for transfers between devices, swap(): return lax.ppermute(array, axes, [(i, i ^ step) for i in range(count)])  38.7 us
    pallas_call x4, Pallas kernels, serve(): pl.pallas_call(functools.partial(serve_kernel, (capacity, slots, grid_wid...  11.9 us
    ppermute x11, starting transfers between devices, swap(): return lax.ppermute(array, axes, [(i, i ^ step) for i in range(count)])  10.8 us
    pallas_call x2, Pallas kernels, small_body(): pl.pallas_call(functools.partial(place_kernel, capacity, slots, turn), ou...  3.46 us
    pallas_call x2, Pallas kernels, split(): pl.pallas_call(functools.partial(split_kernel, planes), out_shape=[blocks...  2.15 us
    unnamed x4, local copies, waits for them, and re-layouts  1.59 us
  transfers between devices with their start and end apart: 11, of which 5 were waited for; matrix products, arithmetic and copies ran while one was open for 0% of the time, Pallas kernels for 24%

profile of v5, /device:TPU:10, one launch (start us, length us, event | category | flops | bytes accessed | tf_op | source)
XLA Modules:
  0.0 70.1 jit_solution(17574886770059992405)
XLA Ops:
  0.0 0.0 collective-permute-start
  0.0 1.4 %pack.1.packed_ref = f32[8,128]{1,0:T(8,128)} custom-call(f32[3,96]{1,0:T(4,128)} %fractions_ref.1, s32[2,96]{1,0:T(2,128)} %cells_ref.1, s32[1,96]{1,0:T(1,128)} %bitcast.21), custom_call_target="tpu_custom_call" | custom-call | tf_op jit(solution)/shard_map/pack/pallas_call | solution.py:298
  1.4 2.6 %collective-permute-start.1 = (f32[8,128]{1,0:T(8,128)}, f32[8,128]{1,0:T(8,128)S(1)}, u32[]{:S(2)}, u32[]{:S(2)}) collective-permute-start(f32[8,128]{1,0:T(8,128)} %pack.1.packed_ref), channel_id=1, source_target_pairs={{0,8},{4,12},{8,0},{12,4},{1,9},{5,13},{9,1},{13,5},{2,10},{6,14},... | collective-permute-start | bytes 12296 | tf_op jit(solution)/shard_map/ppermute | solution.py:275
  4.0 1.6 %copy-done = f32[1,16,16,4,512]{4,3,2,1,0:T(4,128)S(1)} copy-done((f32[1,16,16,4,512]{4,3,2,1,0:T(4,128)S(1)}, f32[1,16,16,4,512]{4,3,2,1,0:T(4,128)}, u32[]{:S(2)}) %copy-start) | copy-done | bytes 2097176
  5.6 1.1 %split.2 = (bf16[1024,512]{1,0:T(8,128)(2,1)S(1)}, bf16[1024,512]{1,0:T(8,128)(2,1)S(1)}) custom-call(f32[4096,128]{1,0:T(8,128)S(1)} %bitcast.15), custom_call_target="tpu_custom_call" | custom-call | tf_op jit(solution)/shard_map/split/pallas_call | solution.py:316
  6.7 0.0 collective-permute-done
  6.7 1.1 %split.3 = (bf16[1024,512]{1,0:T(8,128)(2,1)S(1)}, bf16[1024,512]{1,0:T(8,128)(2,1)S(1)}) custom-call(f32[4096,128]{1,0:T(8,128)S(1)} %bitcast.16), custom_call_target="tpu_custom_call" | custom-call | tf_op jit(solution)/shard_map/split/pallas_call | solution.py:316
  7.8 0.0 collective-permute-done.1
  7.8 0.5 collective-permute-start.2
  8.3 1.5 %across.2 = bf16[152,1024]{1,0:T(8,128)(2,1)S(1)} custom-call(bf16[1024,512]{1,0:T(8,128)(2,1)S(1)} %get-tuple-element.20.refs_0_, bf16[1024,512]{1,0:T(8,128)(2,1)S(1)} %get-tuple-element.21.refs_1_, bf16[1024,512]{1,0:T(8,128)(2,1)S(1)} %get-tuple-element.22.refs_2_, bf16[1024,512]{1,0:T(8,128)(2,1)S(1)} %get-tuple-element.23.refs_3_, ...), custom_call_target="tpu_custom_call" | custom-call | tf_op jit(solution)/shard_map/across/pallas_call | solution.py:332
  9.8 1.7 %collective-permute-done.2 = f32[2,8,128]{2,1,0:T(8,128)S(1)} collective-permute-done((f32[2,8,128]{2,1,0:T(8,128)S(1)}, f32[2,8,128]{2,1,0:T(8,128)S(1)}, u32[]{:S(2)}, u32[]{:S(2)}) %collective-permute-start.2) | collective-permute-done | bytes 8224 | tf_op jit(solution)/shard_map/ppermute | solution.py:275
  11.5 0.5 collective-permute-start.3
  12.0 0.9 %collective-permute-start.9 = (bf16[152,1024]{1,0:T(8,128)(2,1)S(1)}, bf16[152,1024]{1,0:T(8,128)(2,1)S(1)}, u32[]{:S(2)}, u32[]{:S(2)}) collective-permute-start(bf16[152,1024]{1,0:T(8,128)(2,1)S(1)} %across.2), channel_id=1, source_target_pairs={{0,8},{1,9},{2,10},{3,11},{4,12},{5,13},{6,14},{7,15},{8,0},{9,1},... | collective-permute-start | bytes 933896 | tf_op jit(solution)/shard_map/ppermute | solution.py:275
  12.9 2.4 %collective-permute-done.3.refs_4_.refs_5_ = f32[2,2,8,128]{3,2,1,0:T(8,128)S(1)} collective-permute-done((f32[2,2,8,128]{3,2,1,0:T(8,128)S(1)}, f32[2,2,8,128]{3,2,1,0:T(8,128)S(1)}, u32[]{:S(2)}, u32[]{:S(2)}) %collective-permute-start.3) | collective-permute-done | bytes 16416 | tf_op jit(solution)/shard_map/ppermute | solution.py:275
  15.3 1.5 %across.3 = bf16[152,1024]{1,0:T(8,128)(2,1)S(1)} custom-call(bf16[1024,512]{1,0:T(8,128)(2,1)S(1)} %get-tuple-element.20.refs_0_, bf16[1024,512]{1,0:T(8,128)(2,1)S(1)} %get-tuple-element.21.refs_1_, bf16[1024,512]{1,0:T(8,128)(2,1)S(1)} %get-tuple-element.22.refs_2_, bf16[1024,512]{1,0:T(8,128)(2,1)S(1)} %get-tuple-element.23.refs_3_, ...), custom_call_target="tpu_custom_call" | custom-call | tf_op jit(solution)/shard_map/across/pallas_call | solution.py:332
  16.8 3.0 %corner.1 = (bf16[152,1024]{1,0:T(8,128)(2,1)S(1)}, bf16[152,1024]{1,0:T(8,128)(2,1)S(1)}) custom-call(bf16[1024,512]{1,0:T(8,128)(2,1)S(1)} %get-tuple-element.20.refs_0_, bf16[1024,512]{1,0:T(8,128)(2,1)S(1)} %get-tuple-element.21.refs_1_, bf16[1024,512]{1,0:T(8,128)(2,1)S(1)} %get-tuple-element.22.refs_2_, ...), custom_call_target="tpu_custom_call" | custom-call | tf_op jit(solution)/shard_map/corner/pallas_call | solution.py:332
  19.7 5.9 %near.1 = (bf16[152,1024]{1,0:T(8,128)(2,1)S(1)}, bf16[152,1024]{1,0:T(8,128)(2,1)S(1)}, bf16[152,1024]{1,0:T(8,128)(2,1)S(1)}, bf16[152,1024]{1,0:T(8,128)(2,1)S(1)}) custom-call(bf16[1024,512]{1,0:T(8,128)(2,1)S(1)} %get-tuple-element.20.refs_0_, bf16[1024,512]{1,0:T(8,128)(2,1)S(1)} %get-tuple-element.21.refs_1_, ...), custom_call_target="tpu_custom_call" | custom-call | tf_op jit(solution)/shard_map/near/pallas_call | solution.py:332
  25.7 0.5 collective-permute-start.8
  26.2 0.8 %collective-permute-start.6 = (bf16[152,1024]{1,0:T(8,128)(2,1)S(1)}, bf16[152,1024]{1,0:T(8,128)(2,1)S(1)}, u32[]{:S(2)}, u32[]{:S(2)}) collective-permute-start(bf16[152,1024]{1,0:T(8,128)(2,1)S(1)} %across.3), channel_id=1, source_target_pairs={{0,10},{1,11},{2,8},{3,9},{4,14},{5,15},{6,12},{7,13},{8,2},{9,3},... | collective-permute-start | bytes 933896 | tf_op jit(solution)/shard_map/ppermute | solution.py:275
  27.0 2.2 %collective-permute-start.10 = (bf16[152,1024]{1,0:T(8,128)(2,1)S(1)}, bf16[152,1024]{1,0:T(8,128)(2,1)S(1)}, u32[]{:S(2)}, u32[]{:S(2)}) collective-permute-start(bf16[152,1024]{1,0:T(8,128)(2,1)S(1)} %get-tuple-element.28), channel_id=1, source_target_pairs={{0,12},{1,13},{2,14},{3,15},{4,8},{5,9},{6,10},{7,11},{8,4},{9,5},... | collective-permute-start | bytes 933896 | tf_op jit(solution)/shard_map/ppermute | solution.py:275
  29.2 1.5 %collective-permute-start.4 = (bf16[152,1024]{1,0:T(8,128)(2,1)S(1)}, bf16[152,1024]{1,0:T(8,128)(2,1)S(1)}, u32[]{:S(2)}, u32[]{:S(2)}) collective-permute-start(bf16[152,1024]{1,0:T(8,128)(2,1)S(1)} %get-tuple-element.31), channel_id=1, source_target_pairs={{0,2},{1,3},{2,0},{3,1},{4,6},{5,7},{6,4},{7,5},{8,10},{9,11},{10,... | collective-permute-start | bytes 933896 | tf_op jit(solution)/shard_map/ppermute | solution.py:275
  30.7 0.0 collective-permute-done.9.refs_2_
  30.7 1.3 %collective-permute-start.5 = (bf16[152,1024]{1,0:T(8,128)(2,1)S(1)}, bf16[152,1024]{1,0:T(8,128)(2,1)S(1)}, u32[]{:S(2)}, u32[]{:S(2)}) collective-permute-start(bf16[152,1024]{1,0:T(8,128)(2,1)S(1)} %get-tuple-element.32), channel_id=1, source_target_pairs={{0,6},{1,7},{2,4},{3,5},{4,2},{5,3},{6,0},{7,1},{8,14},{9,15},{10,... | collective-permute-start | bytes 933896 | tf_op jit(solution)/shard_map/ppermute | solution.py:275
  32.0 8.3 %collective-permute-done.8.refs_1_ = bf16[152,1024]{1,0:T(8,128)(2,1)S(1)} collective-permute-done((bf16[152,1024]{1,0:T(8,128)(2,1)S(1)}, bf16[152,1024]{1,0:T(8,128)(2,1)S(1)}, u32[]{:S(2)}, u32[]{:S(2)}) %collective-permute-start.8) | collective-permute-done | bytes 311328 | tf_op jit(solution)/shard_map/ppermute | solution.py:275
  40.3 0.0 collective-permute-start.7
  40.3 22.9 %collective-permute-done.10.refs_3_ = bf16[152,1024]{1,0:T(8,128)(2,1)S(1)} collective-permute-done((bf16[152,1024]{1,0:T(8,128)(2,1)S(1)}, bf16[152,1024]{1,0:T(8,128)(2,1)S(1)}, u32[]{:S(2)}, u32[]{:S(2)}) %collective-permute-start.10) | collective-permute-done | bytes 311328 | tf_op jit(solution)/shard_map/ppermute | solution.py:275
  63.2 1.7 %place.2.refs_4_ = bf16[5,96,2048]{2,1,0:T(8,128)(2,1)} custom-call(f32[8,128]{1,0:T(8,128)S(1)} %copy-done.1, bf16[152,1024]{1,0:T(8,128)(2,1)S(1)} %get-tuple-element.33.refs_0_, bf16[152,1024]{1,0:T(8,128)(2,1)S(1)} %collective-permute-done.8.refs_1_, bf16[152,1024]{1,0:T(8,128)(2,1)S(1)} %collective-permute-done.9.refs_2_, ...), custom_call_target="tpu_custom_call" | custom-call | tf_op jit(solution)/shard_map/place/pallas_call | solution.py:360
  64.9 0.0 collective-permute-done.6.refs_2_
  65.0 0.0 collective-permute-done.4.refs_0_
  65.0 0.0 collective-permute-done.5.refs_1_
  65.0 3.4 %collective-permute-done.7.refs_3_ = bf16[152,1024]{1,0:T(8,128)(2,1)S(1)} collective-permute-done((bf16[152,1024]{1,0:T(8,128)(2,1)S(1)}, bf16[152,1024]{1,0:T(8,128)(2,1)S(1)}, u32[]{:S(2)}, u32[]{:S(2)}) %collective-permute-start.7) | collective-permute-done | bytes 311328 | tf_op jit(solution)/shard_map/ppermute | solution.py:275
  68.4 1.7 %place.3 = bf16[5,96,2048]{2,1,0:T(8,128)(2,1)} custom-call(f32[8,128]{1,0:T(8,128)S(1)} %copy-done.1, bf16[152,1024]{1,0:T(8,128)(2,1)S(1)} %collective-permute-done.4.refs_0_, bf16[152,1024]{1,0:T(8,128)(2,1)S(1)} %collective-permute-done.5.refs_1_, bf16[152,1024]{1,0:T(8,128)(2,1)S(1)} %collective-permute-done.6.refs_2_, ...), custom_call_target="tpu_custom_call", output_to_operand_aliasing={{}: (5, {})} | custom-call | tf_op jit(solution)/shard_map/place/pallas_call | solution.py:360
  (5 shorter events, 0.0 us)
Async XLA Ops:
  0.0 6.7 %collective-permute-start = (f32[1,16,16,4,512]{4,3,2,1,0:T(4,128)}, f32[1,16,16,4,512]{4,3,2,1,0:T(4,128)S(1)}, u32[]{:S(2)}, u32[]{:S(2)}) collective-permute-start(f32[1,16,16,4,512]{4,3,2,1,0:T(4,128)} %param.7), channel_id=1, source_target_pairs={{0,1},{1,0},{2,3},{3,2},{4,5},{5,4},{6,7},{7,6},{8,9},{9,8},{10,11... | collective-permute-start | bytes 6291464 | tf_op jit(solution)/shard_map/ppermute | solution.py:275
  1.4 6.4 %collective-permute-start.1 = (f32[8,128]{1,0:T(8,128)}, f32[8,128]{1,0:T(8,128)S(1)}, u32[]{:S(2)}, u32[]{:S(2)}) collective-permute-start(f32[8,128]{1,0:T(8,128)} %pack.1.packed_ref), channel_id=1, source_target_pairs={{0,8},{4,12},{8,0},{12,4},{1,9},{5,13},{9,1},{13,5},{2,10},{6,14},... | collective-permute-start | bytes 12296 | tf_op jit(solution)/shard_map/ppermute | solution.py:275
  4.0 1.6 %copy-start = (f32[1,16,16,4,512]{4,3,2,1,0:T(4,128)S(1)}, f32[1,16,16,4,512]{4,3,2,1,0:T(4,128)}, u32[]{:S(2)}) copy-start(f32[1,16,16,4,512]{4,3,2,1,0:T(4,128)} %param.7) | copy-start | bytes 6291460
  5.6 2.2 %copy-start.1 = (f32[8,128]{1,0:T(8,128)S(1)}, f32[8,128]{1,0:T(8,128)}, u32[]{:S(2)}) copy-start(f32[8,128]{1,0:T(8,128)} %pack.1.packed_ref) | copy-start | bytes 12292
  7.8 3.7 %collective-permute-start.2 = (f32[2,8,128]{2,1,0:T(8,128)S(1)}, f32[2,8,128]{2,1,0:T(8,128)S(1)}, u32[]{:S(2)}, u32[]{:S(2)}) collective-permute-start(f32[2,8,128]{2,1,0:T(8,128)S(1)} %pad_maximum_fusion.1.refs_4_), channel_id=1, source_target_pairs={{0,4},{4,0},{8,12},{12,8},{1,5},{5,1},{9,13},{13,9},{2,6},{6,2},{1... | collective-permute-start | bytes 24584 | tf_op jit(solution)/shard_map/ppermute | solution.py:275
  11.5 3.7 %collective-permute-start.3 = (f32[2,2,8,128]{3,2,1,0:T(8,128)S(1)}, f32[2,2,8,128]{3,2,1,0:T(8,128)S(1)}, u32[]{:S(2)}, u32[]{:S(2)}) collective-permute-start(f32[2,2,8,128]{3,2,1,0:T(8,128)S(1)} %pad_maximum_fusion.refs_4_), channel_id=1, source_target_pairs={{0,2},{1,3},{2,0},{3,1},{4,6},{5,7},{6,4},{7,5},{8,10},{9,11},{10,... | collective-permute-start | bytes 49160 | tf_op jit(solution)/shard_map/ppermute | solution.py:275
  12.0 18.6 %collective-permute-start.9 = (bf16[152,1024]{1,0:T(8,128)(2,1)S(1)}, bf16[152,1024]{1,0:T(8,128)(2,1)S(1)}, u32[]{:S(2)}, u32[]{:S(2)}) collective-permute-start(bf16[152,1024]{1,0:T(8,128)(2,1)S(1)} %across.2), channel_id=1, source_target_pairs={{0,8},{1,9},{2,10},{3,11},{4,12},{5,13},{6,14},{7,15},{8,0},{9,1},... | collective-permute-start | bytes 933896 | tf_op jit(solution)/shard_map/ppermute | solution.py:275
  25.7 14.6 %collective-permute-start.8 = (bf16[152,1024]{1,0:T(8,128)(2,1)S(1)}, bf16[152,1024]{1,0:T(8,128)(2,1)S(1)}, u32[]{:S(2)}, u32[]{:S(2)}) collective-permute-start(bf16[152,1024]{1,0:T(8,128)(2,1)S(1)} %get-tuple-element.34), channel_id=1, source_target_pairs={{0,4},{1,5},{2,6},{3,7},{4,0},{5,1},{6,2},{7,3},{8,12},{9,13},{10,... | collective-permute-start | bytes 933896 | tf_op jit(solution)/shard_map/ppermute | solution.py:275
  26.2 38.8 %collective-permute-start.6 = (bf16[152,1024]{1,0:T(8,128)(2,1)S(1)}, bf16[152,1024]{1,0:T(8,128)(2,1)S(1)}, u32[]{:S(2)}, u32[]{:S(2)}) collective-permute-start(bf16[152,1024]{1,0:T(8,128)(2,1)S(1)} %across.3), channel_id=1, source_target_pairs={{0,10},{1,11},{2,8},{3,9},{4,14},{5,15},{6,12},{7,13},{8,2},{9,3},... | collective-permute-start | bytes 933896 | tf_op jit(solution)/shard_map/ppermute | solution.py:275
  27.0 36.2 %collective-permute-start.10 = (bf16[152,1024]{1,0:T(8,128)(2,1)S(1)}, bf16[152,1024]{1,0:T(8,128)(2,1)S(1)}, u32[]{:S(2)}, u32[]{:S(2)}) collective-permute-start(bf16[152,1024]{1,0:T(8,128)(2,1)S(1)} %get-tuple-element.28), channel_id=1, source_target_pairs={{0,12},{1,13},{2,14},{3,15},{4,8},{5,9},{6,10},{7,11},{8,4},{9,5},... | collective-permute-start | bytes 933896 | tf_op jit(solution)/shard_map/ppermute | solution.py:275
  29.2 35.7 %collective-permute-start.4 = (bf16[152,1024]{1,0:T(8,128)(2,1)S(1)}, bf16[152,1024]{1,0:T(8,128)(2,1)S(1)}, u32[]{:S(2)}, u32[]{:S(2)}) collective-permute-start(bf16[152,1024]{1,0:T(8,128)(2,1)S(1)} %get-tuple-element.31), channel_id=1, source_target_pairs={{0,2},{1,3},{2,0},{3,1},{4,6},{5,7},{6,4},{7,5},{8,10},{9,11},{10,... | collective-permute-start | bytes 933896 | tf_op jit(solution)/shard_map/ppermute | solution.py:275
  30.7 34.3 %collective-permute-start.5 = (bf16[152,1024]{1,0:T(8,128)(2,1)S(1)}, bf16[152,1024]{1,0:T(8,128)(2,1)S(1)}, u32[]{:S(2)}, u32[]{:S(2)}) collective-permute-start(bf16[152,1024]{1,0:T(8,128)(2,1)S(1)} %get-tuple-element.32), channel_id=1, source_target_pairs={{0,6},{1,7},{2,4},{3,5},{4,2},{5,3},{6,0},{7,1},{8,14},{9,15},{10,... | collective-permute-start | bytes 933896 | tf_op jit(solution)/shard_map/ppermute | solution.py:275
  40.3 28.1 %collective-permute-start.7 = (bf16[152,1024]{1,0:T(8,128)(2,1)S(1)}, bf16[152,1024]{1,0:T(8,128)(2,1)S(1)}, u32[]{:S(2)}, u32[]{:S(2)}) collective-permute-start(bf16[152,1024]{1,0:T(8,128)(2,1)S(1)} %get-tuple-element.29), channel_id=1, source_target_pairs={{0,14},{1,15},{2,12},{3,13},{4,10},{5,11},{6,8},{7,9},{8,6},{9,7},... | collective-permute-start | bytes 933896 | tf_op jit(solution)/shard_map/ppermute | solution.py:275

commit v6 on v5

--- a/solution.py
+++ b/solution.py
@@ -132,27 +132,16 @@
     packed_ref[6:7, :electrons] = slot
 
 
-def split_kernel(planes, table_ref, high_ref, low_ref, landed, sems):
+def split_kernel(planes, table_ref, high_ref, low_ref):
     blocks = high_ref.shape[1] // LANES
-    pieces = sems.shape[0]
-    piece = table_ref.shape[0] // pieces
-    count = piece // (blocks * planes)
-    copies = []
-    for index in range(pieces):
-        span = slice(index * piece, (index + 1) * piece)
-        copies.append(pltpu.make_async_copy(table_ref.at[span, :], landed.at[span, :], sems.at[index]))
-        copies[-1].start()
-    for index in range(pieces):
-        copies[index].wait()
-        for block in range(blocks):
-            lanes = slice(block * LANES, (block + 1) * LANES)
-            for plane in range(planes):
-                first = index * piece + block * planes + plane
-                table = landed[pl.ds(first, count, stride=blocks * planes), :]
-                high = table.astype(BF16)
-                start = (plane * pieces + index) * count
-                high_ref[start : start + count, lanes] = high
-                low_ref[start : start + count, lanes] = (table - high.astype(F32)).astype(BF16)
+    count = table_ref.shape[0] // (blocks * planes)
+    for block in range(blocks):
+        for plane in range(planes):
+            table = table_ref[pl.ds(block * planes + plane, count, stride=blocks * planes), :]
+            high = table.astype(BF16)
+            rows, lanes = slice(plane * count, (plane + 1) * count), slice(block * LANES, (block + 1) * LANES)
+            high_ref[rows, lanes] = high
+            low_ref[rows, lanes] = (table - high.astype(F32)).astype(BF16)
 
 
 def slot_weights(home, slab, slots, grid_width, high_ref, low_ref):
@@ -216,10 +205,8 @@
 def serve_kernel(sizes, places, *refs):
     capacity, slots, grid_width = sizes
     count = len(places)
-    weights, sems = refs[-5:-1], refs[-1]
-    tables, homes_refs, outs, staged = refs[:4], refs[4 : -5 - 2 * count], refs[-5 - 2 * count : -5 - count], refs[-5 - count : -5]
+    tables, homes_refs, outs, weights = refs[:4], refs[4 : -4 - count], refs[-4 - count : -4], refs[-4:]
     slab = lax.axis_index("slab")
-    copies = []
     for index in range(count):
         pair = weights[2 * (index % 2) : 2 * (index % 2) + 2]
         which, place = places[index]
@@ -228,25 +215,13 @@
             high_ref, low_ref = tables[2 * half : 2 * half + 2]
             width = high_ref.shape[1]
             result = contract(pair, high_ref[...], low_ref[...])
-            store_slots(staged[index], slice(half * width, (half + 1) * width), result, capacity, slots)
-        copy = pltpu.make_async_copy(staged[index], outs[index], sems.at[index])
-        copy.start()
-        copies.append(copy)
-    for copy in copies:
-        copy.wait()
+            store_slots(outs[index], slice(half * width, (half + 1) * width), result, capacity, slots)
 
 
 def place_kernel(capacity, slots, turn, packed_ref, *refs):
-    pieces, (out_ref, placed, sems), landed = refs[:4], (refs[-7], *refs[-2:]), refs[-6:-2]
+    pieces, (out_ref, placed, sems) = refs[:4], refs[-3:]
     slab, orb = lax.axis_index("slab"), lax.axis_index("orb")
     width = out_ref.shape[2] // 4
-    arrivals = []
-    for half in range(2):
-        lanes = slice(half * width, (half + 1) * width)
-        for index in range(4):
-            arrival = pltpu.make_async_copy(pieces[index].at[:, lanes], landed[index].at[:, lanes], sems.at[4 * half + index])
-            arrival.start()
-            arrivals.append(arrival)
     electrons = out_ref.shape[1]
     owner = to_column(packed_ref[5:6, :electrons])
     slot = to_column(packed_ref[6:7, :electrons])
@@ -257,14 +232,12 @@
     departures = []
     for half in range(2):
         lanes = slice(half * width, (half + 1) * width)
-        for arrival in arrivals[4 * half : 4 * half + 4]:
-            arrival.wait()
         for k in range(5):
             rows = slice(k * capacity, k * capacity + slots)
-            stack = jnp.concatenate([buffer[rows, lanes] for buffer in landed], axis=0)
+            stack = jnp.concatenate([buffer[rows, lanes] for buffer in pieces], axis=0)
             placed[half, k] = jnp.dot(pick, stack, preferred_element_type=F32).astype(BF16)
         start = pl.multiple_of((orb ^ (2 * turn + half)) * width, LANES)
-        departure = pltpu.make_async_copy(placed.at[half], out_ref.at[:, :, pl.ds(start, width)], sems.at[8 + half])
+        departure = pltpu.make_async_copy(placed.at[half], out_ref.at[:, :, pl.ds(start, width)], sems.at[half])
         departure.start()
         departures.append(departure)
     for departure in departures:
@@ -304,8 +277,6 @@
         return pl.pallas_call(
             functools.partial(split_kernel, planes),
             out_shape=[blocks((taps, orb_local))] * 2,
-            in_specs=[HBM],
-            scratch_shapes=[pltpu.VMEM(view.shape, F32), pltpu.SemaphoreType.DMA((8,))],
             compiler_params=vmem,
             name="split",
         )(view)
@@ -316,8 +287,6 @@
         return pl.pallas_call(
             functools.partial(split_kernel, planes),
             out_shape=[blocks((taps, orb_local))] * 2,
-            in_specs=[HBM],
-            scratch_shapes=[pltpu.VMEM(view.shape, F32), pltpu.SemaphoreType.DMA((8,))],
             compiler_params=vmem,
             name="split",
         )(view)
@@ -333,10 +302,8 @@
             functools.partial(serve_kernel, (capacity, slots, grid_width), places),
             out_shape=[blocks((rows, width))] * count,
             in_specs=[VMEM] * (4 + len(homes)),
-            out_specs=[HBM] * count,
-            scratch_shapes=[pltpu.VMEM((rows, width), BF16)] * count
-            + [pltpu.VMEM((5 * slots, taps), BF16)] * 4
-            + [pltpu.SemaphoreType.DMA((count,))],
+            out_specs=[VMEM] * count,
+            scratch_shapes=[pltpu.VMEM((5 * slots, taps), BF16)] * 4,
             compiler_params=vmem,
             name=name,
         )(*tables, *homes)
@@ -360,11 +327,10 @@
         out = pl.pallas_call(
             functools.partial(place_kernel, capacity, slots, turn),
             out_shape=[blocks((5, electrons, 4 * orb_local))],
-            in_specs=[VMEM] + [HBM] * (4 + len(out)),
+            in_specs=[VMEM] * 5 + [HBM] * len(out),
             out_specs=[HBM],
             input_output_aliases={5: 0} if out else {},
-            scratch_shapes=[pltpu.VMEM((rows, width), BF16)] * 4
-            + [pltpu.VMEM((2, 5, electrons, orb_local), BF16), pltpu.SemaphoreType.DMA((10,))],
+            scratch_shapes=[pltpu.VMEM((2, 5, electrons, orb_local), BF16), pltpu.SemaphoreType.DMA((2,))],
             compiler_params=vmem,
             name="place",
         )(packed, *pieces, *out)

time: 70.3 us -> 69.3 us (0.986)
  Pallas kernels: 18.9 us -> 16 us
  starting transfers between devices: 10.8 us -> 13.4 us
    ppermute x11, starting transfers between devices: 10.8 us -> 13.4 us  [swap(): return lax.ppermute(array, axes, [(i, i ^ step) for i in range(count)])]
    pallas_call x4, Pallas kernels: 11.9 us -> 10 us  [serve(): pl.pallas_call(functools.partial(serve_kernel, (capacity, slots, grid_wid...]
    pallas_call x2, Pallas kernels: 3.46 us -> 2.63 us  [small_body(): pl.pallas_call(functools.partial(place_kernel, capacity, slots, turn), ou...]
    ppermute x11, waiting for transfers between devices: 38.7 us -> 38 us  [swap(): return lax.ppermute(array, axes, [(i, i ^ step) for i in range(count)])]
  transfers between devices with their start and end apart: 11 -> 11, of which waited for: 5 -> 5; matrix products, arithmetic and copies ran while one was open for 0% -> 0% of each run, Pallas kernels for 24% -> 21%
where the time goes in v6:
time: 69.3 us; the launch traced here: 69.1 us
  waiting for transfers between devices  38 us (55%)
  Pallas kernels  16 us (23%)
  starting transfers between devices  13.4 us (19%)
  local copies, waits for them, and re-layouts  1.59 us (2%)
    ppermute x11, waiting for transfers between devices, swap(): return lax.ppermute(array, axes, [(i, i ^ step) for i in range(count)])  38 us
    ppermute x11, starting transfers between devices, swap(): return lax.ppermute(array, axes, [(i, i ^ step) for i in range(count)])  13.4 us
    pallas_call x4, Pallas kernels, serve(): pl.pallas_call(functools.partial(serve_kernel, (capacity, slots, grid_wid...  10 us
    pallas_call x2, Pallas kernels, small_body(): pl.pallas_call(functools.partial(place_kernel, capacity, slots, turn), ou...  2.63 us
    pallas_call x2, Pallas kernels, split(): pl.pallas_call(functools.partial(split_kernel, planes), out_shape=[blocks...  1.97 us
    unnamed x4, local copies, waits for them, and re-layouts  1.59 us
    pallas_call x1, Pallas kernels, small_body(): pl.pallas_call(pack_kernel, out_shape=jax.ShapeDtypeStruct((8, LANES), F3...  1.39 us
  transfers between devices with their start and end apart: 11, of which 5 were waited for; matrix products, arithmetic and copies ran while one was open for 0% of the time, Pallas kernels for 21%

profile of v6, /device:TPU:10, one launch (start us, length us, event | category | flops | bytes accessed | tf_op | source)
XLA Modules:
  0.0 69.1 jit_solution(5333159264651442272)
XLA Ops:
  0.0 0.0 collective-permute-start
  0.0 1.4 %pack.1.packed_ref = f32[8,128]{1,0:T(8,128)} custom-call(f32[3,96]{1,0:T(4,128)} %fractions_ref.1, s32[2,96]{1,0:T(2,128)} %cells_ref.1, s32[1,96]{1,0:T(1,128)} %bitcast.21), custom_call_target="tpu_custom_call" | custom-call | tf_op jit(solution)/shard_map/pack/pallas_call | solution.py:271
  1.4 2.6 %collective-permute-start.1 = (f32[8,128]{1,0:T(8,128)}, f32[8,128]{1,0:T(8,128)S(1)}, u32[]{:S(2)}, u32[]{:S(2)}) collective-permute-start(f32[8,128]{1,0:T(8,128)} %pack.1.packed_ref), channel_id=1, source_target_pairs={{0,8},{4,12},{8,0},{12,4},{1,9},{5,13},{9,1},{13,5},{2,10},{6,14},... | collective-permute-start | bytes 12296 | tf_op jit(solution)/shard_map/ppermute | solution.py:248
  4.0 1.6 %copy-done = f32[1,16,16,4,512]{4,3,2,1,0:T(4,128)S(1)} copy-done((f32[1,16,16,4,512]{4,3,2,1,0:T(4,128)S(1)}, f32[1,16,16,4,512]{4,3,2,1,0:T(4,128)}, u32[]{:S(2)}) %copy-start) | copy-done | bytes 2097176
  5.6 1.0 %split.2 = (bf16[1024,512]{1,0:T(8,128)(2,1)S(1)}, bf16[1024,512]{1,0:T(8,128)(2,1)S(1)}) custom-call(f32[4096,128]{1,0:T(8,128)S(1)} %bitcast.15), custom_call_target="tpu_custom_call" | custom-call | tf_op jit(solution)/shard_map/split/pallas_call | solution.py:287
  6.6 0.0 collective-permute-done
  6.6 1.0 %split.3 = (bf16[1024,512]{1,0:T(8,128)(2,1)S(1)}, bf16[1024,512]{1,0:T(8,128)(2,1)S(1)}) custom-call(f32[4096,128]{1,0:T(8,128)S(1)} %bitcast.16), custom_call_target="tpu_custom_call" | custom-call | tf_op jit(solution)/shard_map/split/pallas_call | solution.py:287
  7.6 0.0 collective-permute-done.1
  7.6 0.5 collective-permute-start.2
  8.1 1.4 %across.2 = bf16[152,1024]{1,0:T(8,128)(2,1)S(1)} custom-call(bf16[1024,512]{1,0:T(8,128)(2,1)S(1)} %get-tuple-element.20.refs_0_, bf16[1024,512]{1,0:T(8,128)(2,1)S(1)} %get-tuple-element.21.refs_1_, bf16[1024,512]{1,0:T(8,128)(2,1)S(1)} %get-tuple-element.22.refs_2_, bf16[1024,512]{1,0:T(8,128)(2,1)S(1)} %get-tuple-element.23.refs_3_, ...), custom_call_target="tpu_custom_call" | custom-call | tf_op jit(solution)/shard_map/across/pallas_call | solution.py:301
  9.5 1.8 %collective-permute-done.2 = f32[2,8,128]{2,1,0:T(8,128)S(1)} collective-permute-done((f32[2,8,128]{2,1,0:T(8,128)S(1)}, f32[2,8,128]{2,1,0:T(8,128)S(1)}, u32[]{:S(2)}, u32[]{:S(2)}) %collective-permute-start.2) | collective-permute-done | bytes 8224 | tf_op jit(solution)/shard_map/ppermute | solution.py:248
  11.3 0.5 collective-permute-start.3
  11.8 1.0 %collective-permute-start.9 = (bf16[152,1024]{1,0:T(8,128)(2,1)S(1)}, bf16[152,1024]{1,0:T(8,128)(2,1)S(1)}, u32[]{:S(2)}, u32[]{:S(2)}) collective-permute-start(bf16[152,1024]{1,0:T(8,128)(2,1)S(1)} %across.2), channel_id=1, source_target_pairs={{0,8},{1,9},{2,10},{3,11},{4,12},{5,13},{6,14},{7,15},{8,0},{9,1},... | collective-permute-start | bytes 933896 | tf_op jit(solution)/shard_map/ppermute | solution.py:248
  12.9 2.2 %collective-permute-done.3.refs_4_.refs_5_ = f32[2,2,8,128]{3,2,1,0:T(8,128)S(1)} collective-permute-done((f32[2,2,8,128]{3,2,1,0:T(8,128)S(1)}, f32[2,2,8,128]{3,2,1,0:T(8,128)S(1)}, u32[]{:S(2)}, u32[]{:S(2)}) %collective-permute-start.3) | collective-permute-done | bytes 16416 | tf_op jit(solution)/shard_map/ppermute | solution.py:248
  15.1 1.4 %across.3 = bf16[152,1024]{1,0:T(8,128)(2,1)S(1)} custom-call(bf16[1024,512]{1,0:T(8,128)(2,1)S(1)} %get-tuple-element.20.refs_0_, bf16[1024,512]{1,0:T(8,128)(2,1)S(1)} %get-tuple-element.21.refs_1_, bf16[1024,512]{1,0:T(8,128)(2,1)S(1)} %get-tuple-element.22.refs_2_, bf16[1024,512]{1,0:T(8,128)(2,1)S(1)} %get-tuple-element.23.refs_3_, ...), custom_call_target="tpu_custom_call" | custom-call | tf_op jit(solution)/shard_map/across/pallas_call | solution.py:301
  16.5 2.5 %corner.1 = (bf16[152,1024]{1,0:T(8,128)(2,1)S(1)}, bf16[152,1024]{1,0:T(8,128)(2,1)S(1)}) custom-call(bf16[1024,512]{1,0:T(8,128)(2,1)S(1)} %get-tuple-element.20.refs_0_, bf16[1024,512]{1,0:T(8,128)(2,1)S(1)} %get-tuple-element.21.refs_1_, bf16[1024,512]{1,0:T(8,128)(2,1)S(1)} %get-tuple-element.22.refs_2_, ...), custom_call_target="tpu_custom_call" | custom-call | tf_op jit(solution)/shard_map/corner/pallas_call | solution.py:301
  19.0 4.7 %near.1 = (bf16[152,1024]{1,0:T(8,128)(2,1)S(1)}, bf16[152,1024]{1,0:T(8,128)(2,1)S(1)}, bf16[152,1024]{1,0:T(8,128)(2,1)S(1)}, bf16[152,1024]{1,0:T(8,128)(2,1)S(1)}) custom-call(bf16[1024,512]{1,0:T(8,128)(2,1)S(1)} %get-tuple-element.20.refs_0_, bf16[1024,512]{1,0:T(8,128)(2,1)S(1)} %get-tuple-element.21.refs_1_, ...), custom_call_target="tpu_custom_call" | custom-call | tf_op jit(solution)/shard_map/near/pallas_call | solution.py:301
  23.7 0.5 collective-permute-start.8
  24.2 1.0 %collective-permute-start.6 = (bf16[152,1024]{1,0:T(8,128)(2,1)S(1)}, bf16[152,1024]{1,0:T(8,128)(2,1)S(1)}, u32[]{:S(2)}, u32[]{:S(2)}) collective-permute-start(bf16[152,1024]{1,0:T(8,128)(2,1)S(1)} %across.3), channel_id=1, source_target_pairs={{0,10},{1,11},{2,8},{3,9},{4,14},{5,15},{6,12},{7,13},{8,2},{9,3},... | collective-permute-start | bytes 933896 | tf_op jit(solution)/shard_map/ppermute | solution.py:248
  25.3 2.0 %collective-permute-start.10 = (bf16[152,1024]{1,0:T(8,128)(2,1)S(1)}, bf16[152,1024]{1,0:T(8,128)(2,1)S(1)}, u32[]{:S(2)}, u32[]{:S(2)}) collective-permute-start(bf16[152,1024]{1,0:T(8,128)(2,1)S(1)} %get-tuple-element.28), channel_id=1, source_target_pairs={{0,12},{1,13},{2,14},{3,15},{4,8},{5,9},{6,10},{7,11},{8,4},{9,5},... | collective-permute-start | bytes 933896 | tf_op jit(solution)/shard_map/ppermute | solution.py:248
  27.2 1.5 %collective-permute-start.4 = (bf16[152,1024]{1,0:T(8,128)(2,1)S(1)}, bf16[152,1024]{1,0:T(8,128)(2,1)S(1)}, u32[]{:S(2)}, u32[]{:S(2)}) collective-permute-start(bf16[152,1024]{1,0:T(8,128)(2,1)S(1)} %get-tuple-element.31), channel_id=1, source_target_pairs={{0,2},{1,3},{2,0},{3,1},{4,6},{5,7},{6,4},{7,5},{8,10},{9,11},{10,... | collective-permute-start | bytes 933896 | tf_op jit(solution)/shard_map/ppermute | solution.py:248
  28.7 0.0 collective-permute-done.9.refs_2_
  28.7 1.7 %collective-permute-start.5 = (bf16[152,1024]{1,0:T(8,128)(2,1)S(1)}, bf16[152,1024]{1,0:T(8,128)(2,1)S(1)}, u32[]{:S(2)}, u32[]{:S(2)}) collective-permute-start(bf16[152,1024]{1,0:T(8,128)(2,1)S(1)} %get-tuple-element.32), channel_id=1, source_target_pairs={{0,6},{1,7},{2,4},{3,5},{4,2},{5,3},{6,0},{7,1},{8,14},{9,15},{10,... | collective-permute-start | bytes 933896 | tf_op jit(solution)/shard_map/ppermute | solution.py:248
  30.4 8.6 %collective-permute-done.8.refs_1_ = bf16[152,1024]{1,0:T(8,128)(2,1)S(1)} collective-permute-done((bf16[152,1024]{1,0:T(8,128)(2,1)S(1)}, bf16[152,1024]{1,0:T(8,128)(2,1)S(1)}, u32[]{:S(2)}, u32[]{:S(2)}) %collective-permute-start.8) | collective-permute-done | bytes 311328 | tf_op jit(solution)/shard_map/ppermute | solution.py:248
  39.0 2.1 %collective-permute-start.7 = (bf16[152,1024]{1,0:T(8,128)(2,1)S(1)}, bf16[152,1024]{1,0:T(8,128)(2,1)S(1)}, u32[]{:S(2)}, u32[]{:S(2)}) collective-permute-start(bf16[152,1024]{1,0:T(8,128)(2,1)S(1)} %get-tuple-element.29), channel_id=1, source_target_pairs={{0,14},{1,15},{2,12},{3,13},{4,10},{5,11},{6,8},{7,9},{8,6},{9,7},... | collective-permute-start | bytes 933896 | tf_op jit(solution)/shard_map/ppermute | solution.py:248
  41.0 20.0 %collective-permute-done.10.refs_3_ = bf16[152,1024]{1,0:T(8,128)(2,1)S(1)} collective-permute-done((bf16[152,1024]{1,0:T(8,128)(2,1)S(1)}, bf16[152,1024]{1,0:T(8,128)(2,1)S(1)}, u32[]{:S(2)}, u32[]{:S(2)}) %collective-permute-start.10) | collective-permute-done | bytes 311328 | tf_op jit(solution)/shard_map/ppermute | solution.py:248
  61.0 1.3 %place.2.refs_4_ = bf16[5,96,2048]{2,1,0:T(8,128)(2,1)} custom-call(f32[8,128]{1,0:T(8,128)S(1)} %copy-done.1, bf16[152,1024]{1,0:T(8,128)(2,1)S(1)} %get-tuple-element.33.refs_0_, bf16[152,1024]{1,0:T(8,128)(2,1)S(1)} %collective-permute-done.8.refs_1_, bf16[152,1024]{1,0:T(8,128)(2,1)S(1)} %collective-permute-done.9.refs_2_, ...), custom_call_target="tpu_custom_call" | custom-call | tf_op jit(solution)/shard_map/place/pallas_call | solution.py:327
  62.4 0.0 collective-permute-done.6.refs_2_
  62.4 0.0 collective-permute-done.4.refs_0_
  62.4 0.0 collective-permute-done.5.refs_1_
  62.4 5.4 %collective-permute-done.7.refs_3_ = bf16[152,1024]{1,0:T(8,128)(2,1)S(1)} collective-permute-done((bf16[152,1024]{1,0:T(8,128)(2,1)S(1)}, bf16[152,1024]{1,0:T(8,128)(2,1)S(1)}, u32[]{:S(2)}, u32[]{:S(2)}) %collective-permute-start.7) | collective-permute-done | bytes 311328 | tf_op jit(solution)/shard_map/ppermute | solution.py:248
  67.8 1.3 %place.3 = bf16[5,96,2048]{2,1,0:T(8,128)(2,1)} custom-call(f32[8,128]{1,0:T(8,128)S(1)} %copy-done.1, bf16[152,1024]{1,0:T(8,128)(2,1)S(1)} %collective-permute-done.4.refs_0_, bf16[152,1024]{1,0:T(8,128)(2,1)S(1)} %collective-permute-done.5.refs_1_, bf16[152,1024]{1,0:T(8,128)(2,1)S(1)} %collective-permute-done.6.refs_2_, ...), custom_call_target="tpu_custom_call", output_to_operand_aliasing={{}: (5, {})} | custom-call | tf_op jit(solution)/shard_map/place/pallas_call | solution.py:327
  (5 shorter events, 0.0 us)
Async XLA Ops:
  0.0 6.6 %collective-permute-start = (f32[1,16,16,4,512]{4,3,2,1,0:T(4,128)}, f32[1,16,16,4,512]{4,3,2,1,0:T(4,128)S(1)}, u32[]{:S(2)}, u32[]{:S(2)}) collective-permute-start(f32[1,16,16,4,512]{4,3,2,1,0:T(4,128)} %param.7), channel_id=1, source_target_pairs={{0,1},{1,0},{2,3},{3,2},{4,5},{5,4},{6,7},{7,6},{8,9},{9,8},{10,11... | collective-permute-start | bytes 6291464 | tf_op jit(solution)/shard_map/ppermute | solution.py:248
  1.4 6.2 %collective-permute-start.1 = (f32[8,128]{1,0:T(8,128)}, f32[8,128]{1,0:T(8,128)S(1)}, u32[]{:S(2)}, u32[]{:S(2)}) collective-permute-start(f32[8,128]{1,0:T(8,128)} %pack.1.packed_ref), channel_id=1, source_target_pairs={{0,8},{4,12},{8,0},{12,4},{1,9},{5,13},{9,1},{13,5},{2,10},{6,14},... | collective-permute-start | bytes 12296 | tf_op jit(solution)/shard_map/ppermute | solution.py:248
  4.0 1.6 %copy-start = (f32[1,16,16,4,512]{4,3,2,1,0:T(4,128)S(1)}, f32[1,16,16,4,512]{4,3,2,1,0:T(4,128)}, u32[]{:S(2)}) copy-start(f32[1,16,16,4,512]{4,3,2,1,0:T(4,128)} %param.7) | copy-start | bytes 6291460
  5.6 2.0 %copy-start.1 = (f32[8,128]{1,0:T(8,128)S(1)}, f32[8,128]{1,0:T(8,128)}, u32[]{:S(2)}) copy-start(f32[8,128]{1,0:T(8,128)} %pack.1.packed_ref) | copy-start | bytes 12292
  7.6 3.7 %collective-permute-start.2 = (f32[2,8,128]{2,1,0:T(8,128)S(1)}, f32[2,8,128]{2,1,0:T(8,128)S(1)}, u32[]{:S(2)}, u32[]{:S(2)}) collective-permute-start(f32[2,8,128]{2,1,0:T(8,128)S(1)} %pad_maximum_fusion.1.refs_4_), channel_id=1, source_target_pairs={{0,4},{4,0},{8,12},{12,8},{1,5},{5,1},{9,13},{13,9},{2,6},{6,2},{1... | collective-permute-start | bytes 24584 | tf_op jit(solution)/shard_map/ppermute | solution.py:248
  11.3 3.7 %collective-permute-start.3 = (f32[2,2,8,128]{3,2,1,0:T(8,128)S(1)}, f32[2,2,8,128]{3,2,1,0:T(8,128)S(1)}, u32[]{:S(2)}, u32[]{:S(2)}) collective-permute-start(f32[2,2,8,128]{3,2,1,0:T(8,128)S(1)} %pad_maximum_fusion.refs_4_), channel_id=1, source_target_pairs={{0,2},{1,3},{2,0},{3,1},{4,6},{5,7},{6,4},{7,5},{8,10},{9,11},{10,... | collective-permute-start | bytes 49160 | tf_op jit(solution)/shard_map/ppermute | solution.py:248
  11.8 16.9 %collective-permute-start.9 = (bf16[152,1024]{1,0:T(8,128)(2,1)S(1)}, bf16[152,1024]{1,0:T(8,128)(2,1)S(1)}, u32[]{:S(2)}, u32[]{:S(2)}) collective-permute-start(bf16[152,1024]{1,0:T(8,128)(2,1)S(1)} %across.2), channel_id=1, source_target_pairs={{0,8},{1,9},{2,10},{3,11},{4,12},{5,13},{6,14},{7,15},{8,0},{9,1},... | collective-permute-start | bytes 933896 | tf_op jit(solution)/shard_map/ppermute | solution.py:248
  23.7 15.3 %collective-permute-start.8 = (bf16[152,1024]{1,0:T(8,128)(2,1)S(1)}, bf16[152,1024]{1,0:T(8,128)(2,1)S(1)}, u32[]{:S(2)}, u32[]{:S(2)}) collective-permute-start(bf16[152,1024]{1,0:T(8,128)(2,1)S(1)} %get-tuple-element.34), channel_id=1, source_target_pairs={{0,4},{1,5},{2,6},{3,7},{4,0},{5,1},{6,2},{7,3},{8,12},{9,13},{10,... | collective-permute-start | bytes 933896 | tf_op jit(solution)/shard_map/ppermute | solution.py:248
  24.2 38.1 %collective-permute-start.6 = (bf16[152,1024]{1,0:T(8,128)(2,1)S(1)}, bf16[152,1024]{1,0:T(8,128)(2,1)S(1)}, u32[]{:S(2)}, u32[]{:S(2)}) collective-permute-start(bf16[152,1024]{1,0:T(8,128)(2,1)S(1)} %across.3), channel_id=1, source_target_pairs={{0,10},{1,11},{2,8},{3,9},{4,14},{5,15},{6,12},{7,13},{8,2},{9,3},... | collective-permute-start | bytes 933896 | tf_op jit(solution)/shard_map/ppermute | solution.py:248
  25.3 35.8 %collective-permute-start.10 = (bf16[152,1024]{1,0:T(8,128)(2,1)S(1)}, bf16[152,1024]{1,0:T(8,128)(2,1)S(1)}, u32[]{:S(2)}, u32[]{:S(2)}) collective-permute-start(bf16[152,1024]{1,0:T(8,128)(2,1)S(1)} %get-tuple-element.28), channel_id=1, source_target_pairs={{0,12},{1,13},{2,14},{3,15},{4,8},{5,9},{6,10},{7,11},{8,4},{9,5},... | collective-permute-start | bytes 933896 | tf_op jit(solution)/shard_map/ppermute | solution.py:248
  27.2 35.1 %collective-permute-start.4 = (bf16[152,1024]{1,0:T(8,128)(2,1)S(1)}, bf16[152,1024]{1,0:T(8,128)(2,1)S(1)}, u32[]{:S(2)}, u32[]{:S(2)}) collective-permute-start(bf16[152,1024]{1,0:T(8,128)(2,1)S(1)} %get-tuple-element.31), channel_id=1, source_target_pairs={{0,2},{1,3},{2,0},{3,1},{4,6},{5,7},{6,4},{7,5},{8,10},{9,11},{10,... | collective-permute-start | bytes 933896 | tf_op jit(solution)/shard_map/ppermute | solution.py:248
  28.7 33.7 %collective-permute-start.5 = (bf16[152,1024]{1,0:T(8,128)(2,1)S(1)}, bf16[152,1024]{1,0:T(8,128)(2,1)S(1)}, u32[]{:S(2)}, u32[]{:S(2)}) collective-permute-start(bf16[152,1024]{1,0:T(8,128)(2,1)S(1)} %get-tuple-element.32), channel_id=1, source_target_pairs={{0,6},{1,7},{2,4},{3,5},{4,2},{5,3},{6,0},{7,1},{8,14},{9,15},{10,... | collective-permute-start | bytes 933896 | tf_op jit(solution)/shard_map/ppermute | solution.py:248
  39.0 28.8 %collective-permute-start.7 = (bf16[152,1024]{1,0:T(8,128)(2,1)S(1)}, bf16[152,1024]{1,0:T(8,128)(2,1)S(1)}, u32[]{:S(2)}, u32[]{:S(2)}) collective-permute-start(bf16[152,1024]{1,0:T(8,128)(2,1)S(1)} %get-tuple-element.29), channel_id=1, source_target_pairs={{0,14},{1,15},{2,12},{3,13},{4,10},{5,11},{6,8},{7,9},{8,6},{9,7},... | collective-permute-start | bytes 933896 | tf_op jit(solution)/shard_map/ppermute | solution.py:248

commit v7 on v6

--- a/solution.py
+++ b/solution.py
@@ -8,6 +8,7 @@
 from jax.sharding import PartitionSpec as P
 
 LANES = 128
+BAND = 256
 F32 = jnp.float32
 BF16 = jnp.bfloat16
 
@@ -197,9 +198,13 @@
     return dot(high, table_high) + (dot(low, table_high) + dot(high, table_low))
 
 
-def store_slots(out_ref, lanes, result, capacity, slots):
-    for k in range(5):
-        out_ref[k * capacity : k * capacity + slots, lanes] = result[k * slots : (k + 1) * slots].astype(BF16)
+def store_slots(out_ref, first, result, capacity, slots):
+    lanes = out_ref.shape[1]
+    for band in range(result.shape[1] // lanes):
+        for k in range(5):
+            start = ((first + band) * 5 + k) * capacity
+            count = min(slots, out_ref.shape[0] - start)
+            out_ref[start : start + count, :] = result[k * slots : k * slots + count, band * lanes : (band + 1) * lanes].astype(BF16)
 
 
 def serve_kernel(sizes, places, *refs):
@@ -215,7 +220,7 @@
             high_ref, low_ref = tables[2 * half : 2 * half + 2]
             width = high_ref.shape[1]
             result = contract(pair, high_ref[...], low_ref[...])
-            store_slots(outs[index], slice(half * width, (half + 1) * width), result, capacity, slots)
+            store_slots(outs[index], half * (width // outs[index].shape[1]), result, capacity, slots)
 
 
 def place_kernel(capacity, slots, turn, packed_ref, *refs):
@@ -228,14 +233,21 @@
     step = jnp.zeros_like(owner)
     for index in range(1, 4):
         step = jnp.where(owner == (slab ^ index).astype(F32), float(index), step)
-    pick = (iota((electrons, 4 * slots), 1).astype(F32) == step * float(slots) + slot).astype(BF16)
+    wanted = step * float(slots) + slot
+    column = iota((electrons, 4 * slots), 1).astype(F32)
+    pick = (column == wanted).astype(BF16)
+    pick_last = (column == wanted + float(slots - capacity)).astype(BF16)
+    total, lanes = pieces[0].shape
     departures = []
     for half in range(2):
-        lanes = slice(half * width, (half + 1) * width)
-        for k in range(5):
-            rows = slice(k * capacity, k * capacity + slots)
-            stack = jnp.concatenate([buffer[rows, lanes] for buffer in pieces], axis=0)
-            placed[half, k] = jnp.dot(pick, stack, preferred_element_type=F32).astype(BF16)
+        for band in range(width // lanes):
+            for k in range(5):
+                start = ((half * (width // lanes) + band) * 5 + k) * capacity
+                last = start + slots > total
+                rows = slice(total - slots, total) if last else slice(start, start + slots)
+                stack = jnp.concatenate([piece[rows, :] for piece in pieces], axis=0)
+                result = jnp.dot(pick_last if last else pick, stack, preferred_element_type=F32)
+                placed[half, k, :, band * lanes : (band + 1) * lanes] = result.astype(BF16)
         start = pl.multiple_of((orb ^ (2 * turn + half)) * width, LANES)
         departure = pltpu.make_async_copy(placed.at[half], out_ref.at[:, :, pl.ds(start, width)], sems.at[half])
         departure.start()
@@ -261,7 +273,8 @@
     grid_width, planes, orb_local = spline_table.shape[1], spline_table.shape[3], spline_table.shape[4]
     capacity = slot_capacity(electrons, 4)
     slots = -(-capacity // 16) * 16
-    rows, width = 4 * capacity + slots, 2 * orb_local
+    bands = 2 * orb_local // BAND
+    rows = bands * 5 * capacity
     taps = grid_width * grid_width * planes
     vmem = pltpu.CompilerParams(vmem_limit_bytes=40 * 1024 * 1024)
     blocks = functools.partial(jax.ShapeDtypeStruct, dtype=BF16)
@@ -300,7 +313,7 @@
         count = len(places)
         return pl.pallas_call(
             functools.partial(serve_kernel, (capacity, slots, grid_width), places),
-            out_shape=[blocks((rows, width))] * count,
+            out_shape=[blocks((rows, BAND))] * count,
             in_specs=[VMEM] * (4 + len(homes)),
             out_specs=[VMEM] * count,
             scratch_shapes=[pltpu.VMEM((5 * slots, taps), BF16)] * 4,

time: 69.3 us -> 68.6 us (0.990)
  transfers between devices with their start and end apart: 11 -> 11, of which waited for: 5 -> 5; matrix products, arithmetic and copies ran while one was open for 0% -> 0% of each run, Pallas kernels for 21% -> 22%
where the time goes in v7:
time: 68.6 us; the launch traced here: 68.4 us
  waiting for transfers between devices  37.6 us (55%)
  Pallas kernels  16.1 us (23%)
  starting transfers between devices  13.1 us (19%)
  local copies, waits for them, and re-layouts  1.59 us (2%)
    ppermute x11, waiting for transfers between devices, swap(): return lax.ppermute(array, axes, [(i, i ^ step) for i in range(count)])  37.6 us
    ppermute x11, starting transfers between devices, swap(): return lax.ppermute(array, axes, [(i, i ^ step) for i in range(count)])  13.1 us
    pallas_call x4, Pallas kernels, serve(): pl.pallas_call(functools.partial(serve_kernel, (capacity, slots, grid_wid...  10.1 us
    pallas_call x2, Pallas kernels, small_body(): pl.pallas_call(functools.partial(place_kernel, capacity, slots, turn), ou...  2.64 us
    pallas_call x2, Pallas kernels, split(): pl.pallas_call(functools.partial(split_kernel, planes), out_shape=[blocks...  1.97 us
    unnamed x4, local copies, waits for them, and re-layouts  1.59 us
    pallas_call x1, Pallas kernels, small_body(): pl.pallas_call(pack_kernel, out_shape=jax.ShapeDtypeStruct((8, LANES), F3...  1.39 us
  transfers between devices with their start and end apart: 11, of which 5 were waited for; matrix products, arithmetic and copies ran while one was open for 0% of the time, Pallas kernels for 22%

profile of v7, /device:TPU:10, one launch (start us, length us, event | category | flops | bytes accessed | tf_op | source)
XLA Modules:
  0.0 68.4 jit_solution(13084053610658019712)
XLA Ops:
  0.0 0.0 collective-permute-start
  0.0 1.4 %pack.1.packed_ref = f32[8,128]{1,0:T(8,128)} custom-call(f32[3,96]{1,0:T(4,128)} %fractions_ref.1, s32[2,96]{1,0:T(2,128)} %cells_ref.1, s32[1,96]{1,0:T(1,128)} %bitcast.21), custom_call_target="tpu_custom_call" | custom-call | tf_op jit(solution)/shard_map/pack/pallas_call | solution.py:284
  1.4 2.6 %collective-permute-start.1 = (f32[8,128]{1,0:T(8,128)}, f32[8,128]{1,0:T(8,128)S(1)}, u32[]{:S(2)}, u32[]{:S(2)}) collective-permute-start(f32[8,128]{1,0:T(8,128)} %pack.1.packed_ref), channel_id=1, source_target_pairs={{0,8},{4,12},{8,0},{12,4},{1,9},{5,13},{9,1},{13,5},{2,10},{6,14},... | collective-permute-start | bytes 12296 | tf_op jit(solution)/shard_map/ppermute | solution.py:260
  4.0 1.6 %copy-done = f32[1,16,16,4,512]{4,3,2,1,0:T(4,128)S(1)} copy-done((f32[1,16,16,4,512]{4,3,2,1,0:T(4,128)S(1)}, f32[1,16,16,4,512]{4,3,2,1,0:T(4,128)}, u32[]{:S(2)}) %copy-start) | copy-done | bytes 2097176
  5.6 1.0 %split.2 = (bf16[1024,512]{1,0:T(8,128)(2,1)S(1)}, bf16[1024,512]{1,0:T(8,128)(2,1)S(1)}) custom-call(f32[4096,128]{1,0:T(8,128)S(1)} %bitcast.15), custom_call_target="tpu_custom_call" | custom-call | tf_op jit(solution)/shard_map/split/pallas_call | solution.py:300
  6.6 0.0 collective-permute-done
  6.6 1.0 %split.3 = (bf16[1024,512]{1,0:T(8,128)(2,1)S(1)}, bf16[1024,512]{1,0:T(8,128)(2,1)S(1)}) custom-call(f32[4096,128]{1,0:T(8,128)S(1)} %bitcast.16), custom_call_target="tpu_custom_call" | custom-call | tf_op jit(solution)/shard_map/split/pallas_call | solution.py:300
  7.6 0.0 collective-permute-done.1
  7.6 0.5 collective-permute-start.2
  8.1 1.4 %across.2 = bf16[600,256]{1,0:T(8,128)(2,1)S(1)} custom-call(bf16[1024,512]{1,0:T(8,128)(2,1)S(1)} %get-tuple-element.20.refs_0_, bf16[1024,512]{1,0:T(8,128)(2,1)S(1)} %get-tuple-element.21.refs_1_, bf16[1024,512]{1,0:T(8,128)(2,1)S(1)} %get-tuple-element.22.refs_2_, bf16[1024,512]{1,0:T(8,128)(2,1)S(1)} %get-tuple-element.23.refs_3_, ...), custom_call_target="tpu_custom_call" | custom-call | tf_op jit(solution)/shard_map/across/pallas_call | solution.py:314
  9.5 1.8 %collective-permute-done.2 = f32[2,8,128]{2,1,0:T(8,128)S(1)} collective-permute-done((f32[2,8,128]{2,1,0:T(8,128)S(1)}, f32[2,8,128]{2,1,0:T(8,128)S(1)}, u32[]{:S(2)}, u32[]{:S(2)}) %collective-permute-start.2) | collective-permute-done | bytes 8224 | tf_op jit(solution)/shard_map/ppermute | solution.py:260
  11.3 0.5 collective-permute-start.3
  11.8 1.0 %collective-permute-start.9 = (bf16[600,256]{1,0:T(8,128)(2,1)S(1)}, bf16[600,256]{1,0:T(8,128)(2,1)S(1)}, u32[]{:S(2)}, u32[]{:S(2)}) collective-permute-start(bf16[600,256]{1,0:T(8,128)(2,1)S(1)} %across.2), channel_id=1, source_target_pairs={{0,8},{1,9},{2,10},{3,11},{4,12},{5,13},{6,14},{7,15},{8,0},{9,1},... | collective-permute-start | bytes 921608 | tf_op jit(solution)/shard_map/ppermute | solution.py:260
  12.9 2.2 %collective-permute-done.3.refs_4_.refs_5_ = f32[2,2,8,128]{3,2,1,0:T(8,128)S(1)} collective-permute-done((f32[2,2,8,128]{3,2,1,0:T(8,128)S(1)}, f32[2,2,8,128]{3,2,1,0:T(8,128)S(1)}, u32[]{:S(2)}, u32[]{:S(2)}) %collective-permute-start.3) | collective-permute-done | bytes 16416 | tf_op jit(solution)/shard_map/ppermute | solution.py:260
  15.1 1.4 %across.3 = bf16[600,256]{1,0:T(8,128)(2,1)S(1)} custom-call(bf16[1024,512]{1,0:T(8,128)(2,1)S(1)} %get-tuple-element.20.refs_0_, bf16[1024,512]{1,0:T(8,128)(2,1)S(1)} %get-tuple-element.21.refs_1_, bf16[1024,512]{1,0:T(8,128)(2,1)S(1)} %get-tuple-element.22.refs_2_, bf16[1024,512]{1,0:T(8,128)(2,1)S(1)} %get-tuple-element.23.refs_3_, ...), custom_call_target="tpu_custom_call" | custom-call | tf_op jit(solution)/shard_map/across/pallas_call | solution.py:314
  16.5 2.5 %corner.1 = (bf16[600,256]{1,0:T(8,128)(2,1)S(1)}, bf16[600,256]{1,0:T(8,128)(2,1)S(1)}) custom-call(bf16[1024,512]{1,0:T(8,128)(2,1)S(1)} %get-tuple-element.20.refs_0_, bf16[1024,512]{1,0:T(8,128)(2,1)S(1)} %get-tuple-element.21.refs_1_, bf16[1024,512]{1,0:T(8,128)(2,1)S(1)} %get-tuple-element.22.refs_2_, bf16[1024,512]{1,0:T(8,128)(2,1)S(1)} %get-tuple-element.23.refs_3_, ...), custom_call_target="tpu_custom_call" | custom-call | tf_op jit(solution)/shard_map/corner/pallas_call | solution.py:314
  19.0 4.7 %near.1 = (bf16[600,256]{1,0:T(8,128)(2,1)S(1)}, bf16[600,256]{1,0:T(8,128)(2,1)S(1)}, bf16[600,256]{1,0:T(8,128)(2,1)S(1)}, bf16[600,256]{1,0:T(8,128)(2,1)S(1)}) custom-call(bf16[1024,512]{1,0:T(8,128)(2,1)S(1)} %get-tuple-element.20.refs_0_, bf16[1024,512]{1,0:T(8,128)(2,1)S(1)} %get-tuple-element.21.refs_1_, ...), custom_call_target="tpu_custom_call" | custom-call | tf_op jit(solution)/shard_map/near/pallas_call | solution.py:314
  23.7 0.5 collective-permute-start.8
  24.2 1.0 %collective-permute-start.6 = (bf16[600,256]{1,0:T(8,128)(2,1)S(1)}, bf16[600,256]{1,0:T(8,128)(2,1)S(1)}, u32[]{:S(2)}, u32[]{:S(2)}) collective-permute-start(bf16[600,256]{1,0:T(8,128)(2,1)S(1)} %across.3), channel_id=1, source_target_pairs={{0,10},{1,11},{2,8},{3,9},{4,14},{5,15},{6,12},{7,13},{8,2},{9,3},... | collective-permute-start | bytes 921608 | tf_op jit(solution)/shard_map/ppermute | solution.py:260
  25.3 2.0 %collective-permute-start.10 = (bf16[600,256]{1,0:T(8,128)(2,1)S(1)}, bf16[600,256]{1,0:T(8,128)(2,1)S(1)}, u32[]{:S(2)}, u32[]{:S(2)}) collective-permute-start(bf16[600,256]{1,0:T(8,128)(2,1)S(1)} %get-tuple-element.28), channel_id=1, source_target_pairs={{0,12},{1,13},{2,14},{3,15},{4,8},{5,9},{6,10},{7,11},{8,4},{9,5},... | collective-permute-start | bytes 921608 | tf_op jit(solution)/shard_map/ppermute | solution.py:260
  27.3 1.5 %collective-permute-start.4 = (bf16[600,256]{1,0:T(8,128)(2,1)S(1)}, bf16[600,256]{1,0:T(8,128)(2,1)S(1)}, u32[]{:S(2)}, u32[]{:S(2)}) collective-permute-start(bf16[600,256]{1,0:T(8,128)(2,1)S(1)} %get-tuple-element.31), channel_id=1, source_target_pairs={{0,2},{1,3},{2,0},{3,1},{4,6},{5,7},{6,4},{7,5},{8,10},{9,11},{10,... | collective-permute-start | bytes 921608 | tf_op jit(solution)/shard_map/ppermute | solution.py:260
  28.7 0.0 collective-permute-done.9.refs_2_
  28.8 1.3 %collective-permute-start.5 = (bf16[600,256]{1,0:T(8,128)(2,1)S(1)}, bf16[600,256]{1,0:T(8,128)(2,1)S(1)}, u32[]{:S(2)}, u32[]{:S(2)}) collective-permute-start(bf16[600,256]{1,0:T(8,128)(2,1)S(1)} %get-tuple-element.32), channel_id=1, source_target_pairs={{0,6},{1,7},{2,4},{3,5},{4,2},{5,3},{6,0},{7,1},{8,14},{9,15},{10,... | collective-permute-start | bytes 921608 | tf_op jit(solution)/shard_map/ppermute | solution.py:260
  30.1 8.7 %collective-permute-done.8.refs_1_ = bf16[600,256]{1,0:T(8,128)(2,1)S(1)} collective-permute-done((bf16[600,256]{1,0:T(8,128)(2,1)S(1)}, bf16[600,256]{1,0:T(8,128)(2,1)S(1)}, u32[]{:S(2)}, u32[]{:S(2)}) %collective-permute-start.8) | collective-permute-done | bytes 307232 | tf_op jit(solution)/shard_map/ppermute | solution.py:260
  38.8 2.1 %collective-permute-start.7 = (bf16[600,256]{1,0:T(8,128)(2,1)S(1)}, bf16[600,256]{1,0:T(8,128)(2,1)S(1)}, u32[]{:S(2)}, u32[]{:S(2)}) collective-permute-start(bf16[600,256]{1,0:T(8,128)(2,1)S(1)} %get-tuple-element.29), channel_id=1, source_target_pairs={{0,14},{1,15},{2,12},{3,13},{4,10},{5,11},{6,8},{7,9},{8,6},{9,7},... | collective-permute-start | bytes 921608 | tf_op jit(solution)/shard_map/ppermute | solution.py:260
  40.9 19.7 %collective-permute-done.10.refs_3_ = bf16[600,256]{1,0:T(8,128)(2,1)S(1)} collective-permute-done((bf16[600,256]{1,0:T(8,128)(2,1)S(1)}, bf16[600,256]{1,0:T(8,128)(2,1)S(1)}, u32[]{:S(2)}, u32[]{:S(2)}) %collective-permute-start.10) | collective-permute-done | bytes 307232 | tf_op jit(solution)/shard_map/ppermute | solution.py:260
  60.6 1.3 %place.2.refs_4_ = bf16[5,96,2048]{2,1,0:T(8,128)(2,1)} custom-call(f32[8,128]{1,0:T(8,128)S(1)} %copy-done.1, bf16[600,256]{1,0:T(8,128)(2,1)S(1)} %get-tuple-element.33.refs_0_, bf16[600,256]{1,0:T(8,128)(2,1)S(1)} %collective-permute-done.8.refs_1_, bf16[600,256]{1,0:T(8,128)(2,1)S(1)} %collective-permute-done.9.refs_2_, ...), custom_call_target="tpu_custom_call" | custom-call | tf_op jit(solution)/shard_map/place/pallas_call | solution.py:340
  61.9 0.0 collective-permute-done.6.refs_2_
  61.9 0.0 collective-permute-done.4.refs_0_
  61.9 0.0 collective-permute-done.5.refs_1_
  62.0 5.1 %collective-permute-done.7.refs_3_ = bf16[600,256]{1,0:T(8,128)(2,1)S(1)} collective-permute-done((bf16[600,256]{1,0:T(8,128)(2,1)S(1)}, bf16[600,256]{1,0:T(8,128)(2,1)S(1)}, u32[]{:S(2)}, u32[]{:S(2)}) %collective-permute-start.7) | collective-permute-done | bytes 307232 | tf_op jit(solution)/shard_map/ppermute | solution.py:260
  67.1 1.3 %place.3 = bf16[5,96,2048]{2,1,0:T(8,128)(2,1)} custom-call(f32[8,128]{1,0:T(8,128)S(1)} %copy-done.1, bf16[600,256]{1,0:T(8,128)(2,1)S(1)} %collective-permute-done.4.refs_0_, bf16[600,256]{1,0:T(8,128)(2,1)S(1)} %collective-permute-done.5.refs_1_, bf16[600,256]{1,0:T(8,128)(2,1)S(1)} %collective-permute-done.6.refs_2_, ...), custom_call_target="tpu_custom_call", output_to_operand_aliasing={{}: (5, {})} | custom-call | tf_op jit(solution)/shard_map/place/pallas_call | solution.py:340
  (5 shorter events, 0.0 us)
Async XLA Ops:
  0.0 6.6 %collective-permute-start = (f32[1,16,16,4,512]{4,3,2,1,0:T(4,128)}, f32[1,16,16,4,512]{4,3,2,1,0:T(4,128)S(1)}, u32[]{:S(2)}, u32[]{:S(2)}) collective-permute-start(f32[1,16,16,4,512]{4,3,2,1,0:T(4,128)} %param.7), channel_id=1, source_target_pairs={{0,1},{1,0},{2,3},{3,2},{4,5},{5,4},{6,7},{7,6},{8,9},{9,8},{10,11... | collective-permute-start | bytes 6291464 | tf_op jit(solution)/shard_map/ppermute | solution.py:260
  1.4 6.2 %collective-permute-start.1 = (f32[8,128]{1,0:T(8,128)}, f32[8,128]{1,0:T(8,128)S(1)}, u32[]{:S(2)}, u32[]{:S(2)}) collective-permute-start(f32[8,128]{1,0:T(8,128)} %pack.1.packed_ref), channel_id=1, source_target_pairs={{0,8},{4,12},{8,0},{12,4},{1,9},{5,13},{9,1},{13,5},{2,10},{6,14},... | collective-permute-start | bytes 12296 | tf_op jit(solution)/shard_map/ppermute | solution.py:260
  4.0 1.6 %copy-start = (f32[1,16,16,4,512]{4,3,2,1,0:T(4,128)S(1)}, f32[1,16,16,4,512]{4,3,2,1,0:T(4,128)}, u32[]{:S(2)}) copy-start(f32[1,16,16,4,512]{4,3,2,1,0:T(4,128)} %param.7) | copy-start | bytes 6291460
  5.6 2.0 %copy-start.1 = (f32[8,128]{1,0:T(8,128)S(1)}, f32[8,128]{1,0:T(8,128)}, u32[]{:S(2)}) copy-start(f32[8,128]{1,0:T(8,128)} %pack.1.packed_ref) | copy-start | bytes 12292
  7.6 3.7 %collective-permute-start.2 = (f32[2,8,128]{2,1,0:T(8,128)S(1)}, f32[2,8,128]{2,1,0:T(8,128)S(1)}, u32[]{:S(2)}, u32[]{:S(2)}) collective-permute-start(f32[2,8,128]{2,1,0:T(8,128)S(1)} %pad_maximum_fusion.1.refs_4_), channel_id=1, source_target_pairs={{0,4},{4,0},{8,12},{12,8},{1,5},{5,1},{9,13},{13,9},{2,6},{6,2},{1... | collective-permute-start | bytes 24584 | tf_op jit(solution)/shard_map/ppermute | solution.py:260
  11.3 3.7 %collective-permute-start.3 = (f32[2,2,8,128]{3,2,1,0:T(8,128)S(1)}, f32[2,2,8,128]{3,2,1,0:T(8,128)S(1)}, u32[]{:S(2)}, u32[]{:S(2)}) collective-permute-start(f32[2,2,8,128]{3,2,1,0:T(8,128)S(1)} %pad_maximum_fusion.refs_4_), channel_id=1, source_target_pairs={{0,2},{1,3},{2,0},{3,1},{4,6},{5,7},{6,4},{7,5},{8,10},{9,11},{10,... | collective-permute-start | bytes 49160 | tf_op jit(solution)/shard_map/ppermute | solution.py:260
  11.8 16.9 %collective-permute-start.9 = (bf16[600,256]{1,0:T(8,128)(2,1)S(1)}, bf16[600,256]{1,0:T(8,128)(2,1)S(1)}, u32[]{:S(2)}, u32[]{:S(2)}) collective-permute-start(bf16[600,256]{1,0:T(8,128)(2,1)S(1)} %across.2), channel_id=1, source_target_pairs={{0,8},{1,9},{2,10},{3,11},{4,12},{5,13},{6,14},{7,15},{8,0},{9,1},... | collective-permute-start | bytes 921608 | tf_op jit(solution)/shard_map/ppermute | solution.py:260
  23.7 15.1 %collective-permute-start.8 = (bf16[600,256]{1,0:T(8,128)(2,1)S(1)}, bf16[600,256]{1,0:T(8,128)(2,1)S(1)}, u32[]{:S(2)}, u32[]{:S(2)}) collective-permute-start(bf16[600,256]{1,0:T(8,128)(2,1)S(1)} %get-tuple-element.34), channel_id=1, source_target_pairs={{0,4},{1,5},{2,6},{3,7},{4,0},{5,1},{6,2},{7,3},{8,12},{9,13},{10,... | collective-permute-start | bytes 921608 | tf_op jit(solution)/shard_map/ppermute | solution.py:260
  24.2 37.7 %collective-permute-start.6 = (bf16[600,256]{1,0:T(8,128)(2,1)S(1)}, bf16[600,256]{1,0:T(8,128)(2,1)S(1)}, u32[]{:S(2)}, u32[]{:S(2)}) collective-permute-start(bf16[600,256]{1,0:T(8,128)(2,1)S(1)} %across.3), channel_id=1, source_target_pairs={{0,10},{1,11},{2,8},{3,9},{4,14},{5,15},{6,12},{7,13},{8,2},{9,3},... | collective-permute-start | bytes 921608 | tf_op jit(solution)/shard_map/ppermute | solution.py:260
  25.3 35.3 %collective-permute-start.10 = (bf16[600,256]{1,0:T(8,128)(2,1)S(1)}, bf16[600,256]{1,0:T(8,128)(2,1)S(1)}, u32[]{:S(2)}, u32[]{:S(2)}) collective-permute-start(bf16[600,256]{1,0:T(8,128)(2,1)S(1)} %get-tuple-element.28), channel_id=1, source_target_pairs={{0,12},{1,13},{2,14},{3,15},{4,8},{5,9},{6,10},{7,11},{8,4},{9,5},... | collective-permute-start | bytes 921608 | tf_op jit(solution)/shard_map/ppermute | solution.py:260
  27.3 34.7 %collective-permute-start.4 = (bf16[600,256]{1,0:T(8,128)(2,1)S(1)}, bf16[600,256]{1,0:T(8,128)(2,1)S(1)}, u32[]{:S(2)}, u32[]{:S(2)}) collective-permute-start(bf16[600,256]{1,0:T(8,128)(2,1)S(1)} %get-tuple-element.31), channel_id=1, source_target_pairs={{0,2},{1,3},{2,0},{3,1},{4,6},{5,7},{6,4},{7,5},{8,10},{9,11},{10,... | collective-permute-start | bytes 921608 | tf_op jit(solution)/shard_map/ppermute | solution.py:260
  28.8 33.2 %collective-permute-start.5 = (bf16[600,256]{1,0:T(8,128)(2,1)S(1)}, bf16[600,256]{1,0:T(8,128)(2,1)S(1)}, u32[]{:S(2)}, u32[]{:S(2)}) collective-permute-start(bf16[600,256]{1,0:T(8,128)(2,1)S(1)} %get-tuple-element.32), channel_id=1, source_target_pairs={{0,6},{1,7},{2,4},{3,5},{4,2},{5,3},{6,0},{7,1},{8,14},{9,15},{10,... | collective-permute-start | bytes 921608 | tf_op jit(solution)/shard_map/ppermute | solution.py:260
  38.8 28.3 %collective-permute-start.7 = (bf16[600,256]{1,0:T(8,128)(2,1)S(1)}, bf16[600,256]{1,0:T(8,128)(2,1)S(1)}, u32[]{:S(2)}, u32[]{:S(2)}) collective-permute-start(bf16[600,256]{1,0:T(8,128)(2,1)S(1)} %get-tuple-element.29), channel_id=1, source_target_pairs={{0,14},{1,15},{2,12},{3,13},{4,10},{5,11},{6,8},{7,9},{8,6},{9,7},... | collective-permute-start | bytes 921608 | tf_op jit(solution)/shard_map/ppermute | solution.py:260

commit v8 on v7

--- a/solution.py
+++ b/solution.py
@@ -248,10 +248,11 @@
                 stack = jnp.concatenate([piece[rows, :] for piece in pieces], axis=0)
                 result = jnp.dot(pick_last if last else pick, stack, preferred_element_type=F32)
                 placed[half, k, :, band * lanes : (band + 1) * lanes] = result.astype(BF16)
-        start = pl.multiple_of((orb ^ (2 * turn + half)) * width, LANES)
-        departure = pltpu.make_async_copy(placed.at[half], out_ref.at[:, :, pl.ds(start, width)], sems.at[half])
-        departure.start()
-        departures.append(departure)
+            start = pl.multiple_of((orb ^ (2 * turn + half)) * width + band * lanes, LANES)
+            source = placed.at[half, :, :, band * lanes : (band + 1) * lanes]
+            departure = pltpu.make_async_copy(source, out_ref.at[:, :, pl.ds(start, lanes)], sems.at[half * (width // lanes) + band])
+            departure.start()
+            departures.append(departure)
     for departure in departures:
         departure.wait()
 
@@ -284,6 +285,7 @@
     packed = pl.pallas_call(
         pack_kernel, out_shape=jax.ShapeDtypeStruct((8, LANES), F32), name="pack"
     )(fractions, cell_index, slab_owner.reshape(1, electrons))
+
     def split(table):
         view = table.reshape(grid_width * grid_width, planes, orb_local // LANES, LANES)
         view = view.transpose(0, 2, 1, 3).reshape(taps * orb_local // LANES, LANES)
@@ -294,17 +296,6 @@
             name="split",
         )(view)
 
-    def split(table):
-        view = table.reshape(grid_width * grid_width, planes, orb_local // LANES, LANES)
-        view = view.transpose(0, 2, 1, 3).reshape(taps * orb_local // LANES, LANES)
-        return pl.pallas_call(
-            functools.partial(split_kernel, planes),
-            out_shape=[blocks((taps, orb_local))] * 2,
-            compiler_params=vmem,
-            name="split",
-        )(view)
-
-    along = [packed] + [swap(packed, step, 4, "slab") for step in (1, 2, 3)]
     tables = split(spline_table) + split(partner_table)
     pair = jnp.stack([after(packed, *tables), swap(packed, 2, 4, "slab")])
     side = swap(pair, 1, 4, "slab")
@@ -343,7 +334,7 @@
             in_specs=[VMEM] * 5 + [HBM] * len(out),
             out_specs=[HBM],
             input_output_aliases={5: 0} if out else {},
-            scratch_shapes=[pltpu.VMEM((2, 5, electrons, orb_local), BF16), pltpu.SemaphoreType.DMA((2,))],
+            scratch_shapes=[pltpu.VMEM((2, 5, electrons, orb_local), BF16), pltpu.SemaphoreType.DMA((bands,))],
             compiler_params=vmem,
             name="place",
         )(packed, *pieces, *out)

time: 68.6 us -> 68.5 us (level)
  transfers between devices with their start and end apart: 11 -> 11, of which waited for: 5 -> 5; matrix products, arithmetic and copies ran while one was open for 0% -> 0% of each run, Pallas kernels for 22% -> 21%
where the time goes in v8:
time: 68.5 us; the launch traced here: 68.4 us
  waiting for transfers between devices  37.6 us (55%)
  Pallas kernels  16 us (23%)
  starting transfers between devices  13.1 us (19%)
  local copies, waits for them, and re-layouts  1.59 us (2%)
    ppermute x11, waiting for transfers between devices, swap(): return lax.ppermute(array, axes, [(i, i ^ step) for i in range(count)])  37.6 us
    ppermute x11, starting transfers between devices, swap(): return lax.ppermute(array, axes, [(i, i ^ step) for i in range(count)])  13.1 us
    pallas_call x4, Pallas kernels, serve(): pl.pallas_call(functools.partial(serve_kernel, (capacity, slots, grid_wid...  10.1 us
    pallas_call x2, Pallas kernels, small_body(): pl.pallas_call(functools.partial(place_kernel, capacity, slots, turn), ou...  2.55 us
    pallas_call x2, Pallas kernels, split(): pl.pallas_call(functools.partial(split_kernel, planes), out_shape=[blocks...  1.97 us
    unnamed x4, local copies, waits for them, and re-layouts  1.59 us
    pallas_call x1, Pallas kernels, small_body(): pl.pallas_call(pack_kernel, out_shape=jax.ShapeDtypeStruct((8, LANES), F3...  1.39 us
  transfers between devices with their start and end apart: 11, of which 5 were waited for; matrix products, arithmetic and copies ran while one was open for 0% of the time, Pallas kernels for 21%

profile of v8, /device:TPU:10, one launch (start us, length us, event | category | flops | bytes accessed | tf_op | source)
XLA Modules:
  0.0 68.4 jit_solution(15518827850383854357)
XLA Ops:
  0.0 0.0 collective-permute-start
  0.0 1.4 %pack.1.packed_ref = f32[8,128]{1,0:T(8,128)} custom-call(f32[3,96]{1,0:T(4,128)} %fractions_ref.1, s32[2,96]{1,0:T(2,128)} %cells_ref.1, s32[1,96]{1,0:T(1,128)} %bitcast.21), custom_call_target="tpu_custom_call" | custom-call | tf_op jit(solution)/shard_map/pack/pallas_call | solution.py:285
  1.4 2.6 %collective-permute-start.1 = (f32[8,128]{1,0:T(8,128)}, f32[8,128]{1,0:T(8,128)S(1)}, u32[]{:S(2)}, u32[]{:S(2)}) collective-permute-start(f32[8,128]{1,0:T(8,128)} %pack.1.packed_ref), channel_id=1, source_target_pairs={{0,8},{4,12},{8,0},{12,4},{1,9},{5,13},{9,1},{13,5},{2,10},{6,14},... | collective-permute-start | bytes 12296 | tf_op jit(solution)/shard_map/ppermute | solution.py:261
  4.0 1.6 %copy-done = f32[1,16,16,4,512]{4,3,2,1,0:T(4,128)S(1)} copy-done((f32[1,16,16,4,512]{4,3,2,1,0:T(4,128)S(1)}, f32[1,16,16,4,512]{4,3,2,1,0:T(4,128)}, u32[]{:S(2)}) %copy-start) | copy-done | bytes 2097176
  5.6 1.0 %split.2 = (bf16[1024,512]{1,0:T(8,128)(2,1)S(1)}, bf16[1024,512]{1,0:T(8,128)(2,1)S(1)}) custom-call(f32[4096,128]{1,0:T(8,128)S(1)} %bitcast.15), custom_call_target="tpu_custom_call" | custom-call | tf_op jit(solution)/shard_map/split/pallas_call | solution.py:292
  6.6 0.0 collective-permute-done
  6.6 1.0 %split.3 = (bf16[1024,512]{1,0:T(8,128)(2,1)S(1)}, bf16[1024,512]{1,0:T(8,128)(2,1)S(1)}) custom-call(f32[4096,128]{1,0:T(8,128)S(1)} %bitcast.16), custom_call_target="tpu_custom_call" | custom-call | tf_op jit(solution)/shard_map/split/pallas_call | solution.py:292
  7.6 0.0 collective-permute-done.1
  7.6 0.5 collective-permute-start.2
  8.1 1.4 %across.2 = bf16[600,256]{1,0:T(8,128)(2,1)S(1)} custom-call(bf16[1024,512]{1,0:T(8,128)(2,1)S(1)} %get-tuple-element.20.refs_0_, bf16[1024,512]{1,0:T(8,128)(2,1)S(1)} %get-tuple-element.21.refs_1_, bf16[1024,512]{1,0:T(8,128)(2,1)S(1)} %get-tuple-element.22.refs_2_, bf16[1024,512]{1,0:T(8,128)(2,1)S(1)} %get-tuple-element.23.refs_3_, ...), custom_call_target="tpu_custom_call" | custom-call | tf_op jit(solution)/shard_map/across/pallas_call | solution.py:305
  9.5 1.8 %collective-permute-done.2 = f32[2,8,128]{2,1,0:T(8,128)S(1)} collective-permute-done((f32[2,8,128]{2,1,0:T(8,128)S(1)}, f32[2,8,128]{2,1,0:T(8,128)S(1)}, u32[]{:S(2)}, u32[]{:S(2)}) %collective-permute-start.2) | collective-permute-done | bytes 8224 | tf_op jit(solution)/shard_map/ppermute | solution.py:261
  11.3 0.5 collective-permute-start.3
  11.8 1.0 %collective-permute-start.9 = (bf16[600,256]{1,0:T(8,128)(2,1)S(1)}, bf16[600,256]{1,0:T(8,128)(2,1)S(1)}, u32[]{:S(2)}, u32[]{:S(2)}) collective-permute-start(bf16[600,256]{1,0:T(8,128)(2,1)S(1)} %across.2), channel_id=1, source_target_pairs={{0,8},{1,9},{2,10},{3,11},{4,12},{5,13},{6,14},{7,15},{8,0},{9,1},... | collective-permute-start | bytes 921608 | tf_op jit(solution)/shard_map/ppermute | solution.py:261
  12.9 2.2 %collective-permute-done.3.refs_4_.refs_5_ = f32[2,2,8,128]{3,2,1,0:T(8,128)S(1)} collective-permute-done((f32[2,2,8,128]{3,2,1,0:T(8,128)S(1)}, f32[2,2,8,128]{3,2,1,0:T(8,128)S(1)}, u32[]{:S(2)}, u32[]{:S(2)}) %collective-permute-start.3) | collective-permute-done | bytes 16416 | tf_op jit(solution)/shard_map/ppermute | solution.py:261
  15.1 1.4 %across.3 = bf16[600,256]{1,0:T(8,128)(2,1)S(1)} custom-call(bf16[1024,512]{1,0:T(8,128)(2,1)S(1)} %get-tuple-element.20.refs_0_, bf16[1024,512]{1,0:T(8,128)(2,1)S(1)} %get-tuple-element.21.refs_1_, bf16[1024,512]{1,0:T(8,128)(2,1)S(1)} %get-tuple-element.22.refs_2_, bf16[1024,512]{1,0:T(8,128)(2,1)S(1)} %get-tuple-element.23.refs_3_, ...), custom_call_target="tpu_custom_call" | custom-call | tf_op jit(solution)/shard_map/across/pallas_call | solution.py:305
  16.5 2.5 %corner.1 = (bf16[600,256]{1,0:T(8,128)(2,1)S(1)}, bf16[600,256]{1,0:T(8,128)(2,1)S(1)}) custom-call(bf16[1024,512]{1,0:T(8,128)(2,1)S(1)} %get-tuple-element.20.refs_0_, bf16[1024,512]{1,0:T(8,128)(2,1)S(1)} %get-tuple-element.21.refs_1_, bf16[1024,512]{1,0:T(8,128)(2,1)S(1)} %get-tuple-element.22.refs_2_, bf16[1024,512]{1,0:T(8,128)(2,1)S(1)} %get-tuple-element.23.refs_3_, ...), custom_call_target="tpu_custom_call" | custom-call | tf_op jit(solution)/shard_map/corner/pallas_call | solution.py:305
  19.0 4.7 %near.1 = (bf16[600,256]{1,0:T(8,128)(2,1)S(1)}, bf16[600,256]{1,0:T(8,128)(2,1)S(1)}, bf16[600,256]{1,0:T(8,128)(2,1)S(1)}, bf16[600,256]{1,0:T(8,128)(2,1)S(1)}) custom-call(bf16[1024,512]{1,0:T(8,128)(2,1)S(1)} %get-tuple-element.20.refs_0_, bf16[1024,512]{1,0:T(8,128)(2,1)S(1)} %get-tuple-element.21.refs_1_, ...), custom_call_target="tpu_custom_call" | custom-call | tf_op jit(solution)/shard_map/near/pallas_call | solution.py:305
  23.7 0.5 collective-permute-start.8
  24.2 1.0 %collective-permute-start.6 = (bf16[600,256]{1,0:T(8,128)(2,1)S(1)}, bf16[600,256]{1,0:T(8,128)(2,1)S(1)}, u32[]{:S(2)}, u32[]{:S(2)}) collective-permute-start(bf16[600,256]{1,0:T(8,128)(2,1)S(1)} %across.3), channel_id=1, source_target_pairs={{0,10},{1,11},{2,8},{3,9},{4,14},{5,15},{6,12},{7,13},{8,2},{9,3},... | collective-permute-start | bytes 921608 | tf_op jit(solution)/shard_map/ppermute | solution.py:261
  25.3 2.0 %collective-permute-start.10 = (bf16[600,256]{1,0:T(8,128)(2,1)S(1)}, bf16[600,256]{1,0:T(8,128)(2,1)S(1)}, u32[]{:S(2)}, u32[]{:S(2)}) collective-permute-start(bf16[600,256]{1,0:T(8,128)(2,1)S(1)} %get-tuple-element.28), channel_id=1, source_target_pairs={{0,12},{1,13},{2,14},{3,15},{4,8},{5,9},{6,10},{7,11},{8,4},{9,5},... | collective-permute-start | bytes 921608 | tf_op jit(solution)/shard_map/ppermute | solution.py:261
  27.3 1.5 %collective-permute-start.4 = (bf16[600,256]{1,0:T(8,128)(2,1)S(1)}, bf16[600,256]{1,0:T(8,128)(2,1)S(1)}, u32[]{:S(2)}, u32[]{:S(2)}) collective-permute-start(bf16[600,256]{1,0:T(8,128)(2,1)S(1)} %get-tuple-element.31), channel_id=1, source_target_pairs={{0,2},{1,3},{2,0},{3,1},{4,6},{5,7},{6,4},{7,5},{8,10},{9,11},{10,... | collective-permute-start | bytes 921608 | tf_op jit(solution)/shard_map/ppermute | solution.py:261
  28.7 0.0 collective-permute-done.9.refs_2_
  28.8 1.3 %collective-permute-start.5 = (bf16[600,256]{1,0:T(8,128)(2,1)S(1)}, bf16[600,256]{1,0:T(8,128)(2,1)S(1)}, u32[]{:S(2)}, u32[]{:S(2)}) collective-permute-start(bf16[600,256]{1,0:T(8,128)(2,1)S(1)} %get-tuple-element.32), channel_id=1, source_target_pairs={{0,6},{1,7},{2,4},{3,5},{4,2},{5,3},{6,0},{7,1},{8,14},{9,15},{10,... | collective-permute-start | bytes 921608 | tf_op jit(solution)/shard_map/ppermute | solution.py:261
  30.1 8.7 %collective-permute-done.8.refs_1_ = bf16[600,256]{1,0:T(8,128)(2,1)S(1)} collective-permute-done((bf16[600,256]{1,0:T(8,128)(2,1)S(1)}, bf16[600,256]{1,0:T(8,128)(2,1)S(1)}, u32[]{:S(2)}, u32[]{:S(2)}) %collective-permute-start.8) | collective-permute-done | bytes 307232 | tf_op jit(solution)/shard_map/ppermute | solution.py:261
  38.8 2.1 %collective-permute-start.7 = (bf16[600,256]{1,0:T(8,128)(2,1)S(1)}, bf16[600,256]{1,0:T(8,128)(2,1)S(1)}, u32[]{:S(2)}, u32[]{:S(2)}) collective-permute-start(bf16[600,256]{1,0:T(8,128)(2,1)S(1)} %get-tuple-element.29), channel_id=1, source_target_pairs={{0,14},{1,15},{2,12},{3,13},{4,10},{5,11},{6,8},{7,9},{8,6},{9,7},... | collective-permute-start | bytes 921608 | tf_op jit(solution)/shard_map/ppermute | solution.py:261
  40.9 19.7 %collective-permute-done.10.refs_3_ = bf16[600,256]{1,0:T(8,128)(2,1)S(1)} collective-permute-done((bf16[600,256]{1,0:T(8,128)(2,1)S(1)}, bf16[600,256]{1,0:T(8,128)(2,1)S(1)}, u32[]{:S(2)}, u32[]{:S(2)}) %collective-permute-start.10) | collective-permute-done | bytes 307232 | tf_op jit(solution)/shard_map/ppermute | solution.py:261
  60.6 1.3 %place.2.refs_4_ = bf16[5,96,2048]{2,1,0:T(8,128)(2,1)} custom-call(f32[8,128]{1,0:T(8,128)S(1)} %copy-done.1, bf16[600,256]{1,0:T(8,128)(2,1)S(1)} %get-tuple-element.33.refs_0_, bf16[600,256]{1,0:T(8,128)(2,1)S(1)} %collective-permute-done.8.refs_1_, bf16[600,256]{1,0:T(8,128)(2,1)S(1)} %collective-permute-done.9.refs_2_, ...), custom_call_target="tpu_custom_call" | custom-call | tf_op jit(solution)/shard_map/place/pallas_call | solution.py:331
  61.9 0.0 collective-permute-done.6.refs_2_
  61.9 0.0 collective-permute-done.4.refs_0_
  61.9 0.0 collective-permute-done.5.refs_1_
  61.9 5.2 %collective-permute-done.7.refs_3_ = bf16[600,256]{1,0:T(8,128)(2,1)S(1)} collective-permute-done((bf16[600,256]{1,0:T(8,128)(2,1)S(1)}, bf16[600,256]{1,0:T(8,128)(2,1)S(1)}, u32[]{:S(2)}, u32[]{:S(2)}) %collective-permute-start.7) | collective-permute-done | bytes 307232 | tf_op jit(solution)/shard_map/ppermute | solution.py:261
  67.1 1.3 %place.3 = bf16[5,96,2048]{2,1,0:T(8,128)(2,1)} custom-call(f32[8,128]{1,0:T(8,128)S(1)} %copy-done.1, bf16[600,256]{1,0:T(8,128)(2,1)S(1)} %collective-permute-done.4.refs_0_, bf16[600,256]{1,0:T(8,128)(2,1)S(1)} %collective-permute-done.5.refs_1_, bf16[600,256]{1,0:T(8,128)(2,1)S(1)} %collective-permute-done.6.refs_2_, ...), custom_call_target="tpu_custom_call", output_to_operand_aliasing={{}: (5, {})} | custom-call | tf_op jit(solution)/shard_map/place/pallas_call | solution.py:331
  (5 shorter events, 0.0 us)
Async XLA Ops:
  0.0 6.6 %collective-permute-start = (f32[1,16,16,4,512]{4,3,2,1,0:T(4,128)}, f32[1,16,16,4,512]{4,3,2,1,0:T(4,128)S(1)}, u32[]{:S(2)}, u32[]{:S(2)}) collective-permute-start(f32[1,16,16,4,512]{4,3,2,1,0:T(4,128)} %param.7), channel_id=1, source_target_pairs={{0,1},{1,0},{2,3},{3,2},{4,5},{5,4},{6,7},{7,6},{8,9},{9,8},{10,11... | collective-permute-start | bytes 6291464 | tf_op jit(solution)/shard_map/ppermute | solution.py:261
  1.4 6.2 %collective-permute-start.1 = (f32[8,128]{1,0:T(8,128)}, f32[8,128]{1,0:T(8,128)S(1)}, u32[]{:S(2)}, u32[]{:S(2)}) collective-permute-start(f32[8,128]{1,0:T(8,128)} %pack.1.packed_ref), channel_id=1, source_target_pairs={{0,8},{4,12},{8,0},{12,4},{1,9},{5,13},{9,1},{13,5},{2,10},{6,14},... | collective-permute-start | bytes 12296 | tf_op jit(solution)/shard_map/ppermute | solution.py:261
  4.0 1.6 %copy-start = (f32[1,16,16,4,512]{4,3,2,1,0:T(4,128)S(1)}, f32[1,16,16,4,512]{4,3,2,1,0:T(4,128)}, u32[]{:S(2)}) copy-start(f32[1,16,16,4,512]{4,3,2,1,0:T(4,128)} %param.7) | copy-start | bytes 6291460
  5.6 2.0 %copy-start.1 = (f32[8,128]{1,0:T(8,128)S(1)}, f32[8,128]{1,0:T(8,128)}, u32[]{:S(2)}) copy-start(f32[8,128]{1,0:T(8,128)} %pack.1.packed_ref) | copy-start | bytes 12292
  7.6 3.7 %collective-permute-start.2 = (f32[2,8,128]{2,1,0:T(8,128)S(1)}, f32[2,8,128]{2,1,0:T(8,128)S(1)}, u32[]{:S(2)}, u32[]{:S(2)}) collective-permute-start(f32[2,8,128]{2,1,0:T(8,128)S(1)} %pad_maximum_fusion.1.refs_4_), channel_id=1, source_target_pairs={{0,4},{4,0},{8,12},{12,8},{1,5},{5,1},{9,13},{13,9},{2,6},{6,2},{1... | collective-permute-start | bytes 24584 | tf_op jit(solution)/shard_map/ppermute | solution.py:261
  11.3 3.7 %collective-permute-start.3 = (f32[2,2,8,128]{3,2,1,0:T(8,128)S(1)}, f32[2,2,8,128]{3,2,1,0:T(8,128)S(1)}, u32[]{:S(2)}, u32[]{:S(2)}) collective-permute-start(f32[2,2,8,128]{3,2,1,0:T(8,128)S(1)} %pad_maximum_fusion.refs_4_), channel_id=1, source_target_pairs={{0,2},{1,3},{2,0},{3,1},{4,6},{5,7},{6,4},{7,5},{8,10},{9,11},{10,... | collective-permute-start | bytes 49160 | tf_op jit(solution)/shard_map/ppermute | solution.py:261
  11.8 16.9 %collective-permute-start.9 = (bf16[600,256]{1,0:T(8,128)(2,1)S(1)}, bf16[600,256]{1,0:T(8,128)(2,1)S(1)}, u32[]{:S(2)}, u32[]{:S(2)}) collective-permute-start(bf16[600,256]{1,0:T(8,128)(2,1)S(1)} %across.2), channel_id=1, source_target_pairs={{0,8},{1,9},{2,10},{3,11},{4,12},{5,13},{6,14},{7,15},{8,0},{9,1},... | collective-permute-start | bytes 921608 | tf_op jit(solution)/shard_map/ppermute | solution.py:261
  23.7 15.1 %collective-permute-start.8 = (bf16[600,256]{1,0:T(8,128)(2,1)S(1)}, bf16[600,256]{1,0:T(8,128)(2,1)S(1)}, u32[]{:S(2)}, u32[]{:S(2)}) collective-permute-start(bf16[600,256]{1,0:T(8,128)(2,1)S(1)} %get-tuple-element.34), channel_id=1, source_target_pairs={{0,4},{1,5},{2,6},{3,7},{4,0},{5,1},{6,2},{7,3},{8,12},{9,13},{10,... | collective-permute-start | bytes 921608 | tf_op jit(solution)/shard_map/ppermute | solution.py:261
  24.2 37.6 %collective-permute-start.6 = (bf16[600,256]{1,0:T(8,128)(2,1)S(1)}, bf16[600,256]{1,0:T(8,128)(2,1)S(1)}, u32[]{:S(2)}, u32[]{:S(2)}) collective-permute-start(bf16[600,256]{1,0:T(8,128)(2,1)S(1)} %across.3), channel_id=1, source_target_pairs={{0,10},{1,11},{2,8},{3,9},{4,14},{5,15},{6,12},{7,13},{8,2},{9,3},... | collective-permute-start | bytes 921608 | tf_op jit(solution)/shard_map/ppermute | solution.py:261
  25.3 35.3 %collective-permute-start.10 = (bf16[600,256]{1,0:T(8,128)(2,1)S(1)}, bf16[600,256]{1,0:T(8,128)(2,1)S(1)}, u32[]{:S(2)}, u32[]{:S(2)}) collective-permute-start(bf16[600,256]{1,0:T(8,128)(2,1)S(1)} %get-tuple-element.28), channel_id=1, source_target_pairs={{0,12},{1,13},{2,14},{3,15},{4,8},{5,9},{6,10},{7,11},{8,4},{9,5},... | collective-permute-start | bytes 921608 | tf_op jit(solution)/shard_map/ppermute | solution.py:261
  27.3 34.6 %collective-permute-start.4 = (bf16[600,256]{1,0:T(8,128)(2,1)S(1)}, bf16[600,256]{1,0:T(8,128)(2,1)S(1)}, u32[]{:S(2)}, u32[]{:S(2)}) collective-permute-start(bf16[600,256]{1,0:T(8,128)(2,1)S(1)} %get-tuple-element.31), channel_id=1, source_target_pairs={{0,2},{1,3},{2,0},{3,1},{4,6},{5,7},{6,4},{7,5},{8,10},{9,11},{10,... | collective-permute-start | bytes 921608 | tf_op jit(solution)/shard_map/ppermute | solution.py:261
  28.8 33.2 %collective-permute-start.5 = (bf16[600,256]{1,0:T(8,128)(2,1)S(1)}, bf16[600,256]{1,0:T(8,128)(2,1)S(1)}, u32[]{:S(2)}, u32[]{:S(2)}) collective-permute-start(bf16[600,256]{1,0:T(8,128)(2,1)S(1)} %get-tuple-element.32), channel_id=1, source_target_pairs={{0,6},{1,7},{2,4},{3,5},{4,2},{5,3},{6,0},{7,1},{8,14},{9,15},{10,... | collective-permute-start | bytes 921608 | tf_op jit(solution)/shard_map/ppermute | solution.py:261
  38.8 28.3 %collective-permute-start.7 = (bf16[600,256]{1,0:T(8,128)(2,1)S(1)}, bf16[600,256]{1,0:T(8,128)(2,1)S(1)}, u32[]{:S(2)}, u32[]{:S(2)}) collective-permute-start(bf16[600,256]{1,0:T(8,128)(2,1)S(1)} %get-tuple-element.29), channel_id=1, source_target_pairs={{0,14},{1,15},{2,12},{3,13},{4,10},{5,11},{6,8},{7,9},{8,6},{9,7},... | collective-permute-start | bytes 921608 | tf_op jit(solution)/shard_map/ppermute | solution.py:261

commit v9 on v8

--- a/solution.py
+++ b/solution.py
@@ -195,7 +195,9 @@
 def contract(weights, table_high, table_low):
     dot = functools.partial(jnp.dot, preferred_element_type=F32)
     high, low = weights[0][...], weights[1][...]
-    return dot(high, table_high) + (dot(low, table_high) + dot(high, table_low))
+    both = dot(high, jnp.concatenate([table_high, table_low], axis=1))
+    width = table_high.shape[1]
+    return both[:, :width] + (dot(low, table_high) + both[:, width:])
 
 
 def store_slots(out_ref, first, result, capacity, slots):

time: 68.5 us -> 68.5 us (level)
  no operation moved by 1% of the time
where the time goes in v9:
time: 68.5 us; the launch traced here: 68.4 us
  waiting for transfers between devices  37.6 us (55%)
  Pallas kernels  16 us (23%)
  starting transfers between devices  13.1 us (19%)
  local copies, waits for them, and re-layouts  1.59 us (2%)
    ppermute x11, waiting for transfers between devices, swap(): return lax.ppermute(array, axes, [(i, i ^ step) for i in range(count)])  37.6 us
    ppermute x11, starting transfers between devices, swap(): return lax.ppermute(array, axes, [(i, i ^ step) for i in range(count)])  13.1 us
    pallas_call x4, Pallas kernels, serve(): pl.pallas_call(functools.partial(serve_kernel, (capacity, slots, grid_wid...  10.1 us
    pallas_call x2, Pallas kernels, small_body(): pl.pallas_call(functools.partial(place_kernel, capacity, slots, turn), ou...  2.55 us
    pallas_call x2, Pallas kernels, split(): pl.pallas_call(functools.partial(split_kernel, planes), out_shape=[blocks...  1.97 us
    unnamed x4, local copies, waits for them, and re-layouts  1.59 us
    pallas_call x1, Pallas kernels, small_body(): pl.pallas_call(pack_kernel, out_shape=jax.ShapeDtypeStruct((8, LANES), F3...  1.39 us
  transfers between devices with their start and end apart: 11, of which 5 were waited for; matrix products, arithmetic and copies ran while one was open for 0% of the time, Pallas kernels for 21%

profile of v9, /device:TPU:10, one launch (start us, length us, event | category | flops | bytes accessed | tf_op | source)
XLA Modules:
  0.0 68.4 jit_solution(4179255557788891062)
XLA Ops:
  0.0 0.0 collective-permute-start
  0.0 1.4 %pack.1.packed_ref = f32[8,128]{1,0:T(8,128)} custom-call(f32[3,96]{1,0:T(4,128)} %fractions_ref.1, s32[2,96]{1,0:T(2,128)} %cells_ref.1, s32[1,96]{1,0:T(1,128)} %bitcast.21), custom_call_target="tpu_custom_call" | custom-call | tf_op jit(solution)/shard_map/pack/pallas_call | solution.py:287
  1.4 2.6 %collective-permute-start.1 = (f32[8,128]{1,0:T(8,128)}, f32[8,128]{1,0:T(8,128)S(1)}, u32[]{:S(2)}, u32[]{:S(2)}) collective-permute-start(f32[8,128]{1,0:T(8,128)} %pack.1.packed_ref), channel_id=1, source_target_pairs={{0,8},{4,12},{8,0},{12,4},{1,9},{5,13},{9,1},{13,5},{2,10},{6,14},... | collective-permute-start | bytes 12296 | tf_op jit(solution)/shard_map/ppermute | solution.py:263
  4.0 1.6 %copy-done = f32[1,16,16,4,512]{4,3,2,1,0:T(4,128)S(1)} copy-done((f32[1,16,16,4,512]{4,3,2,1,0:T(4,128)S(1)}, f32[1,16,16,4,512]{4,3,2,1,0:T(4,128)}, u32[]{:S(2)}) %copy-start) | copy-done | bytes 2097176
  5.6 1.0 %split.2 = (bf16[1024,512]{1,0:T(8,128)(2,1)S(1)}, bf16[1024,512]{1,0:T(8,128)(2,1)S(1)}) custom-call(f32[4096,128]{1,0:T(8,128)S(1)} %bitcast.15), custom_call_target="tpu_custom_call" | custom-call | tf_op jit(solution)/shard_map/split/pallas_call | solution.py:294
  6.6 0.0 collective-permute-done
  6.6 1.0 %split.3 = (bf16[1024,512]{1,0:T(8,128)(2,1)S(1)}, bf16[1024,512]{1,0:T(8,128)(2,1)S(1)}) custom-call(f32[4096,128]{1,0:T(8,128)S(1)} %bitcast.16), custom_call_target="tpu_custom_call" | custom-call | tf_op jit(solution)/shard_map/split/pallas_call | solution.py:294
  7.6 0.0 collective-permute-done.1
  7.6 0.5 collective-permute-start.2
  8.1 1.4 %across.2 = bf16[600,256]{1,0:T(8,128)(2,1)S(1)} custom-call(bf16[1024,512]{1,0:T(8,128)(2,1)S(1)} %get-tuple-element.20.refs_0_, bf16[1024,512]{1,0:T(8,128)(2,1)S(1)} %get-tuple-element.21.refs_1_, bf16[1024,512]{1,0:T(8,128)(2,1)S(1)} %get-tuple-element.22.refs_2_, bf16[1024,512]{1,0:T(8,128)(2,1)S(1)} %get-tuple-element.23.refs_3_, ...), custom_call_target="tpu_custom_call" | custom-call | tf_op jit(solution)/shard_map/across/pallas_call | solution.py:307
  9.5 1.8 %collective-permute-done.2 = f32[2,8,128]{2,1,0:T(8,128)S(1)} collective-permute-done((f32[2,8,128]{2,1,0:T(8,128)S(1)}, f32[2,8,128]{2,1,0:T(8,128)S(1)}, u32[]{:S(2)}, u32[]{:S(2)}) %collective-permute-start.2) | collective-permute-done | bytes 8224 | tf_op jit(solution)/shard_map/ppermute | solution.py:263
  11.3 0.5 collective-permute-start.3
  11.8 1.0 %collective-permute-start.9 = (bf16[600,256]{1,0:T(8,128)(2,1)S(1)}, bf16[600,256]{1,0:T(8,128)(2,1)S(1)}, u32[]{:S(2)}, u32[]{:S(2)}) collective-permute-start(bf16[600,256]{1,0:T(8,128)(2,1)S(1)} %across.2), channel_id=1, source_target_pairs={{0,8},{1,9},{2,10},{3,11},{4,12},{5,13},{6,14},{7,15},{8,0},{9,1},... | collective-permute-start | bytes 921608 | tf_op jit(solution)/shard_map/ppermute | solution.py:263
  12.9 2.2 %collective-permute-done.3.refs_4_.refs_5_ = f32[2,2,8,128]{3,2,1,0:T(8,128)S(1)} collective-permute-done((f32[2,2,8,128]{3,2,1,0:T(8,128)S(1)}, f32[2,2,8,128]{3,2,1,0:T(8,128)S(1)}, u32[]{:S(2)}, u32[]{:S(2)}) %collective-permute-start.3) | collective-permute-done | bytes 16416 | tf_op jit(solution)/shard_map/ppermute | solution.py:263
  15.1 1.4 %across.3 = bf16[600,256]{1,0:T(8,128)(2,1)S(1)} custom-call(bf16[1024,512]{1,0:T(8,128)(2,1)S(1)} %get-tuple-element.20.refs_0_, bf16[1024,512]{1,0:T(8,128)(2,1)S(1)} %get-tuple-element.21.refs_1_, bf16[1024,512]{1,0:T(8,128)(2,1)S(1)} %get-tuple-element.22.refs_2_, bf16[1024,512]{1,0:T(8,128)(2,1)S(1)} %get-tuple-element.23.refs_3_, ...), custom_call_target="tpu_custom_call" | custom-call | tf_op jit(solution)/shard_map/across/pallas_call | solution.py:307
  16.5 2.5 %corner.1 = (bf16[600,256]{1,0:T(8,128)(2,1)S(1)}, bf16[600,256]{1,0:T(8,128)(2,1)S(1)}) custom-call(bf16[1024,512]{1,0:T(8,128)(2,1)S(1)} %get-tuple-element.20.refs_0_, bf16[1024,512]{1,0:T(8,128)(2,1)S(1)} %get-tuple-element.21.refs_1_, bf16[1024,512]{1,0:T(8,128)(2,1)S(1)} %get-tuple-element.22.refs_2_, bf16[1024,512]{1,0:T(8,128)(2,1)S(1)} %get-tuple-element.23.refs_3_, ...), custom_call_target="tpu_custom_call" | custom-call | tf_op jit(solution)/shard_map/corner/pallas_call | solution.py:307
  19.0 4.8 %near.1 = (bf16[600,256]{1,0:T(8,128)(2,1)S(1)}, bf16[600,256]{1,0:T(8,128)(2,1)S(1)}, bf16[600,256]{1,0:T(8,128)(2,1)S(1)}, bf16[600,256]{1,0:T(8,128)(2,1)S(1)}) custom-call(bf16[1024,512]{1,0:T(8,128)(2,1)S(1)} %get-tuple-element.20.refs_0_, bf16[1024,512]{1,0:T(8,128)(2,1)S(1)} %get-tuple-element.21.refs_1_, ...), custom_call_target="tpu_custom_call" | custom-call | tf_op jit(solution)/shard_map/near/pallas_call | solution.py:307
  23.7 0.5 collective-permute-start.8
  24.2 1.0 %collective-permute-start.6 = (bf16[600,256]{1,0:T(8,128)(2,1)S(1)}, bf16[600,256]{1,0:T(8,128)(2,1)S(1)}, u32[]{:S(2)}, u32[]{:S(2)}) collective-permute-start(bf16[600,256]{1,0:T(8,128)(2,1)S(1)} %across.3), channel_id=1, source_target_pairs={{0,10},{1,11},{2,8},{3,9},{4,14},{5,15},{6,12},{7,13},{8,2},{9,3},... | collective-permute-start | bytes 921608 | tf_op jit(solution)/shard_map/ppermute | solution.py:263
  25.3 2.0 %collective-permute-start.10 = (bf16[600,256]{1,0:T(8,128)(2,1)S(1)}, bf16[600,256]{1,0:T(8,128)(2,1)S(1)}, u32[]{:S(2)}, u32[]{:S(2)}) collective-permute-start(bf16[600,256]{1,0:T(8,128)(2,1)S(1)} %get-tuple-element.28), channel_id=1, source_target_pairs={{0,12},{1,13},{2,14},{3,15},{4,8},{5,9},{6,10},{7,11},{8,4},{9,5},... | collective-permute-start | bytes 921608 | tf_op jit(solution)/shard_map/ppermute | solution.py:263
  27.3 1.5 %collective-permute-start.4 = (bf16[600,256]{1,0:T(8,128)(2,1)S(1)}, bf16[600,256]{1,0:T(8,128)(2,1)S(1)}, u32[]{:S(2)}, u32[]{:S(2)}) collective-permute-start(bf16[600,256]{1,0:T(8,128)(2,1)S(1)} %get-tuple-element.31), channel_id=1, source_target_pairs={{0,2},{1,3},{2,0},{3,1},{4,6},{5,7},{6,4},{7,5},{8,10},{9,11},{10,... | collective-permute-start | bytes 921608 | tf_op jit(solution)/shard_map/ppermute | solution.py:263
  28.8 0.0 collective-permute-done.9.refs_2_
  28.8 1.3 %collective-permute-start.5 = (bf16[600,256]{1,0:T(8,128)(2,1)S(1)}, bf16[600,256]{1,0:T(8,128)(2,1)S(1)}, u32[]{:S(2)}, u32[]{:S(2)}) collective-permute-start(bf16[600,256]{1,0:T(8,128)(2,1)S(1)} %get-tuple-element.32), channel_id=1, source_target_pairs={{0,6},{1,7},{2,4},{3,5},{4,2},{5,3},{6,0},{7,1},{8,14},{9,15},{10,... | collective-permute-start | bytes 921608 | tf_op jit(solution)/shard_map/ppermute | solution.py:263
  30.1 8.8 %collective-permute-done.8.refs_1_ = bf16[600,256]{1,0:T(8,128)(2,1)S(1)} collective-permute-done((bf16[600,256]{1,0:T(8,128)(2,1)S(1)}, bf16[600,256]{1,0:T(8,128)(2,1)S(1)}, u32[]{:S(2)}, u32[]{:S(2)}) %collective-permute-start.8) | collective-permute-done | bytes 307232 | tf_op jit(solution)/shard_map/ppermute | solution.py:263
  38.8 2.1 %collective-permute-start.7 = (bf16[600,256]{1,0:T(8,128)(2,1)S(1)}, bf16[600,256]{1,0:T(8,128)(2,1)S(1)}, u32[]{:S(2)}, u32[]{:S(2)}) collective-permute-start(bf16[600,256]{1,0:T(8,128)(2,1)S(1)} %get-tuple-element.29), channel_id=1, source_target_pairs={{0,14},{1,15},{2,12},{3,13},{4,10},{5,11},{6,8},{7,9},{8,6},{9,7},... | collective-permute-start | bytes 921608 | tf_op jit(solution)/shard_map/ppermute | solution.py:263
  40.9 19.7 %collective-permute-done.10.refs_3_ = bf16[600,256]{1,0:T(8,128)(2,1)S(1)} collective-permute-done((bf16[600,256]{1,0:T(8,128)(2,1)S(1)}, bf16[600,256]{1,0:T(8,128)(2,1)S(1)}, u32[]{:S(2)}, u32[]{:S(2)}) %collective-permute-start.10) | collective-permute-done | bytes 307232 | tf_op jit(solution)/shard_map/ppermute | solution.py:263
  60.6 1.3 %place.2.refs_4_ = bf16[5,96,2048]{2,1,0:T(8,128)(2,1)} custom-call(f32[8,128]{1,0:T(8,128)S(1)} %copy-done.1, bf16[600,256]{1,0:T(8,128)(2,1)S(1)} %get-tuple-element.33.refs_0_, bf16[600,256]{1,0:T(8,128)(2,1)S(1)} %collective-permute-done.8.refs_1_, bf16[600,256]{1,0:T(8,128)(2,1)S(1)} %collective-permute-done.9.refs_2_, ...), custom_call_target="tpu_custom_call" | custom-call | tf_op jit(solution)/shard_map/place/pallas_call | solution.py:333
  61.9 0.0 collective-permute-done.6.refs_2_
  61.9 0.0 collective-permute-done.4.refs_0_
  61.9 0.0 collective-permute-done.5.refs_1_
  61.9 5.2 %collective-permute-done.7.refs_3_ = bf16[600,256]{1,0:T(8,128)(2,1)S(1)} collective-permute-done((bf16[600,256]{1,0:T(8,128)(2,1)S(1)}, bf16[600,256]{1,0:T(8,128)(2,1)S(1)}, u32[]{:S(2)}, u32[]{:S(2)}) %collective-permute-start.7) | collective-permute-done | bytes 307232 | tf_op jit(solution)/shard_map/ppermute | solution.py:263
  67.1 1.3 %place.3 = bf16[5,96,2048]{2,1,0:T(8,128)(2,1)} custom-call(f32[8,128]{1,0:T(8,128)S(1)} %copy-done.1, bf16[600,256]{1,0:T(8,128)(2,1)S(1)} %collective-permute-done.4.refs_0_, bf16[600,256]{1,0:T(8,128)(2,1)S(1)} %collective-permute-done.5.refs_1_, bf16[600,256]{1,0:T(8,128)(2,1)S(1)} %collective-permute-done.6.refs_2_, ...), custom_call_target="tpu_custom_call", output_to_operand_aliasing={{}: (5, {})} | custom-call | tf_op jit(solution)/shard_map/place/pallas_call | solution.py:333
  (5 shorter events, 0.0 us)
Async XLA Ops:
  0.0 6.6 %collective-permute-start = (f32[1,16,16,4,512]{4,3,2,1,0:T(4,128)}, f32[1,16,16,4,512]{4,3,2,1,0:T(4,128)S(1)}, u32[]{:S(2)}, u32[]{:S(2)}) collective-permute-start(f32[1,16,16,4,512]{4,3,2,1,0:T(4,128)} %param.7), channel_id=1, source_target_pairs={{0,1},{1,0},{2,3},{3,2},{4,5},{5,4},{6,7},{7,6},{8,9},{9,8},{10,11... | collective-permute-start | bytes 6291464 | tf_op jit(solution)/shard_map/ppermute | solution.py:263
  1.4 6.2 %collective-permute-start.1 = (f32[8,128]{1,0:T(8,128)}, f32[8,128]{1,0:T(8,128)S(1)}, u32[]{:S(2)}, u32[]{:S(2)}) collective-permute-start(f32[8,128]{1,0:T(8,128)} %pack.1.packed_ref), channel_id=1, source_target_pairs={{0,8},{4,12},{8,0},{12,4},{1,9},{5,13},{9,1},{13,5},{2,10},{6,14},... | collective-permute-start | bytes 12296 | tf_op jit(solution)/shard_map/ppermute | solution.py:263
  4.0 1.6 %copy-start = (f32[1,16,16,4,512]{4,3,2,1,0:T(4,128)S(1)}, f32[1,16,16,4,512]{4,3,2,1,0:T(4,128)}, u32[]{:S(2)}) copy-start(f32[1,16,16,4,512]{4,3,2,1,0:T(4,128)} %param.7) | copy-start | bytes 6291460
  5.6 2.0 %copy-start.1 = (f32[8,128]{1,0:T(8,128)S(1)}, f32[8,128]{1,0:T(8,128)}, u32[]{:S(2)}) copy-start(f32[8,128]{1,0:T(8,128)} %pack.1.packed_ref) | copy-start | bytes 12292
  7.6 3.7 %collective-permute-start.2 = (f32[2,8,128]{2,1,0:T(8,128)S(1)}, f32[2,8,128]{2,1,0:T(8,128)S(1)}, u32[]{:S(2)}, u32[]{:S(2)}) collective-permute-start(f32[2,8,128]{2,1,0:T(8,128)S(1)} %pad_maximum_fusion.1.refs_4_), channel_id=1, source_target_pairs={{0,4},{4,0},{8,12},{12,8},{1,5},{5,1},{9,13},{13,9},{2,6},{6,2},{1... | collective-permute-start | bytes 24584 | tf_op jit(solution)/shard_map/ppermute | solution.py:263
  11.3 3.7 %collective-permute-start.3 = (f32[2,2,8,128]{3,2,1,0:T(8,128)S(1)}, f32[2,2,8,128]{3,2,1,0:T(8,128)S(1)}, u32[]{:S(2)}, u32[]{:S(2)}) collective-permute-start(f32[2,2,8,128]{3,2,1,0:T(8,128)S(1)} %pad_maximum_fusion.refs_4_), channel_id=1, source_target_pairs={{0,2},{1,3},{2,0},{3,1},{4,6},{5,7},{6,4},{7,5},{8,10},{9,11},{10,... | collective-permute-start | bytes 49160 | tf_op jit(solution)/shard_map/ppermute | solution.py:263
  11.8 16.9 %collective-permute-start.9 = (bf16[600,256]{1,0:T(8,128)(2,1)S(1)}, bf16[600,256]{1,0:T(8,128)(2,1)S(1)}, u32[]{:S(2)}, u32[]{:S(2)}) collective-permute-start(bf16[600,256]{1,0:T(8,128)(2,1)S(1)} %across.2), channel_id=1, source_target_pairs={{0,8},{1,9},{2,10},{3,11},{4,12},{5,13},{6,14},{7,15},{8,0},{9,1},... | collective-permute-start | bytes 921608 | tf_op jit(solution)/shard_map/ppermute | solution.py:263
  23.7 15.1 %collective-permute-start.8 = (bf16[600,256]{1,0:T(8,128)(2,1)S(1)}, bf16[600,256]{1,0:T(8,128)(2,1)S(1)}, u32[]{:S(2)}, u32[]{:S(2)}) collective-permute-start(bf16[600,256]{1,0:T(8,128)(2,1)S(1)} %get-tuple-element.34), channel_id=1, source_target_pairs={{0,4},{1,5},{2,6},{3,7},{4,0},{5,1},{6,2},{7,3},{8,12},{9,13},{10,... | collective-permute-start | bytes 921608 | tf_op jit(solution)/shard_map/ppermute | solution.py:263
  24.2 37.6 %collective-permute-start.6 = (bf16[600,256]{1,0:T(8,128)(2,1)S(1)}, bf16[600,256]{1,0:T(8,128)(2,1)S(1)}, u32[]{:S(2)}, u32[]{:S(2)}) collective-permute-start(bf16[600,256]{1,0:T(8,128)(2,1)S(1)} %across.3), channel_id=1, source_target_pairs={{0,10},{1,11},{2,8},{3,9},{4,14},{5,15},{6,12},{7,13},{8,2},{9,3},... | collective-permute-start | bytes 921608 | tf_op jit(solution)/shard_map/ppermute | solution.py:263
  25.3 35.3 %collective-permute-start.10 = (bf16[600,256]{1,0:T(8,128)(2,1)S(1)}, bf16[600,256]{1,0:T(8,128)(2,1)S(1)}, u32[]{:S(2)}, u32[]{:S(2)}) collective-permute-start(bf16[600,256]{1,0:T(8,128)(2,1)S(1)} %get-tuple-element.28), channel_id=1, source_target_pairs={{0,12},{1,13},{2,14},{3,15},{4,8},{5,9},{6,10},{7,11},{8,4},{9,5},... | collective-permute-start | bytes 921608 | tf_op jit(solution)/shard_map/ppermute | solution.py:263
  27.3 34.6 %collective-permute-start.4 = (bf16[600,256]{1,0:T(8,128)(2,1)S(1)}, bf16[600,256]{1,0:T(8,128)(2,1)S(1)}, u32[]{:S(2)}, u32[]{:S(2)}) collective-permute-start(bf16[600,256]{1,0:T(8,128)(2,1)S(1)} %get-tuple-element.31), channel_id=1, source_target_pairs={{0,2},{1,3},{2,0},{3,1},{4,6},{5,7},{6,4},{7,5},{8,10},{9,11},{10,... | collective-permute-start | bytes 921608 | tf_op jit(solution)/shard_map/ppermute | solution.py:263
  28.8 33.1 %collective-permute-start.5 = (bf16[600,256]{1,0:T(8,128)(2,1)S(1)}, bf16[600,256]{1,0:T(8,128)(2,1)S(1)}, u32[]{:S(2)}, u32[]{:S(2)}) collective-permute-start(bf16[600,256]{1,0:T(8,128)(2,1)S(1)} %get-tuple-element.32), channel_id=1, source_target_pairs={{0,6},{1,7},{2,4},{3,5},{4,2},{5,3},{6,0},{7,1},{8,14},{9,15},{10,... | collective-permute-start | bytes 921608 | tf_op jit(solution)/shard_map/ppermute | solution.py:263
  38.8 28.3 %collective-permute-start.7 = (bf16[600,256]{1,0:T(8,128)(2,1)S(1)}, bf16[600,256]{1,0:T(8,128)(2,1)S(1)}, u32[]{:S(2)}, u32[]{:S(2)}) collective-permute-start(bf16[600,256]{1,0:T(8,128)(2,1)S(1)} %get-tuple-element.29), channel_id=1, source_target_pairs={{0,14},{1,15},{2,12},{3,13},{4,10},{5,11},{6,8},{7,9},{8,6},{9,7},... | collective-permute-start | bytes 921608 | tf_op jit(solution)/shard_map/ppermute | solution.py:263
